TPU v7x, 32 devices: a whole 2x2x4 slice. The times are simulated.
32 devices in a mesh: groups: 2 (over y), units: 8 (over z, x), heads: 2 (over core).
Axes of the slice: x: 2, y: 2, z: 4, core: 2. Of those that a mesh axis runs over, the one named last changes fastest.
Arguments:
- queries: bfloat16 [16, 6144], P(('groups', 'units'), 'heads'), parts along dimension 0, may hold values from -160 to 160
- fresh_key: bfloat16 [16, 1024], P(('groups', 'units'), 'heads'), parts along dimension 0, may hold values from -6 to 6
- fresh_value: bfloat16 [16, 1024], P(('groups', 'units'), 'heads'), parts along dimension 0, may hold values from -6 to 6
- key_cache_pages: bfloat16 [64, 128, 1024], P(('groups', 'units'), None, 'heads'), parts along dimension 0, may hold values from -6 to 6
- value_cache_pages: bfloat16 [64, 128, 1024], P(('groups', 'units'), None, 'heads'), parts along dimension 0, may hold values from -6 to 6
- page_table: int32 [16, 4], P(('groups', 'units')), parts along dimension 0, may hold values from 0 to 3, as said below
- lengths: int32 [16], P(('groups', 'units')), parts along dimension 0, may hold values from 1 to 512, as said below
- resid: bfloat16 [16, 6144], P('groups', 'units'), parts along dimension 0, may hold values from -0.59765625 to 0.59765625
- w_out: bfloat16 [6144, 6144], P('heads', 'units'), may hold values from -0.078125 to 0.078125
- norm_gain: bfloat16 [6144], replicated, may hold values from 0.25 to 1.75
- router: bfloat16 [6144, 8], replicated, may hold values from -0.15625 to 0.15625
- routes: int32 [16, 2], P('groups'), parts along dimension 0, may hold values from 0 to 7, as said below
- w_gate: bfloat16 [6144, 16384], P('heads', 'units'), may hold values from -0.078125 to 0.078125
- w_up: bfloat16 [6144, 16384], P('heads', 'units'), may hold values from -0.078125 to 0.078125
- w_down: bfloat16 [16384, 6144], P('units', 'heads'), may hold values from -0.09375 to 0.09375
Outputs:
- layer_out: bfloat16 [16, 6144], P(('groups', 'units'), 'heads'), parts along dimension 0
There are 2 independent parts, one for each index of `groups`. A program takes and returns all parts, laid end to end along the dimension named above; an argument that names none is the same for every part. Nothing has to cross between parts.
Inputs may be any that keep to these rules, and one draw needn't show every extreme that they name: `page_table`: the 1 requests r of one pool block b = r // 1 use every page of that block exactly once among them. `lengths`: some request has exactly 512 cached tokens. `routes`: each request names two different experts; exactly 2 requests name expert 0.
All inputs are finite; a program needn't handle non-finite values.
Results may differ from a plain program's by a relative error of at most 0.01.
Values may be sent and summed in bfloat16 or wider, within the bound.
No kernel may reach another device: no remote copies, remote signals or barrier semaphores. Data moves between devices by JAX's collectives and lax.ppermute only.
A program may use at most 128 MiB of HBM per device.

v0:
```python
import jax
import jax.numpy as jnp
from jax import lax
from jax.sharding import PartitionSpec as P

HEAD_WIDTH = 128


def attend(
    queries, fresh_key, fresh_value, key_cache_pages, value_cache_pages, page_table, lengths
):
    token_rows = queries.shape[0]
    kv_width = fresh_key.shape[1]
    heads_kv = kv_width // HEAD_WIDTH
    query_group = queries.shape[1] // kv_width
    score_scale = HEAD_WIDTH ** (-0.5)
    key_rows = key_cache_pages[page_table].reshape(token_rows, -1, heads_kv, HEAD_WIDTH)
    value_rows = value_cache_pages[page_table].reshape(token_rows, -1, heads_kv, HEAD_WIDTH)
    query_grid = queries.reshape(token_rows, heads_kv, query_group, HEAD_WIDTH)
    scores = (
        jnp.einsum("rgjd,rtgd->rgjt", query_grid, key_rows, preferred_element_type=jnp.float32)
        * score_scale
    )
    expert_owned = (
        jnp.einsum(
            "fiam,fim->fia",
            query_grid,
            fresh_key.reshape(token_rows, heads_kv, HEAD_WIDTH),
            preferred_element_type=jnp.float32,
        )
        * score_scale
    )
    span = key_rows.shape[1]
    live = (jnp.arange(span, dtype=jnp.int32)[None, :] < lengths[:, None])[:, None, None, :]
    top = jnp.maximum(jnp.max(jnp.where(live, scores, -jnp.inf), axis=-1), expert_owned)
    prob = jnp.where(live, jnp.exp(scores - top[..., None]), 0.0)
    own_p = jnp.exp(expert_owned - top)
    total = jnp.sum(prob, axis=-1) + own_p
    weights = (prob / total[..., None]).astype(jnp.bfloat16)
    owned_weight = (own_p / total).astype(jnp.bfloat16)
    blended_values = jnp.einsum(
        "rgjt,rtgd->rgjd", weights, value_rows, preferred_element_type=jnp.float32
    )
    blended_values = blended_values + owned_weight.astype(jnp.float32)[
        ..., None
    ] * fresh_value.reshape(token_rows, heads_kv, 1, HEAD_WIDTH).astype(jnp.float32)
    return blended_values.reshape(token_rows, -1).astype(jnp.bfloat16)


def route_weight(logits, routes):
    picks = (
        routes[:, :, None] == jnp.arange(logits.shape[1], dtype=jnp.int32)[None, None, :]
    ).astype(jnp.float32)
    chosen = jnp.sum(picks * logits[:, None, :], axis=-1)
    first = jax.nn.sigmoid(chosen[:, 0] - chosen[:, 1])
    second = jax.nn.sigmoid(chosen[:, 1] - chosen[:, 0])
    return jnp.where(routes[:, 0] == 0, first, jnp.where(routes[:, 1] == 0, second, 0.0))


def body(
    queries,
    fresh_key,
    fresh_value,
    key_cache_pages,
    value_cache_pages,
    page_table,
    lengths,
    resid,
    w_out,
    norm_gain,
    router,
    routes,
    w_gate,
    w_up,
    w_down,
):
    own_rows = queries.shape[0]
    half_width = w_gate.shape[0]
    all_rows = routes.shape[0]
    routed_count = all_rows * routes.shape[1] // router.shape[1]
    unit_index = lax.axis_index("units")
    head_index = lax.axis_index("heads")
    attn = attend(
        queries, fresh_key, fresh_value, key_cache_pages, value_cache_pages, page_table, lengths
    )
    proj_part = jnp.dot(
        lax.all_gather(attn, "units", axis=0, tiled=True), w_out, preferred_element_type=jnp.float32
    )
    proj = lax.psum(proj_part, "heads")
    h1_cols = (resid.astype(jnp.float32) + proj).astype(jnp.bfloat16)
    h1 = lax.all_gather(h1_cols, "units", axis=1, tiled=True)
    is_routed = jnp.any(routes == 0, axis=1)
    slot_of = jnp.cumsum(is_routed.astype(jnp.int32)) - 1
    slot_ids = jnp.arange(routed_count, dtype=jnp.int32)
    row_ids = jnp.arange(all_rows, dtype=jnp.int32)
    match = (slot_of[None, :] == slot_ids[:, None]) & is_routed[None, :]
    picked_rows = jnp.sum(jnp.where(match, row_ids[None, :], 0), axis=1)
    h1_sel = h1[picked_rows]
    hf_sel = h1_sel.astype(jnp.float32)
    rstd = lax.rsqrt(jnp.mean(hf_sel * hf_sel, axis=-1, keepdims=True) + 1e-05)
    xn_sel = (hf_sel * rstd * norm_gain.astype(jnp.float32)).astype(jnp.bfloat16)
    logits = jnp.dot(xn_sel, router, preferred_element_type=jnp.float32)
    route = route_weight(logits, routes[picked_rows])
    xn_half = lax.dynamic_slice_in_dim(xn_sel, head_index * half_width, half_width, 1)
    gate_part = jnp.dot(xn_half, w_gate, preferred_element_type=jnp.float32)
    up_part = jnp.dot(xn_half, w_up, preferred_element_type=jnp.float32)
    gate, up = lax.psum((gate_part, up_part), "heads")
    hidden = (jax.nn.silu(gate) * up * route[:, None]).astype(jnp.bfloat16)
    full_term = jnp.dot(hidden, w_down, preferred_element_type=jnp.float32)
    own_start = unit_index * own_rows
    own_h1 = lax.dynamic_slice_in_dim(
        lax.dynamic_slice_in_dim(h1, own_start, own_rows, 0), head_index * half_width, half_width, 1
    )
    own_routed = lax.dynamic_slice_in_dim(is_routed, own_start, own_rows, 0)
    own_slot = jnp.maximum(lax.dynamic_slice_in_dim(slot_of, own_start, own_rows, 0), 0)
    moe_sel = lax.psum(full_term, "units")
    moe_own = jnp.where(own_routed[:, None], moe_sel[own_slot], 0.0)
    return (own_h1.astype(jnp.float32) + moe_own).astype(jnp.bfloat16)


def solution(mesh):
    in_specs = (
        P(("groups", "units"), "heads"),
        P(("groups", "units"), "heads"),
        P(("groups", "units"), "heads"),
        P(("groups", "units"), None, "heads"),
        P(("groups", "units"), None, "heads"),
        P(("groups", "units"), None),
        P(("groups", "units")),
        P("groups", "units"),
        P("heads", "units"),
        P(),
        P(),
        P("groups", None),
        P("heads", "units"),
        P("heads", "units"),
        P("units", "heads"),
    )
    out_specs = P(("groups", "units"), "heads")
    return jax.shard_map(body, mesh=mesh, in_specs=in_specs, out_specs=out_specs, check_vma=False)
```

profile of v0, /device:TPU:0, one launch (start us, length us, event | category | flops | bytes accessed | tf_op | source)
XLA Modules:
  0.0 143.6 jit_solution(2690438309002651802)
XLA Ops:
  0.0 0.0 copy-start
  0.7 0.7 fusion.34
  1.4 0.0 copy-done
  1.4 0.6 gather_fusion
  2.0 0.1 reshape.166
  2.1 0.7 reduce.5
  2.9 0.3 select_reduce_fusion
  3.2 0.8 fusion.26
  4.0 0.2 bitcast_reduce_fusion
  4.2 1.6 %gather_fusion.1 = bf16[4,128,512]{2,1,0:T(8,128)(2,1)S(1)} fusion(bf16[4,128,512]{2,1,0:T(8,128)(2,1)} %param.19, s32[1024]{0:T(1024)S(1)} %pad_clamp_fusion.1), kind=kCustom, calls=%fused_computation.1 | custom fusion | bytes 1048592 | tf_op jit(solution)/shard_map/gather | solution.py:18
  5.9 0.1 reshape.169
  6.0 0.7 convert_element_type.92
  6.7 0.2 fusion
  6.9 32.3 %all-gather = bf16[8,1,3072]{2,1,0:T(2,128)(2,1)S(1)} all-gather(bf16[1,1,3072]{2,1,0:T(2,128)(2,1)S(1)} %reshape.227), channel_id=1, replica_groups=mesh['groups'=2,'units'=8,'heads'=2] {'units'}, dimensions={0}, use_global_device_ids=true | all-gather | bytes 55296 | tf_op jit(solution)/shard_map/all_gather | solution.py:87
  39.3 3.1 %fusion.7 = f32[8,768]{1,0:T(8,128)S(1)} fusion(bf16[3072,768]{1,0:T(8,128)(2,1)} %param.23, bf16[8,1,3072]{2,1,0:T(2,128)(2,1)S(1)} %all-gather), kind=kOutput, calls=%fused_computation.19 | convolution fusion | flops 37748736 | bytes 4792320 | tf_op jit(solution)/shard_map/dot_general | solution.py:86
  42.3 3.4 %psum.28 = f32[8,768]{1,0:T(8,128)S(1)} all-reduce(f32[8,768]{1,0:T(8,128)S(1)} %fusion.7), channel_id=1, replica_groups=mesh['groups'=2,'units'=8,'heads'=2] {'heads'}, use_global_device_ids=true, to_apply=%region_2.3 | all-reduce | flops 6144 | bytes 49152 | tf_op jit(solution)/shard_map/psum | solution.py:89
  45.7 0.7 add_convert_fusion
  46.5 30.5 %all_gather.7 = bf16[8,6144]{1,0:T(8,128)(2,1)S(1)} all-gather(bf16[8,768]{1,0:T(8,128)(2,1)S(1)} %add_convert_fusion), channel_id=1, replica_groups=mesh['groups'=2,'units'=8,'heads'=2] {'units'}, dimensions={1}, use_global_device_ids=true | all-gather | bytes 110592 | tf_op jit(solution)/shard_map/all_gather | solution.py:91
  77.0 0.7 compare_reduce_fusion
  77.7 0.2 reduce-window.7
  77.9 0.1 fusion.28
  78.0 0.1 copy.36
  78.1 0.1 fusion.29
  78.2 0.6 gather_fusion.2
  78.8 0.2 fusion.4
  79.0 0.7 convert_element_type.88
  79.7 0.1 fusion.6
  79.8 6.3 %fusion.23 = f32[2,2048]{1,0:T(2,128)S(1)} fusion(bf16[3072,2048]{1,0:T(8,128)(2,1)} %param.27, bf16[2,6144]{1,0:T(2,128)(2,1)S(1)} %fusion.6, s32[]{:T(128)S(6)} %select_n.74), kind=kOutput, calls=%fused_computation.38 | convolution fusion | flops 25165824 | bytes 12611588 | tf_op jit(solution)/shard_map/dot_general | solution.py:105
  86.1 0.0 copy-start.2
  86.1 0.0 copy-start.1
  86.1 6.3 %fusion.21 = f32[2,2048]{1,0:T(2,128)S(1)} fusion(bf16[3072,2048]{1,0:T(8,128)(2,1)} %param.28, bf16[2,6144]{1,0:T(2,128)(2,1)S(1)} %fusion.6, s32[]{:T(128)S(6)} %select_n.74), kind=kOutput, calls=%fused_computation.36 | convolution fusion | flops 25165824 | bytes 12611588 | tf_op jit(solution)/shard_map/dot_general | solution.py:106
  92.5 3.4 %all-reduce = (f32[2,2048]{1,0:T(2,128)S(1)}, f32[2,2048]{1,0:T(2,128)S(1)}) all-reduce(f32[2,2048]{1,0:T(2,128)S(1)} %fusion.21, f32[2,2048]{1,0:T(2,128)S(1)} %fusion.23), channel_id=1, replica_groups=mesh['groups'=2,'units'=8,'heads'=2] {'heads'}, use_global_device_ids=true, to_apply=%region_8.9 | all-reduce | flops 8192 | bytes 65536 | tf_op jit(solution)/shard_map/psum | solution.py:107
  95.9 0.0 copy-done.2
  95.9 0.2 fusion.40
  96.1 0.0 copy-done.1
  96.1 0.1 copy.39
  96.1 0.6 gather_fusion.3
  96.7 0.2 fusion.25
  96.9 0.2 fusion.31
  97.1 6.3 %fusion.18 = f32[2,3072]{1,0:T(2,128)S(1)} fusion(bf16[2048,3072]{1,0:T(8,128)(2,1)} %param.29, f32[2,2048]{1,0:T(2,128)S(1)} %get-tuple-element.16, f32[2,2048]{1,0:T(2,128)S(1)} %get-tuple-element.17, f32[2]{0:T(128)S(1)} %fusion.31), kind=kOutput, calls=%fused_computation.33 | convolution fusion | flops 25194496 | bytes 12640264 | tf_op jit(solution)/shard_map/dot_general | solution.py:109
  103.4 37.0 %psum.31 = f32[2,3072]{1,0:T(2,128)S(1)} all-reduce(f32[2,3072]{1,0:T(2,128)S(1)} %fusion.18), channel_id=1, replica_groups=mesh['groups'=2,'units'=8,'heads'=2] {'units'}, use_global_device_ids=true, to_apply=%region_10.11 | all-reduce | flops 6144 | bytes 49152 | tf_op jit(solution)/shard_map/psum | solution.py:116
  140.4 0.6 fusion.39
  141.0 0.7 dynamic_slice.14
  141.7 1.9 %fusion.17 = bf16[1,3072]{1,0:T(2,128)(2,1)} fusion(pred[]{:T(512)} %bitcast.7, f32[2,3072]{1,0:T(2,128)S(1)} %psum.31, s32[]{:T(128)} %bitcast.11, bf16[8,6144]{1,0:T(8,128)(2,1)S(1)} %all_gather.7, s32[]{:T(128)S(6)} %select_n.73, s32[]{:T(128)S(6)} %select_n.75), kind=kLoop, calls=%fused_computation.32 | loop fusion | flops 12288 | bytes 24589 | tf_op jit(solution)/shard_map/convert_element_type | solution.py:118
  (10 shorter events, 0.1 us)
Async XLA Ops:
  0.0 1.4 copy-start
  86.1 9.8 %copy-start.2 = (bf16[6144,8]{0,1:T(8,128)(2,1)S(1)}, bf16[6144,8]{0,1:T(8,128)(2,1)}, u32[]{:S(2)}) copy-start(bf16[6144,8]{0,1:T(8,128)(2,1)} %param.25) | copy-start | bytes 294916
  86.1 9.9 %copy-start.1 = (s32[8,2]{0,1:T(2,128)S(1)}, s32[8,2]{0,1:T(2,128)}, u32[]{:S(2)}) copy-start(s32[8,2]{0,1:T(2,128)} %param.26) | copy-start | bytes 196
where the time goes:
time: 144 us
  blocking collectives  107 us (74%)
  matrix products  23.6 us (16%)
  other arithmetic  8.01 us (6%)
  local copies, waits for them, and re-layouts  4.5 us (3%)
    psum x1, blocking collectives, body(): moe_sel = lax.psum(full_term, 'units')  37 us
    all_gather x1, blocking collectives, body(): lax.all_gather(attn, 'units', axis=0, tiled=True)  32.3 us
    all_gather x1, blocking collectives, body(): h1 = lax.all_gather(h1_cols, 'units', axis=1, tiled=True)  30.5 us
    dot_general x1, matrix products, body(): full_term = jnp.dot(hidden, w_down, preferred_element_type=jnp.float32)  6.35 us
    dot_general x1, matrix products, body(): up_part = jnp.dot(xn_half, w_up, preferred_element_type=jnp.float32)  6.35 us
    dot_general x1, matrix products, body(): gate_part = jnp.dot(xn_half, w_gate, preferred_element_type=jnp.float32)  6.31 us
    psum x1, blocking collectives, body(): proj = lax.psum(proj_part, 'heads')  3.41 us
    psum x1, blocking collectives, body(): gate, up = lax.psum((gate_part, up_part), 'heads')  3.4 us

commit v1 on v0

--- a/solution.py
+++ b/solution.py
@@ -1,9 +1,17 @@
+import functools
+
 import jax
 import jax.numpy as jnp
 from jax import lax
+from jax.experimental import pallas as pl
+from jax.experimental.pallas import tpu as pltpu
 from jax.sharding import PartitionSpec as P
 
 HEAD_WIDTH = 128
+LANES = 128
+F32 = jnp.float32
+BF16 = jnp.bfloat16
+MIB = 2**20
 
 
 def attend(
@@ -118,6 +126,236 @@
     return (own_h1.astype(jnp.float32) + moe_own).astype(jnp.bfloat16)
 
 
+def attn_kernel(table_ref, len_ref, q_ref, fk_ref, fv_ref, k_ref, v_ref, o_ref):
+    pages, page_tokens, kv_width = k_ref.shape
+    heads_kv = kv_width // HEAD_WIDTH
+    group = q_ref.shape[1] // kv_width
+    rows = -(-group // 8) * 8
+    span = pages * page_tokens
+    scale = HEAD_WIDTH ** (-0.5)
+    length = len_ref[0]
+    q = q_ref[...].astype(F32)
+    fk = fk_ref[...].astype(F32)
+    fv = fv_ref[...].astype(F32)
+    pad = [jnp.zeros((rows - group, HEAD_WIDTH), F32)] if rows > group else []
+    live = lax.broadcasted_iota(jnp.int32, (rows, span), 1) < length
+    blended = []
+    for g in range(heads_kv):
+        lanes = slice(g * HEAD_WIDTH, (g + 1) * HEAD_WIDTH)
+        first = g * group
+        q_g = jnp.concatenate(
+            [q[:, (first + j) * HEAD_WIDTH : (first + j + 1) * HEAD_WIDTH] for j in range(group)] + pad,
+            axis=0,
+        )
+        keys = jnp.concatenate([k_ref[table_ref[0, p], :, lanes] for p in range(pages)], axis=0)
+        values = jnp.concatenate([v_ref[table_ref[0, p], :, lanes] for p in range(pages)], axis=0)
+        s = (
+            lax.dot_general(
+                q_g.astype(BF16), keys, (((1,), (1,)), ((), ())), preferred_element_type=F32
+            )
+            * scale
+        )
+        own = jnp.sum(q_g * fk[:, lanes], axis=1, keepdims=True) * scale
+        top = jnp.maximum(jnp.max(jnp.where(live, s, -jnp.inf), axis=1, keepdims=True), own)
+        prob = jnp.where(live, jnp.exp(s - top), 0.0)
+        own_p = jnp.exp(own - top)
+        total = jnp.sum(prob, axis=1, keepdims=True) + own_p
+        weights = (prob / total).astype(BF16)
+        own_weight = (own_p / total).astype(BF16).astype(F32)
+        out = jnp.dot(weights, values, preferred_element_type=F32) + own_weight * fv[:, lanes]
+        blended.append(out[:group])
+    attn = jnp.concatenate(blended, axis=0).astype(BF16)
+    for r in range(o_ref.shape[0]):
+        o_ref[r] = attn
+
+
+def proj_kernel(attn_ref, w_ref, o_ref):
+    attn = attn_ref[...].astype(F32)
+    x = jnp.concatenate([attn[:, j, :] for j in range(attn.shape[1])], axis=1).astype(BF16)
+    o_ref[...] = jnp.dot(x, w_ref[...], preferred_element_type=F32)
+
+
+def resid_kernel(resid_ref, mine_ref, other_ref, o_ref):
+    h1 = (resid_ref[...].astype(F32) + (mine_ref[...] + other_ref[...])).astype(BF16)
+    for r in range(o_ref.shape[0]):
+        o_ref[r] = h1
+
+
+def routed_rows(routes_ref):
+    count = routes_ref.shape[0]
+    first = jnp.int32(count - 1)
+    last = jnp.int32(0)
+    for r in range(count):
+        hit = jnp.logical_or(routes_ref[r, 0] == 0, routes_ref[r, 1] == 0)
+        first = jnp.where(hit, jnp.minimum(first, r), first)
+        last = jnp.where(hit, r, last)
+    return first, last
+
+
+def expert_kernel(
+    routes_ref, h1_ref, gain_ref, router_ref, routes_v_ref, wg_ref, wu_ref, gu_ref, route_ref, own_ref,
+    gu_all, route_all, own_all,
+):
+    units = h1_ref.shape[0]
+    half = wg_ref.shape[0]
+    hidden = wg_ref.shape[1]
+    head = lax.axis_index("heads")
+    unit = lax.axis_index("units")
+    h1 = jnp.concatenate([h1_ref[u] for u in range(units)], axis=1).astype(F32)
+    gain = gain_ref[...].astype(F32)
+    rstd = lax.rsqrt(jnp.mean(h1 * h1, axis=1, keepdims=True) + 1e-05)
+    xn = (h1 * rstd * gain).astype(BF16)
+    x_half = jnp.where(head == 0, xn[:, :half].astype(F32), xn[:, half:].astype(F32)).astype(BF16)
+    own_all[...] = jnp.where(head == 0, h1[:, :half], h1[:, half:])
+    own_ref[...] = own_all[pl.ds(unit, 1), :]
+    gu_all[:, :hidden] = jnp.dot(x_half, wg_ref[...], preferred_element_type=F32)
+    gu_all[:, hidden:] = jnp.dot(x_half, wu_ref[...], preferred_element_type=F32)
+    logits = jnp.dot(xn, router_ref[...], preferred_element_type=F32)
+    expert_ids = lax.broadcasted_iota(jnp.int32, logits.shape, 1)
+    one = routes_v_ref[:, 0:1]
+    two = routes_v_ref[:, 1:2]
+    chosen_one = jnp.sum(jnp.where(expert_ids == one, logits, 0.0), axis=1, keepdims=True)
+    chosen_two = jnp.sum(jnp.where(expert_ids == two, logits, 0.0), axis=1, keepdims=True)
+    diff = jnp.where(one == 0, chosen_one - chosen_two, chosen_two - chosen_one)
+    route = jnp.where(jnp.logical_or(one == 0, two == 0), 1.0 / (1.0 + jnp.exp(-diff)), 0.0)
+    route_all[...] = jnp.broadcast_to(route, route_all.shape)
+    for slot, r in enumerate(routed_rows(routes_ref)):
+        gu_ref[slot : slot + 1, :] = gu_all[pl.ds(r, 1), :]
+        route_ref[slot : slot + 1, :] = route_all[pl.ds(r, 1), :]
+
+
+def down_kernel(routes_ref, mine_ref, other_ref, route_ref, wd_ref, o_ref):
+    hidden = wd_ref.shape[0]
+    gu = mine_ref[...] + other_ref[...]
+    gate = gu[:, :hidden]
+    up = gu[:, hidden:]
+    act = (gate / (1.0 + jnp.exp(-gate)) * up * route_ref[:, 0:1]).astype(BF16)
+    full = jnp.dot(act, wd_ref[...], preferred_element_type=F32)
+    o_ref[...] = jnp.zeros(o_ref.shape, F32)
+    for slot, r in enumerate(routed_rows(routes_ref)):
+        for j in range(o_ref.shape[1]):
+            o_ref[r, j : j + 1, :] = full[slot : slot + 1, j * LANES : (j + 1) * LANES]
+
+
+def sum_kernel(parts_ref, own_ref, o_ref):
+    moe = parts_ref[0]
+    for u in range(1, parts_ref.shape[0]):
+        moe = moe + parts_ref[u]
+    for j in range(parts_ref.shape[1]):
+        lanes = slice(j * LANES, (j + 1) * LANES)
+        o_ref[:, lanes] = (own_ref[:, lanes] + moe[j : j + 1, :]).astype(o_ref.dtype)
+
+
+SMEM = pl.BlockSpec(memory_space=pltpu.SMEM)
+VMEM = pl.BlockSpec(memory_space=pltpu.VMEM)
+
+
+def in_vmem(x):
+    return pltpu.with_memory_space_constraint(x, pltpu.VMEM)
+
+
+def small_body(
+    queries,
+    fresh_key,
+    fresh_value,
+    key_cache_pages,
+    value_cache_pages,
+    page_table,
+    lengths,
+    resid,
+    w_out,
+    norm_gain,
+    router,
+    routes,
+    w_gate,
+    w_up,
+    w_down,
+):
+    rows = routes.shape[0]
+    half = w_gate.shape[0]
+    chunks = half // LANES
+    hidden = w_gate.shape[1]
+    cols = w_out.shape[1]
+    swap = [(0, 1), (1, 0)]
+
+    def exchange(x):
+        return lax.all_to_all(x, "units", split_axis=0, concat_axis=0, tiled=True)
+
+    def call(kernel, out, specs, name, scratch=(), limit=6):
+        return pl.pallas_call(
+            kernel,
+            out_shape=out,
+            in_specs=specs,
+            out_specs=jax.tree.map(lambda _: VMEM, out),
+            scratch_shapes=scratch,
+            compiler_params=pltpu.CompilerParams(vmem_limit_bytes=limit * MIB),
+            name=name,
+        )
+
+    attn = call(
+        attn_kernel,
+        jax.ShapeDtypeStruct((rows, chunks, LANES), BF16),
+        [SMEM, SMEM, VMEM, VMEM, VMEM, VMEM, VMEM],
+        "attend",
+    )(
+        page_table, lengths, queries, fresh_key, fresh_value,
+        in_vmem(key_cache_pages), in_vmem(value_cache_pages),
+    )
+    attn_all = exchange(attn)
+    proj = call(proj_kernel, jax.ShapeDtypeStruct((rows, cols), F32), [VMEM] * 2, "proj")(
+        attn_all, in_vmem(w_out)
+    )
+    proj_other = lax.ppermute(proj, "heads", swap)
+    h1_cols = call(
+        resid_kernel, jax.ShapeDtypeStruct((rows, rows, cols), BF16), [VMEM] * 3, "resid"
+    )(resid, proj, proj_other)
+    h1 = exchange(h1_cols)
+    gu, route, own_h1 = call(
+        expert_kernel,
+        (
+            jax.ShapeDtypeStruct((2, 2 * hidden), F32),
+            jax.ShapeDtypeStruct((2, LANES), F32),
+            jax.ShapeDtypeStruct((1, half), F32),
+        ),
+        [SMEM] + [VMEM] * 6,
+        "expert",
+        scratch=(
+            pltpu.VMEM((rows, 2 * hidden), F32),
+            pltpu.VMEM((rows, LANES), F32),
+            pltpu.VMEM((rows, half), F32),
+        ),
+    )(
+        routes, h1, norm_gain.reshape(1, -1), in_vmem(router), routes, in_vmem(w_gate), in_vmem(w_up)
+    )
+    gu_other = lax.ppermute(gu, "heads", swap)
+    full = call(
+        down_kernel,
+        jax.ShapeDtypeStruct((rows, chunks, LANES), F32),
+        [SMEM] + [VMEM] * 4,
+        "down",
+    )(routes, gu, gu_other, route, in_vmem(w_down))
+    parts = exchange(full)
+    return call(sum_kernel, jax.ShapeDtypeStruct((1, half), BF16), [VMEM] * 2, "total")(
+        parts, own_h1
+    )
+
+
+def one_tile(*args):
+    queries, routes, router = args[0], args[11], args[10]
+    rows = routes.shape[0]
+    units = lax.axis_size("units")
+    return (
+        queries.shape[0] == 1
+        and rows == 8
+        and units == rows
+        and rows * routes.shape[1] // router.shape[1] == 2
+    )
+
+
+def dispatch(*args):
+    return small_body(*args) if one_tile(*args) else body(*args)
+
+
 def solution(mesh):
     in_specs = (
         P(("groups", "units"), "heads"),
@@ -137,4 +375,4 @@
         P("units", "heads"),
     )
     out_specs = P(("groups", "units"), "heads")
-    return jax.shard_map(body, mesh=mesh, in_specs=in_specs, out_specs=out_specs, check_vma=False)
+    return jax.shard_map(dispatch, mesh=mesh, in_specs=in_specs, out_specs=out_specs, check_vma=False)

time: 144 us -> 65.4 us (0.45)
  blocking collectives: 107 us -> 23.4 us
  matrix products: 23.6 us -> 0 us
  local copies, waits for them, and re-layouts: 4.5 us -> 20 us
  Pallas kernels: 0 us -> 10.7 us
  other arithmetic: 8.01 us -> 0 us
  waiting for transfers between devices: 0 us -> 6.41 us
  starting transfers between devices: 0 us -> 3.39 us
    all_gather x2 -> x0, blocking collectives: 62.9 us -> none  [the longest x1 32.3 us: body(): lax.all_gather(attn, 'units', axis=0, tiled=True)]
    psum x3 -> x0, blocking collectives: 43.8 us -> none  [the longest x1 37 us: body(): moe_sel = lax.psum(full_term, 'units')]
    dot_general x8 -> x0, matrix products: 23.6 us -> none  [the longest x1 6.35 us: body(): full_term = jnp.dot(hidden, w_down, preferred_element_type=jnp.float32)]
    all_to_all x0 -> x2, blocking collectives: none -> 23.4 us  [exchange(): return lax.all_to_all(x, 'units', split_axis=0, concat_axis=0, tiled=True)]
    unnamed x8 -> x24, local copies, waits for them, and re-layouts: 0.11 us -> 19.3 us
    pallas_call x0 -> x6, Pallas kernels: none -> 10.7 us  [the longest x1 4.42 us: small_body(): call(expert_kernel, (jax.ShapeDtypeStruct((2, 2 * hidden), F32), jax.Shap...]
    convert_element_type x7 -> x0, other arithmetic: 4.17 us -> none  [the longest x1 1.94 us: body(): return (own_h1.astype(jnp.float32) + moe_own).astype(jnp.bfloat16)]
    all_to_all x0 -> x1, waiting for transfers between devices: none -> 4 us  [exchange(): return lax.all_to_all(x, 'units', split_axis=0, concat_axis=0, tiled=True)]
  transfers between devices with their start and end apart: 0 -> 3, of which waited for: 0 -> 3; matrix products, arithmetic and copies ran while one was open for 0% -> 5% of each run, Pallas kernels for 0% -> 0%
where the time goes in v1:
time: 65.4 us; the launch traced here: 64.6 us
  blocking collectives  23.4 us (36%)
  local copies, waits for them, and re-layouts  20 us (31%)
  Pallas kernels  10.7 us (16%)
  waiting for transfers between devices  6.41 us (10%)
  starting transfers between devices  3.39 us (5%)
  between operations  0.7 us (1%)
    all_to_all x2, blocking collectives, exchange(): return lax.all_to_all(x, 'units', split_axis=0, concat_axis=0, tiled=True)  23.4 us
    unnamed x24, local copies, waits for them, and re-layouts  19.3 us
    pallas_call x1, Pallas kernels, small_body(): call(expert_kernel, (jax.ShapeDtypeStruct((2, 2 * hidden), F32), jax.Shap...  4.42 us
    all_to_all x1, waiting for transfers between devices, exchange(): return lax.all_to_all(x, 'units', split_axis=0, concat_axis=0, tiled=True)  4 us
    all_to_all x1, starting transfers between devices, exchange(): return lax.all_to_all(x, 'units', split_axis=0, concat_axis=0, tiled=True)  3.36 us
    pallas_call x1, Pallas kernels, small_body(): call(down_kernel, jax.ShapeDtypeStruct((rows, chunks, LANES), F32), [SMEM...  2.37 us
    pallas_call x1, Pallas kernels, small_body(): call(attn_kernel, jax.ShapeDtypeStruct((rows, chunks, LANES), BF16), [SME...  1.95 us
  transfers between devices with their start and end apart: 3, of which 3 were waited for; matrix products, arithmetic and copies ran while one was open for 5% of the time, Pallas kernels for 0%

profile of v1, /device:TPU:0, one launch (start us, length us, event | category | flops | bytes accessed | tf_op | source)
XLA Modules:
  0.0 64.6 jit_solution(4576804849200115351)
XLA Ops:
  0.7 0.0 copy-start.4
  0.7 1.0 %copy-done.4 = bf16[4,128,512]{2,1,0:T(8,128)(2,1)S(1)} copy-done((bf16[4,128,512]{2,1,0:T(8,128)(2,1)S(1)}, bf16[4,128,512]{2,1,0:T(8,128)(2,1)}, u32[]{:S(2)}) %copy-start.4) | copy-done | bytes 524312
  1.7 0.0 copy-start.5
  1.7 1.0 %copy-done.5 = bf16[4,128,512]{2,1,0:T(8,128)(2,1)S(1)} copy-done((bf16[4,128,512]{2,1,0:T(8,128)(2,1)S(1)}, bf16[4,128,512]{2,1,0:T(8,128)(2,1)}, u32[]{:S(2)}) %copy-start.5) | copy-done | bytes 524312
  2.7 0.0 copy-start.6
  2.7 0.7 %copy-done.6 = bf16[1,3072]{1,0:T(2,128)(2,1)S(1)} copy-done((bf16[1,3072]{1,0:T(2,128)(2,1)S(1)}, bf16[1,3072]{1,0:T(2,128)(2,1)}, u32[]{:S(2)}) %copy-start.6) | copy-done | bytes 6168
  3.4 0.0 copy-start.8
  3.4 0.7 %copy-done.8 = bf16[1,512]{1,0:T(2,128)(2,1)S(1)} copy-done((bf16[1,512]{1,0:T(2,128)(2,1)S(1)}, bf16[1,512]{1,0:T(2,128)(2,1)}, u32[]{:S(2)}) %copy-start.8) | copy-done | bytes 1048
  4.1 0.0 copy-start.9
  4.1 0.7 %copy-done.9 = bf16[1,512]{1,0:T(2,128)(2,1)S(1)} copy-done((bf16[1,512]{1,0:T(2,128)(2,1)S(1)}, bf16[1,512]{1,0:T(2,128)(2,1)}, u32[]{:S(2)}) %copy-start.9) | copy-done | bytes 1048
  4.8 0.0 copy-start.10
  4.8 0.7 %copy-done.10 = s32[1,4]{1,0:T(1,128)S(1)} copy-done((s32[1,4]{1,0:T(1,128)S(1)}, s32[1,4]{1,0:T(1,128)}, u32[]{:S(2)}) %copy-start.10) | copy-done | bytes 40
  5.5 1.9 %attend.1 = bf16[8,24,128]{2,1,0:T(8,128)(2,1)S(1)} custom-call(s32[1,4]{1,0:T(1,128)S(1)} %copy-done.10, s32[1]{0:T(128)S(6)} %copy.20.len_ref, bf16[1,3072]{1,0:T(2,128)(2,1)S(1)} %copy-done.6, bf16[1,512]{1,0:T(2,128)(2,1)S(1)} %copy-done.8, bf16[1,512]{1,0:T(2,128)(2,1)S(1)} %copy-done.9, bf16[4,128,512]{2,1,0:T(8,128)(2,1)S(1)} %copy-done.4, ...), custom_call_target="tpu_custom_call" | custom-call | tf_op jit(solution)/shard_map/attend/pallas_call | solution.py:295
  7.4 13.8 %all_to_all.15.attn_ref = bf16[8,24,128]{2,1,0:T(8,128)(2,1)S(1)} all-to-all(bf16[8,24,128]{2,1,0:T(8,128)(2,1)S(1)} %attend.1), channel_id=1, replica_groups=mesh['groups'=2,'units'=8,'heads'=2] {'units'}, dimensions={0} | all-to-all | bytes 98304 | tf_op jit(solution)/shard_map/all_to_all | solution.py:282
  21.3 0.0 copy-start.3
  21.3 2.3 %copy-done.3 = bf16[3072,768]{1,0:T(8,128)(2,1)S(1)} copy-done((bf16[3072,768]{1,0:T(8,128)(2,1)S(1)}, bf16[3072,768]{1,0:T(8,128)(2,1)}, u32[]{:S(2)}) %copy-start.3) | copy-done | bytes 4718616
  23.6 0.7 %proj.1.mine_ref = f32[8,768]{1,0:T(8,128)S(1)} custom-call(bf16[8,24,128]{2,1,0:T(8,128)(2,1)S(1)} %all_to_all.15.attn_ref, bf16[3072,768]{1,0:T(8,128)(2,1)S(1)} %copy-done.3), custom_call_target="tpu_custom_call" | custom-call | tf_op jit(solution)/shard_map/proj/pallas_call | solution.py:305
  24.3 0.0 collective-permute-start
  24.3 1.2 %collective-permute-done.other_ref = f32[8,768]{1,0:T(8,128)S(1)} collective-permute-done((f32[8,768]{1,0:T(8,128)S(1)}, f32[8,768]{1,0:T(8,128)S(1)}, u32[]{:S(2)}, u32[]{:S(2)}) %collective-permute-start) | collective-permute-done | bytes 24608 | tf_op jit(solution)/shard_map/ppermute | solution.py:308
  25.5 0.0 copy-start.7
  25.5 0.7 %copy-done.7 = bf16[8,768]{1,0:T(8,128)(2,1)S(1)} copy-done((bf16[8,768]{1,0:T(8,128)(2,1)S(1)}, bf16[8,768]{1,0:T(8,128)(2,1)}, u32[]{:S(2)}) %copy-start.7) | copy-done | bytes 12312
  26.2 0.7 %resid.1 = bf16[8,8,768]{2,1,0:T(8,128)(2,1)} custom-call(bf16[8,768]{1,0:T(8,128)(2,1)S(1)} %copy-done.7, f32[8,768]{1,0:T(8,128)S(1)} %proj.1.mine_ref, f32[8,768]{1,0:T(8,128)S(1)} %collective-permute-done.other_ref), custom_call_target="tpu_custom_call" | custom-call | tf_op jit(solution)/shard_map/resid/pallas_call | solution.py:309
  26.9 3.4 %all-to-all-start.1 = ((bf16[8,8,768]{2,1,0:T(8,128)(2,1)}), bf16[8,8,768]{2,1,0:T(8,128)(2,1)S(1)}, u32[]{:S(2)}, u32[]{:S(2)}) async-start(bf16[8,8,768]{2,1,0:T(8,128)(2,1)} %resid.1), calls=%async_computation.1 | async-start | bytes 196608 | tf_op jit(solution)/shard_map/all_to_all | solution.py:282
  30.2 0.8 %copy.19.routes_ref.routes_v_ref = s32[8,2]{1,0:T(8,128)S(1)} copy(s32[8,2]{0,1:T(2,128)} %param.26) | data formatting | bytes 128 | tf_op args[11]
  31.0 0.7 %reshape.3.gain_ref = bf16[1,6144]{1,0:T(2,128)(2,1)S(1)} reshape(bf16[6144]{0:T(1024)(128)(2,1)} %param.24) | data formatting | bytes 24576 | tf_op jit(solution)/shard_map/reshape | solution.py:328
  31.7 1.6 %copy.17.router_ref = bf16[6144,8]{1,0:T(8,128)(2,1)S(1)} copy(bf16[6144,8]{0,1:T(8,128)(2,1)} %param.25) | data formatting | bytes 196608 | tf_op args[10]
  33.3 4.0 %all-to-all-done.1.h1_ref = bf16[8,8,768]{2,1,0:T(8,128)(2,1)S(1)} async-done(((bf16[8,8,768]{2,1,0:T(8,128)(2,1)}), bf16[8,8,768]{2,1,0:T(8,128)(2,1)S(1)}, u32[]{:S(2)}, u32[]{:S(2)}) %all-to-all-start.1) | async-done | bytes 98336 | tf_op jit(solution)/shard_map/all_to_all | solution.py:282
  37.3 0.0 copy-start
  37.3 4.6 %copy-done = bf16[3072,2048]{1,0:T(8,128)(2,1)S(1)} copy-done((bf16[3072,2048]{1,0:T(8,128)(2,1)S(1)}, bf16[3072,2048]{1,0:T(8,128)(2,1)}, u32[]{:S(2)}) %copy-start) | copy-done | bytes 12582936
  41.9 0.0 copy-start.1
  41.9 4.6 %copy-done.1 = bf16[3072,2048]{1,0:T(8,128)(2,1)S(1)} copy-done((bf16[3072,2048]{1,0:T(8,128)(2,1)S(1)}, bf16[3072,2048]{1,0:T(8,128)(2,1)}, u32[]{:S(2)}) %copy-start.1) | copy-done | bytes 12582936
  46.5 0.0 copy-start.2
  46.5 4.4 %expert.1 = (f32[2,4096]{1,0:T(2,128)S(1)}, f32[2,128]{1,0:T(2,128)S(1)}, f32[1,3072]{1,0:T(1,128)S(1)}) custom-call(s32[8,2]{1,0:T(8,128)S(1)} %copy.19.routes_ref.routes_v_ref, bf16[8,8,768]{2,1,0:T(8,128)(2,1)S(1)} %all-to-all-done.1.h1_ref, bf16[1,6144]{1,0:T(2,128)(2,1)S(1)} %reshape.3.gain_ref, bf16[6144,8]{1,0:T(8,128)(2,1)S(1)} %copy.17.router_ref, ...), custom_call_target="tpu_custom_call" | custom-call | tf_op jit(solution)/shard_map/expert/pallas_call | solution.py:313
  50.9 0.0 collective-permute-start.1
  50.9 1.2 %collective-permute-done.1.other_ref = f32[2,4096]{1,0:T(2,128)S(1)} collective-permute-done((f32[2,4096]{1,0:T(2,128)S(1)}, f32[2,4096]{1,0:T(2,128)S(1)}, u32[]{:S(2)}, u32[]{:S(2)}) %collective-permute-start.1) | collective-permute-done | bytes 32800 | tf_op jit(solution)/shard_map/ppermute | solution.py:330
  52.1 0.0 copy-done.2
  52.1 2.4 %down.1 = f32[8,24,128]{2,1,0:T(8,128)S(1)} custom-call(s32[8,2]{1,0:T(8,128)S(1)} %copy.19.routes_ref.routes_v_ref, f32[2,4096]{1,0:T(2,128)S(1)} %get-tuple-element.8.mine_ref, f32[2,4096]{1,0:T(2,128)S(1)} %collective-permute-done.1.other_ref, f32[2,128]{1,0:T(2,128)S(1)} %get-tuple-element.9.route_ref, bf16[2048,3072]{1,0:T(8,128)(2,1)S(1)} %copy-done.2), custom_call_target="tpu_custom_call" | custom-call | tf_op jit(solution)/shard_map/down/pallas_call | solution.py:331
  54.5 9.5 %all_to_all.16.parts_ref = f32[8,24,128]{2,1,0:T(8,128)S(1)} all-to-all(f32[8,24,128]{2,1,0:T(8,128)S(1)} %down.1), channel_id=1, replica_groups=mesh['groups'=2,'units'=8,'heads'=2] {'units'}, dimensions={0} | all-to-all | bytes 196608 | tf_op jit(solution)/shard_map/all_to_all | solution.py:282
  64.0 0.6 total.1
Async XLA Ops:
  0.7 1.0 %copy-start.4 = (bf16[4,128,512]{2,1,0:T(8,128)(2,1)S(1)}, bf16[4,128,512]{2,1,0:T(8,128)(2,1)}, u32[]{:S(2)}) copy-start(bf16[4,128,512]{2,1,0:T(8,128)(2,1)} %k_ref.1) | copy-start | bytes 1572868
  1.7 1.0 %copy-start.5 = (bf16[4,128,512]{2,1,0:T(8,128)(2,1)S(1)}, bf16[4,128,512]{2,1,0:T(8,128)(2,1)}, u32[]{:S(2)}) copy-start(bf16[4,128,512]{2,1,0:T(8,128)(2,1)} %v_ref.1) | copy-start | bytes 1572868
  2.7 0.7 %copy-start.6 = (bf16[1,3072]{1,0:T(2,128)(2,1)S(1)}, bf16[1,3072]{1,0:T(2,128)(2,1)}, u32[]{:S(2)}) copy-start(bf16[1,3072]{1,0:T(2,128)(2,1)} %q_ref.1) | copy-start | bytes 18436
  3.4 0.7 %copy-start.8 = (bf16[1,512]{1,0:T(2,128)(2,1)S(1)}, bf16[1,512]{1,0:T(2,128)(2,1)}, u32[]{:S(2)}) copy-start(bf16[1,512]{1,0:T(2,128)(2,1)} %fk_ref.1) | copy-start | bytes 3076
  4.1 0.7 %copy-start.9 = (bf16[1,512]{1,0:T(2,128)(2,1)S(1)}, bf16[1,512]{1,0:T(2,128)(2,1)}, u32[]{:S(2)}) copy-start(bf16[1,512]{1,0:T(2,128)(2,1)} %fv_ref.1) | copy-start | bytes 3076
  4.8 0.7 %copy-start.10 = (s32[1,4]{1,0:T(1,128)S(1)}, s32[1,4]{1,0:T(1,128)}, u32[]{:S(2)}) copy-start(s32[1,4]{1,0:T(1,128)} %table_ref.1) | copy-start | bytes 52
  21.3 2.3 %copy-start.3 = (bf16[3072,768]{1,0:T(8,128)(2,1)S(1)}, bf16[3072,768]{1,0:T(8,128)(2,1)}, u32[]{:S(2)}) copy-start(bf16[3072,768]{1,0:T(8,128)(2,1)} %w_ref.1) | copy-start | bytes 14155780
  24.3 1.2 %collective-permute-start = (f32[8,768]{1,0:T(8,128)S(1)}, f32[8,768]{1,0:T(8,128)S(1)}, u32[]{:S(2)}, u32[]{:S(2)}) collective-permute-start(f32[8,768]{1,0:T(8,128)S(1)} %proj.1.mine_ref), channel_id=1, source_target_pairs={{0,1},{1,0},{2,3},{3,2},{4,5},{5,4},{6,7},{7,6},{8,9},{9,8},{10,11... | collective-permute-start | bytes 73736 | tf_op jit(solution)/shard_map/ppermute | solution.py:308
  25.5 0.7 %copy-start.7 = (bf16[8,768]{1,0:T(8,128)(2,1)S(1)}, bf16[8,768]{1,0:T(8,128)(2,1)}, u32[]{:S(2)}) copy-start(bf16[8,768]{1,0:T(8,128)(2,1)} %resid_ref.1) | copy-start | bytes 36868
  26.9 10.4 %all-to-all-start.1 = ((bf16[8,8,768]{2,1,0:T(8,128)(2,1)}), bf16[8,8,768]{2,1,0:T(8,128)(2,1)S(1)}, u32[]{:S(2)}, u32[]{:S(2)}) async-start(bf16[8,8,768]{2,1,0:T(8,128)(2,1)} %resid.1), calls=%async_computation.1 | async-start | bytes 196608 | tf_op jit(solution)/shard_map/all_to_all | solution.py:282
  37.3 4.6 %copy-start = (bf16[3072,2048]{1,0:T(8,128)(2,1)S(1)}, bf16[3072,2048]{1,0:T(8,128)(2,1)}, u32[]{:S(2)}) copy-start(bf16[3072,2048]{1,0:T(8,128)(2,1)} %wg_ref.1) | copy-start | bytes 37748740
  41.9 4.6 %copy-start.1 = (bf16[3072,2048]{1,0:T(8,128)(2,1)S(1)}, bf16[3072,2048]{1,0:T(8,128)(2,1)}, u32[]{:S(2)}) copy-start(bf16[3072,2048]{1,0:T(8,128)(2,1)} %wu_ref.1) | copy-start | bytes 37748740
  46.5 5.7 %copy-start.2 = (bf16[2048,3072]{1,0:T(8,128)(2,1)S(1)}, bf16[2048,3072]{1,0:T(8,128)(2,1)}, u32[]{:S(2)}) copy-start(bf16[2048,3072]{1,0:T(8,128)(2,1)} %wd_ref.1) | copy-start | bytes 37748740
  50.9 1.2 %collective-permute-start.1 = (f32[2,4096]{1,0:T(2,128)S(1)}, f32[2,4096]{1,0:T(2,128)S(1)}, u32[]{:S(2)}, u32[]{:S(2)}) collective-permute-start(f32[2,4096]{1,0:T(2,128)S(1)} %get-tuple-element.8.mine_ref), channel_id=1, source_target_pairs={{0,1},{1,0},{2,3},{3,2},{4,5},{5,4},{6,7},{7,6},{8,9},{9,8},{10,11... | collective-permute-start | bytes 98312 | tf_op jit(solution)/shard_map/ppermute | solution.py:330

commit v2 on v1

--- a/solution.py
+++ b/solution.py
@@ -126,7 +126,27 @@
     return (own_h1.astype(jnp.float32) + moe_own).astype(jnp.bfloat16)
 
 
-def attn_kernel(table_ref, len_ref, q_ref, fk_ref, fv_ref, k_ref, v_ref, o_ref):
+def attn_kernel(
+    len_ref, table_hbm, q_hbm, fk_hbm, fv_hbm, k_hbm, v_hbm, o_ref,
+    table_ref, q_ref, fk_ref, fv_ref, k_ref, v_ref, sems,
+):
+    copies = [
+        pltpu.make_async_copy(src, dst, sems.at[i])
+        for i, (src, dst) in enumerate(
+            (
+                (table_hbm, table_ref),
+                (q_hbm, q_ref),
+                (fk_hbm, fk_ref),
+                (k_hbm, k_ref),
+                (v_hbm, v_ref),
+                (fv_hbm, fv_ref),
+            )
+        )
+    ]
+    for copy in copies:
+        copy.start()
+    for copy in copies:
+        copy.wait()
     pages, page_tokens, kv_width = k_ref.shape
     heads_kv = kv_width // HEAD_WIDTH
     group = q_ref.shape[1] // kv_width
@@ -182,18 +202,18 @@
 
 
 def routed_rows(routes_ref):
-    count = routes_ref.shape[0]
+    count = routes_ref.shape[1]
     first = jnp.int32(count - 1)
     last = jnp.int32(0)
     for r in range(count):
-        hit = jnp.logical_or(routes_ref[r, 0] == 0, routes_ref[r, 1] == 0)
+        hit = jnp.logical_or(routes_ref[0, r] == 0, routes_ref[1, r] == 0)
         first = jnp.where(hit, jnp.minimum(first, r), first)
         last = jnp.where(hit, r, last)
     return first, last
 
 
 def expert_kernel(
-    routes_ref, h1_ref, gain_ref, router_ref, routes_v_ref, wg_ref, wu_ref, gu_ref, route_ref, own_ref,
+    routes_ref, h1_ref, gain_ref, router_ref, wg_ref, wu_ref, gu_ref, route_ref, own_ref,
     gu_all, route_all, own_all,
 ):
     units = h1_ref.shape[0]
@@ -202,7 +222,7 @@
     head = lax.axis_index("heads")
     unit = lax.axis_index("units")
     h1 = jnp.concatenate([h1_ref[u] for u in range(units)], axis=1).astype(F32)
-    gain = gain_ref[...].astype(F32)
+    gain = gain_ref[...].astype(F32).reshape(1, -1)
     rstd = lax.rsqrt(jnp.mean(h1 * h1, axis=1, keepdims=True) + 1e-05)
     xn = (h1 * rstd * gain).astype(BF16)
     x_half = jnp.where(head == 0, xn[:, :half].astype(F32), xn[:, half:].astype(F32)).astype(BF16)
@@ -210,10 +230,16 @@
     own_ref[...] = own_all[pl.ds(unit, 1), :]
     gu_all[:, :hidden] = jnp.dot(x_half, wg_ref[...], preferred_element_type=F32)
     gu_all[:, hidden:] = jnp.dot(x_half, wu_ref[...], preferred_element_type=F32)
-    logits = jnp.dot(xn, router_ref[...], preferred_element_type=F32)
+    logits = lax.dot_general(
+        xn, router_ref[...], (((1,), (1,)), ((), ())), preferred_element_type=F32
+    )
     expert_ids = lax.broadcasted_iota(jnp.int32, logits.shape, 1)
-    one = routes_v_ref[:, 0:1]
-    two = routes_v_ref[:, 1:2]
+    row_ids = lax.broadcasted_iota(jnp.int32, (h1.shape[0], 1), 0)
+    one = jnp.zeros(row_ids.shape, jnp.int32)
+    two = jnp.zeros(row_ids.shape, jnp.int32)
+    for r in range(h1.shape[0]):
+        one = jnp.where(row_ids == r, routes_ref[0, r], one)
+        two = jnp.where(row_ids == r, routes_ref[1, r], two)
     chosen_one = jnp.sum(jnp.where(expert_ids == one, logits, 0.0), axis=1, keepdims=True)
     chosen_two = jnp.sum(jnp.where(expert_ids == two, logits, 0.0), axis=1, keepdims=True)
     diff = jnp.where(one == 0, chosen_one - chosen_two, chosen_two - chosen_one)
@@ -248,6 +274,11 @@
 
 SMEM = pl.BlockSpec(memory_space=pltpu.SMEM)
 VMEM = pl.BlockSpec(memory_space=pltpu.VMEM)
+ANY = pl.BlockSpec(memory_space=pltpu.HBM)
+
+
+def in_hbm(x):
+    return pltpu.with_memory_space_constraint(x, pltpu.HBM)
 
 
 def in_vmem(x):
@@ -277,29 +308,46 @@
     hidden = w_gate.shape[1]
     cols = w_out.shape[1]
     swap = [(0, 1), (1, 0)]
+    routes_t = routes.T
 
     def exchange(x):
         return lax.all_to_all(x, "units", split_axis=0, concat_axis=0, tiled=True)
 
-    def call(kernel, out, specs, name, scratch=(), limit=6):
-        return pl.pallas_call(
-            kernel,
+    def call(kernel, out, specs, name, scratch=(), limit=6, more=()):
+        more = [in_hbm(w) for w in more]
+
+        def whole(*refs):
+            n = len(specs)
+            kernel(*refs[:n], *refs[n + len(more):])
+
+        f = pl.pallas_call(
+            whole,
             out_shape=out,
-            in_specs=specs,
+            in_specs=specs + [ANY] * len(more),
             out_specs=jax.tree.map(lambda _: VMEM, out),
             scratch_shapes=scratch,
             compiler_params=pltpu.CompilerParams(vmem_limit_bytes=limit * MIB),
             name=name,
         )
+        return lambda *ops: f(*ops, *more)
 
     attn = call(
         attn_kernel,
         jax.ShapeDtypeStruct((rows, chunks, LANES), BF16),
-        [SMEM, SMEM, VMEM, VMEM, VMEM, VMEM, VMEM],
+        [SMEM] + [ANY] * 6,
         "attend",
+        scratch=(
+            pltpu.SMEM(page_table.shape, page_table.dtype),
+            *(
+                pltpu.VMEM(x.shape, x.dtype)
+                for x in (queries, fresh_key, fresh_value, key_cache_pages, value_cache_pages)
+            ),
+            pltpu.SemaphoreType.DMA((6,)),
+        ),
+        more=(w_gate, w_up, w_down),
     )(
-        page_table, lengths, queries, fresh_key, fresh_value,
-        in_vmem(key_cache_pages), in_vmem(value_cache_pages),
+        lengths,
+        *map(in_hbm, (page_table, queries, fresh_key, fresh_value, key_cache_pages, value_cache_pages)),
     )
     attn_all = exchange(attn)
     proj = call(proj_kernel, jax.ShapeDtypeStruct((rows, cols), F32), [VMEM] * 2, "proj")(
@@ -317,7 +365,7 @@
             jax.ShapeDtypeStruct((2, LANES), F32),
             jax.ShapeDtypeStruct((1, half), F32),
         ),
-        [SMEM] + [VMEM] * 6,
+        [SMEM] + [VMEM] * 5,
         "expert",
         scratch=(
             pltpu.VMEM((rows, 2 * hidden), F32),
@@ -325,7 +373,7 @@
             pltpu.VMEM((rows, half), F32),
         ),
     )(
-        routes, h1, norm_gain.reshape(1, -1), in_vmem(router), routes, in_vmem(w_gate), in_vmem(w_up)
+        routes_t, h1, norm_gain, router.T, in_vmem(w_gate), in_vmem(w_up)
     )
     gu_other = lax.ppermute(gu, "heads", swap)
     full = call(
@@ -333,7 +381,7 @@
         jax.ShapeDtypeStruct((rows, chunks, LANES), F32),
         [SMEM] + [VMEM] * 4,
         "down",
-    )(routes, gu, gu_other, route, in_vmem(w_down))
+    )(routes_t, gu, gu_other, route, in_vmem(w_down))
     parts = exchange(full)
     return call(sum_kernel, jax.ShapeDtypeStruct((1, half), BF16), [VMEM] * 2, "total")(
         parts, own_h1

time: 65.4 us -> 47.9 us (0.73)
  local copies, waits for them, and re-layouts: 20 us -> 0.06 us
  blocking collectives: 23.4 us -> 33.1 us
  waiting for transfers between devices: 6.41 us -> 2.39 us
  starting transfers between devices: 3.39 us -> 0.05 us
    unnamed x24 -> x28, local copies, waits for them, and re-layouts: 19.3 us -> 0.06 us
    all_to_all x2 -> x3, blocking collectives: 23.4 us -> 33.1 us  [exchange(): return lax.all_to_all(x, 'units', split_axis=0, concat_axis=0, tiled=True)]
    all_to_all x1 -> x0, waiting for transfers between devices: 4 us -> none  [exchange(): return lax.all_to_all(x, 'units', split_axis=0, concat_axis=0, tiled=True)]
    all_to_all x1 -> x0, starting transfers between devices: 3.36 us -> none  [exchange(): return lax.all_to_all(x, 'units', split_axis=0, concat_axis=0, tiled=True)]
    reshape x1 -> x0, local copies, waits for them, and re-layouts: 0.72 us -> none  [small_body(): norm_gain.reshape(1, -1)]
  transfers between devices with their start and end apart: 3 -> 2, of which waited for: 3 -> 2; matrix products, arithmetic and copies ran while one was open for 5% -> 0% of each run, Pallas kernels for 0% -> 0%
where the time goes in v2:
time: 47.9 us; the launch traced here: 47.7 us
  blocking collectives  33.1 us (69%)
  Pallas kernels  11 us (23%)
  waiting for transfers between devices  2.39 us (5%)
  between operations  1 us (2%)
    all_to_all x3, blocking collectives, exchange(): return lax.all_to_all(x, 'units', split_axis=0, concat_axis=0, tiled=True)  33.1 us
    pallas_call x6, Pallas kernels, call(): return lambda *ops: f(*ops, *more)  11 us
    ppermute x1, waiting for transfers between devices, small_body(): proj_other = lax.ppermute(proj, 'heads', swap)  1.2 us
    ppermute x1, waiting for transfers between devices, small_body(): gu_other = lax.ppermute(gu, 'heads', swap)  1.19 us
  transfers between devices with their start and end apart: 2, of which 2 were waited for; matrix products, arithmetic and copies ran while one was open for 0% of the time, Pallas kernels for 0%

profile of v2, /device:TPU:0, one launch (start us, length us, event | category | flops | bytes accessed | tf_op | source)
XLA Modules:
  0.0 47.7 jit_solution(5441400960648497837)
XLA Ops:
  0.0 0.0 slice-start
  0.0 0.0 slice-start.3
  0.8 0.0 copy-start
  0.8 0.0 copy-start.3
  0.8 0.0 slice-start.1
  0.8 0.0 slice-start.2
  0.8 0.0 slice-start.4
  0.9 0.0 slice-start.5
  0.9 0.0 copy-start.1
  0.9 0.0 copy-start.2
  0.9 0.0 copy-start.4
  0.9 3.1 %attend.1 = bf16[8,24,128]{2,1,0:T(8,128)(2,1)S(1)} custom-call(s32[1]{0:T(128)S(6)} %copy.16.refs_0_, s32[1,4]{1,0:T(1,128)} %refs_1_.2, bf16[1,3072]{1,0:T(2,128)(2,1)} %refs_2_.2, bf16[1,512]{1,0:T(2,128)(2,1)} %refs_3_.1, bf16[1,512]{1,0:T(2,128)(2,1)} %refs_4_.3, bf16[4,128,512]{2,1,0:T(8,128)(2,1)} %refs_5_.2, bf16[4,128,512]{2,1,0:T(8,128)(2,1)} %refs_6_.1, ...), custom_call_target="tpu_custom_call" | custom-call | tf_op jit(solution)/shard_map/attend/pallas_call | solution.py:332
  4.0 14.1 %all_to_all.15.refs_0_ = bf16[8,24,128]{2,1,0:T(8,128)(2,1)S(1)} all-to-all(bf16[8,24,128]{2,1,0:T(8,128)(2,1)S(1)} %attend.1), channel_id=1, replica_groups=mesh['groups'=2,'units'=8,'heads'=2] {'units'}, dimensions={0} | all-to-all | bytes 98304 | tf_op jit(solution)/shard_map/all_to_all | solution.py:314
  18.1 0.0 copy-done
  18.2 0.0 slice-start.6
  18.2 0.7 %proj.1.refs_1_ = f32[8,768]{1,0:T(8,128)S(1)} custom-call(bf16[8,24,128]{2,1,0:T(8,128)(2,1)S(1)} %all_to_all.15.refs_0_, bf16[3072,768]{1,0:T(8,128)(2,1)S(1)} %copy-done), custom_call_target="tpu_custom_call" | custom-call | tf_op jit(solution)/shard_map/proj/pallas_call | solution.py:332
  18.9 0.0 collective-permute-start
  18.9 1.2 %collective-permute-done.refs_2_ = f32[8,768]{1,0:T(8,128)S(1)} collective-permute-done((f32[8,768]{1,0:T(8,128)S(1)}, f32[8,768]{1,0:T(8,128)S(1)}, u32[]{:S(2)}, u32[]{:S(2)}) %collective-permute-start) | collective-permute-done | bytes 24608 | tf_op jit(solution)/shard_map/ppermute | solution.py:356
  20.1 0.0 copy-done.3
  20.1 9.5 %all_to_all.16.refs_1_ = bf16[8,8,768]{2,1,0:T(8,128)(2,1)S(1)} all-to-all(bf16[8,8,768]{2,1,0:T(8,128)(2,1)S(1)} %resid.1), channel_id=1, replica_groups=mesh['groups'=2,'units'=8,'heads'=2] {'units'}, dimensions={0} | all-to-all | bytes 196608 | tf_op jit(solution)/shard_map/all_to_all | solution.py:314
  29.6 0.0 slice-done
  29.6 0.0 slice-done.3
  29.6 0.0 slice-done.1
  29.6 0.0 slice-done.2
  29.6 0.0 slice-done.4
  29.6 0.0 slice-done.5
  29.6 0.0 copy-done.1
  29.7 0.0 copy-done.2
  29.7 0.0 copy-done.4
  29.7 0.0 slice-start.7
  29.7 0.0 slice-start.8
  29.7 4.2 %expert.1 = (f32[2,4096]{1,0:T(2,128)S(1)}, f32[2,128]{1,0:T(2,128)S(1)}, f32[1,3072]{1,0:T(1,128)S(1)}) custom-call(s32[2,8]{1,0:T(2,128)S(1)} %bitcast.9, bf16[8,8,768]{2,1,0:T(8,128)(2,1)S(1)} %all_to_all.16.refs_1_, bf16[6144]{0:T(1024)(128)(2,1)S(1)} %copy-done.2, bf16[8,6144]{1,0:T(8,128)(2,1)S(1)} %bitcast.8, bf16[3072,2048]{1,0:T(8,128)(2,1)S(1)} %bitcast.3, ...), custom_call_target="tpu_custom_call" | custom-call | tf_op jit(solution)/shard_map/expert/pallas_call | solution.py:332
  33.9 0.1 collective-permute-start.1
  34.0 1.2 %collective-permute-done.1.refs_2_ = f32[2,4096]{1,0:T(2,128)S(1)} collective-permute-done((f32[2,4096]{1,0:T(2,128)S(1)}, f32[2,4096]{1,0:T(2,128)S(1)}, u32[]{:S(2)}, u32[]{:S(2)}) %collective-permute-start.1) | collective-permute-done | bytes 32800 | tf_op jit(solution)/shard_map/ppermute | solution.py:378
  35.2 0.0 slice-done.6
  35.2 0.0 slice-done.7
  35.2 0.0 slice-done.8
  35.2 2.3 %down.1 = f32[8,24,128]{2,1,0:T(8,128)S(1)} custom-call(s32[2,8]{1,0:T(2,128)S(1)} %bitcast.10, f32[2,4096]{1,0:T(2,128)S(1)} %get-tuple-element.8.refs_1_, f32[2,4096]{1,0:T(2,128)S(1)} %collective-permute-done.1.refs_2_, f32[2,128]{1,0:T(2,128)S(1)} %get-tuple-element.9.refs_3_, bf16[2048,3072]{1,0:T(8,128)(2,1)S(1)} %bitcast.7), custom_call_target="tpu_custom_call" | custom-call | tf_op jit(solution)/shard_map/down/pallas_call | solution.py:332
  37.5 9.5 %all_to_all.17.refs_0_ = f32[8,24,128]{2,1,0:T(8,128)S(1)} all-to-all(f32[8,24,128]{2,1,0:T(8,128)S(1)} %down.1), channel_id=1, replica_groups=mesh['groups'=2,'units'=8,'heads'=2] {'units'}, dimensions={0} | all-to-all | bytes 196608 | tf_op jit(solution)/shard_map/all_to_all | solution.py:314
  47.0 0.6 %total.1 = bf16[1,3072]{1,0:T(2,128)(2,1)} custom-call(f32[8,24,128]{2,1,0:T(8,128)S(1)} %all_to_all.17.refs_0_, f32[1,3072]{1,0:T(1,128)S(1)} %get-tuple-element.10.refs_1_), custom_call_target="tpu_custom_call" | custom-call | tf_op jit(solution)/shard_map/total/pallas_call | solution.py:332
  (4 shorter events, 0.0 us)
Async XLA Ops:
  0.0 29.6 %slice-start = ((s8[12582912]{0:T(1024)(128)(4,1)}), s8[4194304]{0:T(1024)(128)(4,1)S(1)}, s32[]{:S(2)}) async-start(s8[12582912]{0:T(1024)(128)(4,1)} %bitcast.2), calls=%async_computation.3 | async-start | bytes 8388608
  0.0 29.6 %slice-start.3 = ((s8[12582912]{0:T(1024)(128)(4,1)}), s8[4194304]{0:T(1024)(128)(4,1)S(1)}, s32[]{:S(2)}) async-start(s8[12582912]{0:T(1024)(128)(4,1)} %bitcast.4), calls=%async_computation.6 | async-start | bytes 8388608
  0.8 17.3 %copy-start = (bf16[3072,768]{1,0:T(8,128)(2,1)S(1)}, bf16[3072,768]{1,0:T(8,128)(2,1)}, u32[]{:S(2)}) copy-start(bf16[3072,768]{1,0:T(8,128)(2,1)} %refs_1_.3) | copy-start | bytes 14155780
  0.8 19.3 %copy-start.3 = (bf16[8,768]{1,0:T(8,128)(2,1)S(1)}, bf16[8,768]{1,0:T(8,128)(2,1)}, u32[]{:S(2)}) copy-start(bf16[8,768]{1,0:T(8,128)(2,1)} %refs_0_.2) | copy-start | bytes 36868
  0.8 28.8 %slice-start.1 = ((s8[12582912]{0:T(1024)(128)(4,1)}), s8[4194304]{0:T(1024)(128)(4,1)S(1)}, s32[]{:S(2)}) async-start(s8[12582912]{0:T(1024)(128)(4,1)} %bitcast.2), calls=%async_computation.4 | async-start | bytes 8388608
  0.8 28.8 %slice-start.2 = ((s8[12582912]{0:T(1024)(128)(4,1)}), s8[4194304]{0:T(1024)(128)(4,1)S(1)}, s32[]{:S(2)}) async-start(s8[12582912]{0:T(1024)(128)(4,1)} %bitcast.2), calls=%async_computation.5 | async-start | bytes 8388608
  0.8 28.8 %slice-start.4 = ((s8[12582912]{0:T(1024)(128)(4,1)}), s8[4194304]{0:T(1024)(128)(4,1)S(1)}, s32[]{:S(2)}) async-start(s8[12582912]{0:T(1024)(128)(4,1)} %bitcast.4), calls=%async_computation.7 | async-start | bytes 8388608
  0.9 28.8 %slice-start.5 = ((s8[12582912]{0:T(1024)(128)(4,1)}), s8[4194304]{0:T(1024)(128)(4,1)S(1)}, s32[]{:S(2)}) async-start(s8[12582912]{0:T(1024)(128)(4,1)} %bitcast.4), calls=%async_computation.8 | async-start | bytes 8388608
  0.9 28.8 %copy-start.1 = (bf16[6144,8]{0,1:T(8,128)(2,1)S(1)}, bf16[6144,8]{0,1:T(8,128)(2,1)}, u32[]{:S(2)}) copy-start(bf16[6144,8]{0,1:T(8,128)(2,1)} %param.25) | copy-start | bytes 294916
  0.9 28.8 %copy-start.2 = (bf16[6144]{0:T(1024)(128)(2,1)S(1)}, bf16[6144]{0:T(1024)(128)(2,1)}, u32[]{:S(2)}) copy-start(bf16[6144]{0:T(1024)(128)(2,1)} %refs_2_.3) | copy-start | bytes 36868
  0.9 28.8 %copy-start.4 = (s32[8,2]{0,1:T(2,128)S(1)}, s32[8,2]{0,1:T(2,128)}, u32[]{:S(2)}) copy-start(s32[8,2]{0,1:T(2,128)} %param.26) | copy-start | bytes 196
  18.2 17.0 %slice-start.6 = ((s8[12582912]{0:T(1024)(128)(4,1)}), s8[4194304]{0:T(1024)(128)(4,1)S(1)}, s32[]{:S(2)}) async-start(s8[12582912]{0:T(1024)(128)(4,1)} %bitcast.6), calls=%async_computation.9 | async-start | bytes 8388608
  18.9 1.2 %collective-permute-start = (f32[8,768]{1,0:T(8,128)S(1)}, f32[8,768]{1,0:T(8,128)S(1)}, u32[]{:S(2)}, u32[]{:S(2)}) collective-permute-start(f32[8,768]{1,0:T(8,128)S(1)} %proj.1.refs_1_), channel_id=1, source_target_pairs={{0,1},{1,0},{2,3},{3,2},{4,5},{5,4},{6,7},{7,6},{8,9},{9,8},{10,11... | collective-permute-start | bytes 73736 | tf_op jit(solution)/shard_map/ppermute | solution.py:356
  29.7 5.5 %slice-start.7 = ((s8[12582912]{0:T(1024)(128)(4,1)}), s8[4194304]{0:T(1024)(128)(4,1)S(1)}, s32[]{:S(2)}) async-start(s8[12582912]{0:T(1024)(128)(4,1)} %bitcast.6), calls=%async_computation.10 | async-start | bytes 8388608
  29.7 5.5 %slice-start.8 = ((s8[12582912]{0:T(1024)(128)(4,1)}), s8[4194304]{0:T(1024)(128)(4,1)S(1)}, s32[]{:S(2)}) async-start(s8[12582912]{0:T(1024)(128)(4,1)} %bitcast.6), calls=%async_computation.11 | async-start | bytes 8388608
  33.9 1.3 %collective-permute-start.1 = (f32[2,4096]{1,0:T(2,128)S(1)}, f32[2,4096]{1,0:T(2,128)S(1)}, u32[]{:S(2)}, u32[]{:S(2)}) collective-permute-start(f32[2,4096]{1,0:T(2,128)S(1)} %get-tuple-element.8.refs_1_), channel_id=1, source_target_pairs={{0,1},{1,0},{2,3},{3,2},{4,5},{5,4},{6,7},{7,6},{8,9},{9,8},{10,11... | collective-permute-start | bytes 98312 | tf_op jit(solution)/shard_map/ppermute | solution.py:378

commit v3 on v2

--- a/solution.py
+++ b/solution.py
@@ -130,23 +130,19 @@
     len_ref, table_hbm, q_hbm, fk_hbm, fv_hbm, k_hbm, v_hbm, o_ref,
     table_ref, q_ref, fk_ref, fv_ref, k_ref, v_ref, sems,
 ):
-    copies = [
-        pltpu.make_async_copy(src, dst, sems.at[i])
-        for i, (src, dst) in enumerate(
-            (
-                (table_hbm, table_ref),
-                (q_hbm, q_ref),
-                (fk_hbm, fk_ref),
-                (k_hbm, k_ref),
-                (v_hbm, v_ref),
-                (fv_hbm, fv_ref),
-            )
-        )
-    ]
-    for copy in copies:
+    pairs = {
+        "q": (q_hbm, q_ref),
+        "fk": (fk_hbm, fk_ref),
+        "table": (table_hbm, table_ref),
+        "k": (k_hbm, k_ref),
+        "v": (v_hbm, v_ref),
+        "fv": (fv_hbm, fv_ref),
+    }
+    copies = {
+        name: pltpu.make_async_copy(src, dst, sems.at[i]) for i, (name, (src, dst)) in enumerate(pairs.items())
+    }
+    for copy in copies.values():
         copy.start()
-    for copy in copies:
-        copy.wait()
     pages, page_tokens, kv_width = k_ref.shape
     heads_kv = kv_width // HEAD_WIDTH
     group = q_ref.shape[1] // kv_width
@@ -154,36 +150,59 @@
     span = pages * page_tokens
     scale = HEAD_WIDTH ** (-0.5)
     length = len_ref[0]
+    pad = [jnp.zeros((rows - group, HEAD_WIDTH), F32)] if rows > group else []
+    live = lax.broadcasted_iota(jnp.int32, (rows, span), 1) < length
+    heads = [slice(g * HEAD_WIDTH, (g + 1) * HEAD_WIDTH) for g in range(heads_kv)]
+    copies["q"].wait()
+    copies["fk"].wait()
     q = q_ref[...].astype(F32)
     fk = fk_ref[...].astype(F32)
-    fv = fv_ref[...].astype(F32)
-    pad = [jnp.zeros((rows - group, HEAD_WIDTH), F32)] if rows > group else []
-    live = lax.broadcasted_iota(jnp.int32, (rows, span), 1) < length
-    blended = []
-    for g in range(heads_kv):
-        lanes = slice(g * HEAD_WIDTH, (g + 1) * HEAD_WIDTH)
-        first = g * group
-        q_g = jnp.concatenate(
-            [q[:, (first + j) * HEAD_WIDTH : (first + j + 1) * HEAD_WIDTH] for j in range(group)] + pad,
+    q_grid = [
+        jnp.concatenate(
+            [q[:, (g * group + j) * HEAD_WIDTH : (g * group + j + 1) * HEAD_WIDTH] for j in range(group)] + pad,
             axis=0,
         )
-        keys = jnp.concatenate([k_ref[table_ref[0, p], :, lanes] for p in range(pages)], axis=0)
-        values = jnp.concatenate([v_ref[table_ref[0, p], :, lanes] for p in range(pages)], axis=0)
-        s = (
-            lax.dot_general(
-                q_g.astype(BF16), keys, (((1,), (1,)), ((), ())), preferred_element_type=F32
-            )
-            * scale
+        for g in range(heads_kv)
+    ]
+    owns = [
+        jnp.sum(q_g * fk[:, lanes], axis=1, keepdims=True) * scale for q_g, lanes in zip(q_grid, heads)
+    ]
+    q_grid = [q_g.astype(BF16) for q_g in q_grid]
+    copies["table"].wait()
+    copies["k"].wait()
+    table = [table_ref[0, p] for p in range(pages)]
+    scores = [
+        lax.dot_general(
+            q_g,
+            jnp.concatenate([k_ref[page, :, lanes] for page in table], axis=0),
+            (((1,), (1,)), ((), ())),
+            preferred_element_type=F32,
         )
-        own = jnp.sum(q_g * fk[:, lanes], axis=1, keepdims=True) * scale
+        * scale
+        for q_g, lanes in zip(q_grid, heads)
+    ]
+    weights, own_weights = [], []
+    for s, own in zip(scores, owns):
         top = jnp.maximum(jnp.max(jnp.where(live, s, -jnp.inf), axis=1, keepdims=True), own)
         prob = jnp.where(live, jnp.exp(s - top), 0.0)
         own_p = jnp.exp(own - top)
         total = jnp.sum(prob, axis=1, keepdims=True) + own_p
-        weights = (prob / total).astype(BF16)
-        own_weight = (own_p / total).astype(BF16).astype(F32)
-        out = jnp.dot(weights, values, preferred_element_type=F32) + own_weight * fv[:, lanes]
-        blended.append(out[:group])
+        weights.append((prob / total).astype(BF16))
+        own_weights.append((own_p / total).astype(BF16).astype(F32))
+    copies["v"].wait()
+    copies["fv"].wait()
+    fv = fv_ref[...].astype(F32)
+    blended = [
+        (
+            jnp.dot(
+                w,
+                jnp.concatenate([v_ref[page, :, lanes] for page in table], axis=0),
+                preferred_element_type=F32,
+            )
+            + own_w * fv[:, lanes]
+        )[:group]
+        for w, own_w, lanes in zip(weights, own_weights, heads)
+    ]
     attn = jnp.concatenate(blended, axis=0).astype(BF16)
     for r in range(o_ref.shape[0]):
         o_ref[r] = attn
@@ -212,61 +231,66 @@
     return first, last
 
 
-def expert_kernel(
-    routes_ref, h1_ref, gain_ref, router_ref, wg_ref, wu_ref, gu_ref, route_ref, own_ref,
-    gu_all, route_all, own_all,
-):
-    units = h1_ref.shape[0]
-    half = wg_ref.shape[0]
+def expert_kernel(routes_ref, h1_ref, gain_ref, wg_ref, wu_ref, gu_ref, gu_all):
+    units, _, cols = h1_ref.shape
     hidden = wg_ref.shape[1]
+    per_half = units // 2
+    head = lax.axis_index("heads")
+    half = per_half * cols
+    gain = gain_ref[...].astype(F32).reshape(1, -1)
+    gain = jnp.where(head == 0, gain[:, :half], gain[:, half:])
+    h1 = jnp.concatenate([h1_ref[head * per_half + i] for i in range(per_half)], axis=1).astype(F32)
+    x = (h1 * gain).astype(BF16)
+    gu_all[:, :hidden] = jnp.dot(x, wg_ref[...], preferred_element_type=F32)
+    gu_all[:, hidden:] = jnp.dot(x, wu_ref[...], preferred_element_type=F32)
+    for slot, r in enumerate(routed_rows(routes_ref)):
+        gu_ref[slot : slot + 1, :] = gu_all[pl.ds(r, 1), :]
+
+
+def side_kernel(routes_ref, h1_ref, gain_ref, router_ref, stat_ref, own_ref, h_all, router_all):
+    units, _, cols = h1_ref.shape
+    per_half = units // 2
     head = lax.axis_index("heads")
     unit = lax.axis_index("units")
-    h1 = jnp.concatenate([h1_ref[u] for u in range(units)], axis=1).astype(F32)
+    for u in range(units):
+        h_all[:, u * cols : (u + 1) * cols] = h1_ref[u].astype(F32)
+    own = h_all[pl.ds(unit, 1), :]
+    half = per_half * cols
+    own_ref[...] = jnp.where(head == 0, own[:, :half], own[:, half:])
+    router_all[...] = router_ref[...].astype(F32)
     gain = gain_ref[...].astype(F32).reshape(1, -1)
-    rstd = lax.rsqrt(jnp.mean(h1 * h1, axis=1, keepdims=True) + 1e-05)
-    xn = (h1 * rstd * gain).astype(BF16)
-    x_half = jnp.where(head == 0, xn[:, :half].astype(F32), xn[:, half:].astype(F32)).astype(BF16)
-    own_all[...] = jnp.where(head == 0, h1[:, :half], h1[:, half:])
-    own_ref[...] = own_all[pl.ds(unit, 1), :]
-    gu_all[:, :hidden] = jnp.dot(x_half, wg_ref[...], preferred_element_type=F32)
-    gu_all[:, hidden:] = jnp.dot(x_half, wu_ref[...], preferred_element_type=F32)
-    logits = lax.dot_general(
-        xn, router_ref[...], (((1,), (1,)), ((), ())), preferred_element_type=F32
-    )
-    expert_ids = lax.broadcasted_iota(jnp.int32, logits.shape, 1)
-    row_ids = lax.broadcasted_iota(jnp.int32, (h1.shape[0], 1), 0)
-    one = jnp.zeros(row_ids.shape, jnp.int32)
-    two = jnp.zeros(row_ids.shape, jnp.int32)
-    for r in range(h1.shape[0]):
-        one = jnp.where(row_ids == r, routes_ref[0, r], one)
-        two = jnp.where(row_ids == r, routes_ref[1, r], two)
-    chosen_one = jnp.sum(jnp.where(expert_ids == one, logits, 0.0), axis=1, keepdims=True)
-    chosen_two = jnp.sum(jnp.where(expert_ids == two, logits, 0.0), axis=1, keepdims=True)
-    diff = jnp.where(one == 0, chosen_one - chosen_two, chosen_two - chosen_one)
-    route = jnp.where(jnp.logical_or(one == 0, two == 0), 1.0 / (1.0 + jnp.exp(-diff)), 0.0)
-    route_all[...] = jnp.broadcast_to(route, route_all.shape)
     for slot, r in enumerate(routed_rows(routes_ref)):
-        gu_ref[slot : slot + 1, :] = gu_all[pl.ds(r, 1), :]
-        route_ref[slot : slot + 1, :] = route_all[pl.ds(r, 1), :]
-
-
-def down_kernel(routes_ref, mine_ref, other_ref, route_ref, wd_ref, o_ref):
+        h = h_all[pl.ds(r, 1), :]
+        rstd = lax.rsqrt(jnp.mean(h * h, axis=1, keepdims=True) + 1e-05)
+        xn = (h * rstd * gain).astype(BF16).astype(F32)
+        other = jnp.where(routes_ref[0, r] == 0, routes_ref[1, r], routes_ref[0, r])
+        diff = jnp.sum(xn * router_all[0:1, :], axis=1, keepdims=True) - jnp.sum(
+            xn * router_all[pl.ds(other, 1), :], axis=1, keepdims=True
+        )
+        route = 1.0 / (1.0 + jnp.exp(-diff))
+        lane_ids = lax.broadcasted_iota(jnp.int32, (1, LANES), 1)
+        stat_ref[slot : slot + 1, :] = jnp.where(lane_ids == 0, rstd, route)
+
+
+def down_kernel(routes_ref, mine_ref, other_ref, stat_ref, wd_ref, o16_ref, o_ref):
     hidden = wd_ref.shape[0]
-    gu = mine_ref[...] + other_ref[...]
-    gate = gu[:, :hidden]
-    up = gu[:, hidden:]
-    act = (gate / (1.0 + jnp.exp(-gate)) * up * route_ref[:, 0:1]).astype(BF16)
+    rstd = stat_ref[:, 0:1]
+    route = stat_ref[:, 1:2]
+    gate = (mine_ref[:, :hidden] + other_ref[:, :hidden]) * rstd
+    up = (mine_ref[:, hidden:] + other_ref[:, hidden:]) * (rstd * route)
+    act = (gate / (1.0 + jnp.exp(-gate)) * up).astype(BF16)
     full = jnp.dot(act, wd_ref[...], preferred_element_type=F32)
     o_ref[...] = jnp.zeros(o_ref.shape, F32)
     for slot, r in enumerate(routed_rows(routes_ref)):
         for j in range(o_ref.shape[1]):
             o_ref[r, j : j + 1, :] = full[slot : slot + 1, j * LANES : (j + 1) * LANES]
+    o16_ref[...] = o_ref[...].astype(BF16)
 
 
 def sum_kernel(parts_ref, own_ref, o_ref):
-    moe = parts_ref[0]
+    moe = parts_ref[0].astype(F32)
     for u in range(1, parts_ref.shape[0]):
-        moe = moe + parts_ref[u]
+        moe = moe + parts_ref[u].astype(F32)
     for j in range(parts_ref.shape[1]):
         lanes = slice(j * LANES, (j + 1) * LANES)
         o_ref[:, lanes] = (own_ref[:, lanes] + moe[j : j + 1, :]).astype(o_ref.dtype)
@@ -358,30 +382,28 @@
         resid_kernel, jax.ShapeDtypeStruct((rows, rows, cols), BF16), [VMEM] * 3, "resid"
     )(resid, proj, proj_other)
     h1 = exchange(h1_cols)
-    gu, route, own_h1 = call(
+    gu = call(
         expert_kernel,
-        (
-            jax.ShapeDtypeStruct((2, 2 * hidden), F32),
-            jax.ShapeDtypeStruct((2, LANES), F32),
-            jax.ShapeDtypeStruct((1, half), F32),
-        ),
-        [SMEM] + [VMEM] * 5,
+        jax.ShapeDtypeStruct((2, 2 * hidden), F32),
+        [SMEM] + [VMEM] * 4,
         "expert",
-        scratch=(
-            pltpu.VMEM((rows, 2 * hidden), F32),
-            pltpu.VMEM((rows, LANES), F32),
-            pltpu.VMEM((rows, half), F32),
-        ),
-    )(
-        routes_t, h1, norm_gain, router.T, in_vmem(w_gate), in_vmem(w_up)
-    )
+        scratch=(pltpu.VMEM((rows, 2 * hidden), F32),),
+    )(routes_t, h1, norm_gain, in_vmem(w_gate), in_vmem(w_up))
     gu_other = lax.ppermute(gu, "heads", swap)
+    stat, own_h1 = call(
+        side_kernel,
+        (jax.ShapeDtypeStruct((2, LANES), F32), jax.ShapeDtypeStruct((1, half), F32)),
+        [SMEM] + [VMEM] * 3,
+        "side",
+        scratch=(pltpu.VMEM((rows, 2 * half), F32), pltpu.VMEM(router.shape[::-1], F32)),
+    )(routes_t, h1, norm_gain, router.T)
     full = call(
         down_kernel,
-        jax.ShapeDtypeStruct((rows, chunks, LANES), F32),
+        jax.ShapeDtypeStruct((rows, chunks, LANES), BF16),
         [SMEM] + [VMEM] * 4,
         "down",
-    )(routes_t, gu, gu_other, route, in_vmem(w_down))
+        scratch=(pltpu.VMEM((rows, chunks, LANES), F32),),
+    )(routes_t, gu, gu_other, stat, in_vmem(w_down))
     parts = exchange(full)
     return call(sum_kernel, jax.ShapeDtypeStruct((1, half), BF16), [VMEM] * 2, "total")(
         parts, own_h1

time: 47.9 us -> 46.4 us (0.969)
  waiting for transfers between devices: 2.39 us -> 1.46 us
    ppermute x1, waiting for transfers between devices: 1.19 us -> 0.26 us  [small_body(): gu_other = lax.ppermute(gu, 'heads', swap)]
    pallas_call x6 -> x7, Pallas kernels: 11 us -> 10.8 us  [call(): return lambda *ops: f(*ops, *more)]
  transfers between devices with their start and end apart: 2 -> 2, of which waited for: 2 -> 2; matrix products, arithmetic and copies ran while one was open for 0% -> 0% of each run, Pallas kernels for 0% -> 2%
where the time goes in v3:
time: 46.4 us; the launch traced here: 46.1 us
  blocking collectives  32.8 us (71%)
  Pallas kernels  10.8 us (23%)
  waiting for transfers between devices  1.46 us (3%)
  between operations  1 us (2%)
    all_to_all x3, blocking collectives, exchange(): return lax.all_to_all(x, 'units', split_axis=0, concat_axis=0, tiled=True)  32.8 us
    pallas_call x7, Pallas kernels, call(): return lambda *ops: f(*ops, *more)  10.8 us
    ppermute x1, waiting for transfers between devices, small_body(): proj_other = lax.ppermute(proj, 'heads', swap)  1.2 us
  transfers between devices with their start and end apart: 2, of which 2 were waited for; matrix products, arithmetic and copies ran while one was open for 0% of the time, Pallas kernels for 2%

profile of v3, /device:TPU:0, one launch (start us, length us, event | category | flops | bytes accessed | tf_op | source)
XLA Modules:
  0.0 46.1 jit_solution(17389417969958145489)
XLA Ops:
  0.0 0.0 slice-start
  0.0 0.0 slice-start.3
  0.8 0.0 copy-start
  0.8 0.0 copy-start.3
  0.8 0.0 slice-start.1
  0.8 0.0 slice-start.2
  0.8 0.0 slice-start.4
  0.9 0.0 slice-start.5
  0.9 0.0 copy-start.2
  0.9 0.0 copy-start.4
  0.9 2.2 %attend.1 = bf16[8,24,128]{2,1,0:T(8,128)(2,1)S(1)} custom-call(s32[1]{0:T(128)S(6)} %copy.16.refs_0_, s32[1,4]{1,0:T(1,128)} %refs_1_.2, bf16[1,3072]{1,0:T(2,128)(2,1)} %refs_2_.3, bf16[1,512]{1,0:T(2,128)(2,1)} %refs_3_.2, bf16[1,512]{1,0:T(2,128)(2,1)} %refs_4_.3, bf16[4,128,512]{2,1,0:T(8,128)(2,1)} %refs_5_.1, bf16[4,128,512]{2,1,0:T(8,128)(2,1)} %refs_6_.1, ...), custom_call_target="tpu_custom_call" | custom-call | tf_op jit(solution)/shard_map/attend/pallas_call | solution.py:356
  3.1 14.1 %all_to_all.15.refs_0_ = bf16[8,24,128]{2,1,0:T(8,128)(2,1)S(1)} all-to-all(bf16[8,24,128]{2,1,0:T(8,128)(2,1)S(1)} %attend.1), channel_id=1, replica_groups=mesh['groups'=2,'units'=8,'heads'=2] {'units'}, dimensions={0} | all-to-all | bytes 98304 | tf_op jit(solution)/shard_map/all_to_all | solution.py:338
  17.2 0.0 copy-done
  17.2 0.0 slice-start.6
  17.2 0.7 %proj.1.refs_1_ = f32[8,768]{1,0:T(8,128)S(1)} custom-call(bf16[8,24,128]{2,1,0:T(8,128)(2,1)S(1)} %all_to_all.15.refs_0_, bf16[3072,768]{1,0:T(8,128)(2,1)S(1)} %copy-done), custom_call_target="tpu_custom_call" | custom-call | tf_op jit(solution)/shard_map/proj/pallas_call | solution.py:356
  17.9 0.0 collective-permute-start
  17.9 1.2 %collective-permute-done.refs_2_ = f32[8,768]{1,0:T(8,128)S(1)} collective-permute-done((f32[8,768]{1,0:T(8,128)S(1)}, f32[8,768]{1,0:T(8,128)S(1)}, u32[]{:S(2)}, u32[]{:S(2)}) %collective-permute-start) | collective-permute-done | bytes 24608 | tf_op jit(solution)/shard_map/ppermute | solution.py:380
  19.1 0.0 copy-done.3
  19.1 9.5 %all_to_all.16.refs_1_ = bf16[8,8,768]{2,1,0:T(8,128)(2,1)S(1)} all-to-all(bf16[8,8,768]{2,1,0:T(8,128)(2,1)S(1)} %resid.1), channel_id=1, replica_groups=mesh['groups'=2,'units'=8,'heads'=2] {'units'}, dimensions={0} | all-to-all | bytes 196608 | tf_op jit(solution)/shard_map/all_to_all | solution.py:338
  28.6 0.0 slice-done
  28.6 0.0 slice-done.3
  28.6 0.0 slice-done.1
  28.6 0.0 slice-done.2
  28.7 0.0 slice-done.4
  28.7 0.0 slice-done.5
  28.7 0.0 copy-done.2
  28.7 0.0 copy-done.4
  28.7 0.0 copy-start.1
  28.7 0.0 slice-start.7
  28.7 0.0 slice-start.8
  28.8 3.9 %expert.1.refs_1_ = f32[2,4096]{1,0:T(2,128)S(1)} custom-call(s32[2,8]{1,0:T(2,128)S(1)} %bitcast.9, bf16[8,8,768]{2,1,0:T(8,128)(2,1)S(1)} %all_to_all.16.refs_1_, bf16[6144]{0:T(1024)(128)(2,1)S(1)} %copy-done.2, bf16[3072,2048]{1,0:T(8,128)(2,1)S(1)} %bitcast.3, bf16[3072,2048]{1,0:T(8,128)(2,1)S(1)} %bitcast.5), custom_call_target="tpu_custom_call" | custom-call | tf_op jit(solution)/shard_map/expert/pallas_call | solution.py:356
  32.7 0.0 collective-permute-start.1
  32.7 0.0 copy-done.1
  32.7 0.9 %side.1 = (f32[2,128]{1,0:T(2,128)S(1)}, f32[1,3072]{1,0:T(1,128)S(1)}) custom-call(s32[2,8]{1,0:T(2,128)S(1)} %bitcast.10, bf16[8,8,768]{2,1,0:T(8,128)(2,1)S(1)} %all_to_all.16.refs_1_, bf16[6144]{0:T(1024)(128)(2,1)S(1)} %copy-done.2, bf16[8,6144]{1,0:T(8,128)(2,1)S(1)} %bitcast.8), custom_call_target="tpu_custom_call" | custom-call | tf_op jit(solution)/shard_map/side/pallas_call | solution.py:356
  33.6 0.3 collective-permute-done.1.refs_2_
  33.9 0.0 slice-done.6
  33.9 0.0 slice-done.7
  33.9 0.0 slice-done.8
  33.9 2.4 %down.1 = bf16[8,24,128]{2,1,0:T(8,128)(2,1)S(1)} custom-call(s32[2,8]{1,0:T(2,128)S(1)} %bitcast.11, f32[2,4096]{1,0:T(2,128)S(1)} %expert.1.refs_1_, f32[2,4096]{1,0:T(2,128)S(1)} %collective-permute-done.1.refs_2_, f32[2,128]{1,0:T(2,128)S(1)} %get-tuple-element.7.refs_3_, bf16[2048,3072]{1,0:T(8,128)(2,1)S(1)} %bitcast.7), custom_call_target="tpu_custom_call" | custom-call | tf_op jit(solution)/shard_map/down/pallas_call | solution.py:356
  36.3 9.2 %all_to_all.17.refs_0_ = bf16[8,24,128]{2,1,0:T(8,128)(2,1)S(1)} all-to-all(bf16[8,24,128]{2,1,0:T(8,128)(2,1)S(1)} %down.1), channel_id=1, replica_groups=mesh['groups'=2,'units'=8,'heads'=2] {'units'}, dimensions={0} | all-to-all | bytes 98304 | tf_op jit(solution)/shard_map/all_to_all | solution.py:338
  45.5 0.6 %total.1 = bf16[1,3072]{1,0:T(2,128)(2,1)} custom-call(bf16[8,24,128]{2,1,0:T(8,128)(2,1)S(1)} %all_to_all.17.refs_0_, f32[1,3072]{1,0:T(1,128)S(1)} %get-tuple-element.8.refs_1_), custom_call_target="tpu_custom_call" | custom-call | tf_op jit(solution)/shard_map/total/pallas_call | solution.py:356
  (4 shorter events, 0.0 us)
Async XLA Ops:
  0.0 28.6 %slice-start = ((s8[12582912]{0:T(1024)(128)(4,1)}), s8[4194304]{0:T(1024)(128)(4,1)S(1)}, s32[]{:S(2)}) async-start(s8[12582912]{0:T(1024)(128)(4,1)} %bitcast.2), calls=%async_computation.3 | async-start | bytes 8388608
  0.0 28.6 %slice-start.3 = ((s8[12582912]{0:T(1024)(128)(4,1)}), s8[4194304]{0:T(1024)(128)(4,1)S(1)}, s32[]{:S(2)}) async-start(s8[12582912]{0:T(1024)(128)(4,1)} %bitcast.4), calls=%async_computation.6 | async-start | bytes 8388608
  0.8 16.4 %copy-start = (bf16[3072,768]{1,0:T(8,128)(2,1)S(1)}, bf16[3072,768]{1,0:T(8,128)(2,1)}, u32[]{:S(2)}) copy-start(bf16[3072,768]{1,0:T(8,128)(2,1)} %refs_1_.3) | copy-start | bytes 14155780
  0.8 18.3 %copy-start.3 = (bf16[8,768]{1,0:T(8,128)(2,1)S(1)}, bf16[8,768]{1,0:T(8,128)(2,1)}, u32[]{:S(2)}) copy-start(bf16[8,768]{1,0:T(8,128)(2,1)} %refs_0_.2) | copy-start | bytes 36868
  0.8 27.8 %slice-start.1 = ((s8[12582912]{0:T(1024)(128)(4,1)}), s8[4194304]{0:T(1024)(128)(4,1)S(1)}, s32[]{:S(2)}) async-start(s8[12582912]{0:T(1024)(128)(4,1)} %bitcast.2), calls=%async_computation.4 | async-start | bytes 8388608
  0.8 27.8 %slice-start.2 = ((s8[12582912]{0:T(1024)(128)(4,1)}), s8[4194304]{0:T(1024)(128)(4,1)S(1)}, s32[]{:S(2)}) async-start(s8[12582912]{0:T(1024)(128)(4,1)} %bitcast.2), calls=%async_computation.5 | async-start | bytes 8388608
  0.8 27.8 %slice-start.4 = ((s8[12582912]{0:T(1024)(128)(4,1)}), s8[4194304]{0:T(1024)(128)(4,1)S(1)}, s32[]{:S(2)}) async-start(s8[12582912]{0:T(1024)(128)(4,1)} %bitcast.4), calls=%async_computation.7 | async-start | bytes 8388608
  0.9 27.8 %slice-start.5 = ((s8[12582912]{0:T(1024)(128)(4,1)}), s8[4194304]{0:T(1024)(128)(4,1)S(1)}, s32[]{:S(2)}) async-start(s8[12582912]{0:T(1024)(128)(4,1)} %bitcast.4), calls=%async_computation.8 | async-start | bytes 8388608
  0.9 27.8 %copy-start.2 = (bf16[6144]{0:T(1024)(128)(2,1)S(1)}, bf16[6144]{0:T(1024)(128)(2,1)}, u32[]{:S(2)}) copy-start(bf16[6144]{0:T(1024)(128)(2,1)} %refs_2_.5) | copy-start | bytes 36868
  0.9 27.8 %copy-start.4 = (s32[8,2]{0,1:T(2,128)S(1)}, s32[8,2]{0,1:T(2,128)}, u32[]{:S(2)}) copy-start(s32[8,2]{0,1:T(2,128)} %param.26) | copy-start | bytes 196
  17.2 16.7 %slice-start.6 = ((s8[12582912]{0:T(1024)(128)(4,1)}), s8[4194304]{0:T(1024)(128)(4,1)S(1)}, s32[]{:S(2)}) async-start(s8[12582912]{0:T(1024)(128)(4,1)} %bitcast.6), calls=%async_computation.9 | async-start | bytes 8388608
  17.9 1.2 %collective-permute-start = (f32[8,768]{1,0:T(8,128)S(1)}, f32[8,768]{1,0:T(8,128)S(1)}, u32[]{:S(2)}, u32[]{:S(2)}) collective-permute-start(f32[8,768]{1,0:T(8,128)S(1)} %proj.1.refs_1_), channel_id=1, source_target_pairs={{0,1},{1,0},{2,3},{3,2},{4,5},{5,4},{6,7},{7,6},{8,9},{9,8},{10,11... | collective-permute-start | bytes 73736 | tf_op jit(solution)/shard_map/ppermute | solution.py:380
  28.7 4.0 %copy-start.1 = (bf16[6144,8]{0,1:T(8,128)(2,1)S(1)}, bf16[6144,8]{0,1:T(8,128)(2,1)}, u32[]{:S(2)}) copy-start(bf16[6144,8]{0,1:T(8,128)(2,1)} %param.25) | copy-start | bytes 294916
  28.7 5.2 %slice-start.7 = ((s8[12582912]{0:T(1024)(128)(4,1)}), s8[4194304]{0:T(1024)(128)(4,1)S(1)}, s32[]{:S(2)}) async-start(s8[12582912]{0:T(1024)(128)(4,1)} %bitcast.6), calls=%async_computation.10 | async-start | bytes 8388608
  28.7 5.2 %slice-start.8 = ((s8[12582912]{0:T(1024)(128)(4,1)}), s8[4194304]{0:T(1024)(128)(4,1)S(1)}, s32[]{:S(2)}) async-start(s8[12582912]{0:T(1024)(128)(4,1)} %bitcast.6), calls=%async_computation.11 | async-start | bytes 8388608
  32.7 1.2 %collective-permute-start.1 = (f32[2,4096]{1,0:T(2,128)S(1)}, f32[2,4096]{1,0:T(2,128)S(1)}, u32[]{:S(2)}, u32[]{:S(2)}) collective-permute-start(f32[2,4096]{1,0:T(2,128)S(1)} %expert.1.refs_1_), channel_id=1, source_target_pairs={{0,1},{1,0},{2,3},{3,2},{4,5},{5,4},{6,7},{7,6},{8,9},{9,8},{10,11... | collective-permute-start | bytes 98312 | tf_op jit(solution)/shard_map/ppermute | solution.py:392

commit v4 on v3

--- a/solution.py
+++ b/solution.py
@@ -126,35 +126,29 @@
     return (own_h1.astype(jnp.float32) + moe_own).astype(jnp.bfloat16)
 
 
-def attn_kernel(
-    len_ref, table_hbm, q_hbm, fk_hbm, fv_hbm, k_hbm, v_hbm, o_ref,
-    table_ref, q_ref, fk_ref, fv_ref, k_ref, v_ref, sems,
-):
-    pairs = {
-        "q": (q_hbm, q_ref),
-        "fk": (fk_hbm, fk_ref),
-        "table": (table_hbm, table_ref),
-        "k": (k_hbm, k_ref),
-        "v": (v_hbm, v_ref),
-        "fv": (fv_hbm, fv_ref),
-    }
-    copies = {
-        name: pltpu.make_async_copy(src, dst, sems.at[i]) for i, (name, (src, dst)) in enumerate(pairs.items())
-    }
-    for copy in copies.values():
-        copy.start()
+def begin_kernel(o_ref):
+    o_ref[...] = jnp.zeros(o_ref.shape, F32)
+
+
+def attn_kernel(begun_ref, len_ref, table_ref, q_ref, fk_ref, fv_ref, k_ref, v_ref, o_ref):
     pages, page_tokens, kv_width = k_ref.shape
     heads_kv = kv_width // HEAD_WIDTH
     group = q_ref.shape[1] // kv_width
     rows = -(-group // 8) * 8
-    span = pages * page_tokens
     scale = HEAD_WIDTH ** (-0.5)
     length = len_ref[0]
     pad = [jnp.zeros((rows - group, HEAD_WIDTH), F32)] if rows > group else []
-    live = lax.broadcasted_iota(jnp.int32, (rows, span), 1) < length
+    table = table_ref[...]
+    slots = lax.broadcasted_iota(jnp.int32, table.shape, 1)
+    tokens = lax.broadcasted_iota(jnp.int32, (rows, page_tokens), 1)
+    live = jnp.concatenate(
+        [
+            tokens + page_tokens * jnp.sum(jnp.where(table == page, slots, 0), axis=1, keepdims=True) < length
+            for page in range(pages)
+        ],
+        axis=1,
+    )
     heads = [slice(g * HEAD_WIDTH, (g + 1) * HEAD_WIDTH) for g in range(heads_kv)]
-    copies["q"].wait()
-    copies["fk"].wait()
     q = q_ref[...].astype(F32)
     fk = fk_ref[...].astype(F32)
     q_grid = [
@@ -168,13 +162,10 @@
         jnp.sum(q_g * fk[:, lanes], axis=1, keepdims=True) * scale for q_g, lanes in zip(q_grid, heads)
     ]
     q_grid = [q_g.astype(BF16) for q_g in q_grid]
-    copies["table"].wait()
-    copies["k"].wait()
-    table = [table_ref[0, p] for p in range(pages)]
     scores = [
         lax.dot_general(
             q_g,
-            jnp.concatenate([k_ref[page, :, lanes] for page in table], axis=0),
+            jnp.concatenate([k_ref[page, :, lanes] for page in range(pages)], axis=0),
             (((1,), (1,)), ((), ())),
             preferred_element_type=F32,
         )
@@ -189,14 +180,12 @@
         total = jnp.sum(prob, axis=1, keepdims=True) + own_p
         weights.append((prob / total).astype(BF16))
         own_weights.append((own_p / total).astype(BF16).astype(F32))
-    copies["v"].wait()
-    copies["fv"].wait()
     fv = fv_ref[...].astype(F32)
     blended = [
         (
             jnp.dot(
                 w,
-                jnp.concatenate([v_ref[page, :, lanes] for page in table], axis=0),
+                jnp.concatenate([v_ref[page, :, lanes] for page in range(pages)], axis=0),
                 preferred_element_type=F32,
             )
             + own_w * fv[:, lanes]
@@ -208,16 +197,28 @@
         o_ref[r] = attn
 
 
-def proj_kernel(attn_ref, w_ref, o_ref):
+def proj_kernel(attn_ref, w_ref, routes_ref, o_ref, slot_ref):
     attn = attn_ref[...].astype(F32)
     x = jnp.concatenate([attn[:, j, :] for j in range(attn.shape[1])], axis=1).astype(BF16)
     o_ref[...] = jnp.dot(x, w_ref[...], preferred_element_type=F32)
-
-
-def resid_kernel(resid_ref, mine_ref, other_ref, o_ref):
-    h1 = (resid_ref[...].astype(F32) + (mine_ref[...] + other_ref[...])).astype(BF16)
+    hit = jnp.logical_or(routes_ref[0:1, :] == 0, routes_ref[1:2, :] == 0)
+    ids = lax.broadcasted_iota(jnp.int32, hit.shape, 1)
+    first = jnp.min(jnp.where(hit, ids, hit.shape[1]), axis=1, keepdims=True)
+    last = jnp.max(jnp.where(hit, ids, -1), axis=1, keepdims=True)
+    request = lax.broadcasted_iota(jnp.int32, slot_ref.shape, 0)
+    lane = lax.broadcasted_iota(jnp.int32, slot_ref.shape, 1)
+    chosen = jnp.where(lane == 0, first, jnp.where(lane == 1, last, -1))
+    slot_ref[...] = jnp.where(request == chosen, 1.0, 0.0)
+
+
+def resid_kernel(resid_ref, mine_ref, other_ref, slot_ref, o_ref):
+    h1 = (resid_ref[...].astype(F32) + (mine_ref[...] + other_ref[...])).astype(BF16).astype(F32)
+    routed = [
+        jnp.sum(jnp.where(slot_ref[:, s : s + 1] > 0.0, h1, 0.0), axis=0, keepdims=True) for s in range(2)
+    ]
     for r in range(o_ref.shape[0]):
-        o_ref[r] = h1
+        own = h1[r : r + 1]
+        o_ref[r] = jnp.concatenate(routed + [own, own], axis=0).astype(BF16)
 
 
 def routed_rows(routes_ref):
@@ -231,7 +232,7 @@
     return first, last
 
 
-def expert_kernel(routes_ref, h1_ref, gain_ref, wg_ref, wu_ref, gu_ref, gu_all):
+def expert_kernel(h1_ref, gain_ref, wg_ref, wu_ref, gu_ref):
     units, _, cols = h1_ref.shape
     hidden = wg_ref.shape[1]
     per_half = units // 2
@@ -239,40 +240,36 @@
     half = per_half * cols
     gain = gain_ref[...].astype(F32).reshape(1, -1)
     gain = jnp.where(head == 0, gain[:, :half], gain[:, half:])
-    h1 = jnp.concatenate([h1_ref[head * per_half + i] for i in range(per_half)], axis=1).astype(F32)
+    h1 = jnp.concatenate([h1_ref[head * per_half + i].astype(F32)[:2] for i in range(per_half)], axis=1)
     x = (h1 * gain).astype(BF16)
-    gu_all[:, :hidden] = jnp.dot(x, wg_ref[...], preferred_element_type=F32)
-    gu_all[:, hidden:] = jnp.dot(x, wu_ref[...], preferred_element_type=F32)
-    for slot, r in enumerate(routed_rows(routes_ref)):
-        gu_ref[slot : slot + 1, :] = gu_all[pl.ds(r, 1), :]
-
-
-def side_kernel(routes_ref, h1_ref, gain_ref, router_ref, stat_ref, own_ref, h_all, router_all):
+    gu_ref[:, :hidden] = jnp.dot(x, wg_ref[...], preferred_element_type=F32)
+    gu_ref[:, hidden:] = jnp.dot(x, wu_ref[...], preferred_element_type=F32)
+
+
+def side_kernel(routes_ref, h1_ref, gain_ref, router_ref, stat_ref, own_ref, router_all):
     units, _, cols = h1_ref.shape
     per_half = units // 2
     head = lax.axis_index("heads")
-    unit = lax.axis_index("units")
-    for u in range(units):
-        h_all[:, u * cols : (u + 1) * cols] = h1_ref[u].astype(F32)
-    own = h_all[pl.ds(unit, 1), :]
-    half = per_half * cols
-    own_ref[...] = jnp.where(head == 0, own[:, :half], own[:, half:])
+    for i in range(per_half):
+        own_ref[:, i * cols : (i + 1) * cols] = h1_ref[head * per_half + i].astype(F32)[2:3]
     router_all[...] = router_ref[...].astype(F32)
     gain = gain_ref[...].astype(F32).reshape(1, -1)
-    for slot, r in enumerate(routed_rows(routes_ref)):
-        h = h_all[pl.ds(r, 1), :]
-        rstd = lax.rsqrt(jnp.mean(h * h, axis=1, keepdims=True) + 1e-05)
-        xn = (h * rstd * gain).astype(BF16).astype(F32)
-        other = jnp.where(routes_ref[0, r] == 0, routes_ref[1, r], routes_ref[0, r])
-        diff = jnp.sum(xn * router_all[0:1, :], axis=1, keepdims=True) - jnp.sum(
-            xn * router_all[pl.ds(other, 1), :], axis=1, keepdims=True
-        )
-        route = 1.0 / (1.0 + jnp.exp(-diff))
-        lane_ids = lax.broadcasted_iota(jnp.int32, (1, LANES), 1)
-        stat_ref[slot : slot + 1, :] = jnp.where(lane_ids == 0, rstd, route)
-
-
-def down_kernel(routes_ref, mine_ref, other_ref, stat_ref, wd_ref, o16_ref, o_ref):
+    h = jnp.concatenate([h1_ref[u].astype(F32)[:2] for u in range(units)], axis=1)
+    rstd = lax.rsqrt(jnp.mean(h * h, axis=1, keepdims=True) + 1e-05)
+    xn = (h * rstd * gain).astype(BF16).astype(F32)
+    other = []
+    for r in routed_rows(routes_ref):
+        other.append(jnp.where(routes_ref[0, r] == 0, routes_ref[1, r], routes_ref[0, r]))
+    first = jnp.sum(xn * router_all[0:1, :], axis=1, keepdims=True)
+    second = jnp.sum(
+        xn * jnp.concatenate([router_all[pl.ds(e, 1), :] for e in other], axis=0), axis=1, keepdims=True
+    )
+    route = 1.0 / (1.0 + jnp.exp(second - first))
+    lane_ids = lax.broadcasted_iota(jnp.int32, stat_ref.shape, 1)
+    stat_ref[...] = jnp.where(lane_ids == 0, rstd, route)
+
+
+def down_kernel(mine_ref, other_ref, stat_ref, slot_ref, wd_ref, o_ref, full_ref):
     hidden = wd_ref.shape[0]
     rstd = stat_ref[:, 0:1]
     route = stat_ref[:, 1:2]
@@ -280,11 +277,12 @@
     up = (mine_ref[:, hidden:] + other_ref[:, hidden:]) * (rstd * route)
     act = (gate / (1.0 + jnp.exp(-gate)) * up).astype(BF16)
     full = jnp.dot(act, wd_ref[...], preferred_element_type=F32)
-    o_ref[...] = jnp.zeros(o_ref.shape, F32)
-    for slot, r in enumerate(routed_rows(routes_ref)):
-        for j in range(o_ref.shape[1]):
-            o_ref[r, j : j + 1, :] = full[slot : slot + 1, j * LANES : (j + 1) * LANES]
-    o16_ref[...] = o_ref[...].astype(BF16)
+    for j in range(o_ref.shape[1]):
+        for s in range(2):
+            full_ref[s, j : j + 1, :] = full[s : s + 1, j * LANES : (j + 1) * LANES]
+    for r in range(o_ref.shape[0]):
+        block = jnp.where(slot_ref[r : r + 1, 1:2] > 0.0, full_ref[1], 0.0)
+        o_ref[r] = jnp.where(slot_ref[r : r + 1, 0:1] > 0.0, full_ref[0], block).astype(BF16)
 
 
 def sum_kernel(parts_ref, own_ref, o_ref):
@@ -355,55 +353,48 @@
         )
         return lambda *ops: f(*ops, *more)
 
+    begun = call(
+        begin_kernel, jax.ShapeDtypeStruct((8, LANES), F32), [], "begin", more=(w_gate,)
+    )()
     attn = call(
         attn_kernel,
         jax.ShapeDtypeStruct((rows, chunks, LANES), BF16),
-        [SMEM] + [ANY] * 6,
+        [VMEM, SMEM] + [VMEM] * 6,
         "attend",
-        scratch=(
-            pltpu.SMEM(page_table.shape, page_table.dtype),
-            *(
-                pltpu.VMEM(x.shape, x.dtype)
-                for x in (queries, fresh_key, fresh_value, key_cache_pages, value_cache_pages)
-            ),
-            pltpu.SemaphoreType.DMA((6,)),
-        ),
         more=(w_gate, w_up, w_down),
     )(
-        lengths,
-        *map(in_hbm, (page_table, queries, fresh_key, fresh_value, key_cache_pages, value_cache_pages)),
+        begun, lengths, *map(in_vmem, (page_table, queries, fresh_key, fresh_value, key_cache_pages, value_cache_pages)),
     )
     attn_all = exchange(attn)
-    proj = call(proj_kernel, jax.ShapeDtypeStruct((rows, cols), F32), [VMEM] * 2, "proj")(
-        attn_all, in_vmem(w_out)
-    )
+    proj, slots = call(
+        proj_kernel,
+        (jax.ShapeDtypeStruct((rows, cols), F32), jax.ShapeDtypeStruct((rows, LANES), F32)),
+        [VMEM] * 3,
+        "proj",
+    )(attn_all, in_vmem(w_out), routes_t)
     proj_other = lax.ppermute(proj, "heads", swap)
-    h1_cols = call(
-        resid_kernel, jax.ShapeDtypeStruct((rows, rows, cols), BF16), [VMEM] * 3, "resid"
-    )(resid, proj, proj_other)
+    h1_cols = call(resid_kernel, jax.ShapeDtypeStruct((rows, 4, cols), BF16), [VMEM] * 4, "resid")(
+        resid, proj, proj_other, slots
+    )
     h1 = exchange(h1_cols)
-    gu = call(
-        expert_kernel,
-        jax.ShapeDtypeStruct((2, 2 * hidden), F32),
-        [SMEM] + [VMEM] * 4,
-        "expert",
-        scratch=(pltpu.VMEM((rows, 2 * hidden), F32),),
-    )(routes_t, h1, norm_gain, in_vmem(w_gate), in_vmem(w_up))
+    gu = call(expert_kernel, jax.ShapeDtypeStruct((2, 2 * hidden), F32), [VMEM] * 4, "expert")(
+        h1, norm_gain, in_vmem(w_gate), in_vmem(w_up)
+    )
     gu_other = lax.ppermute(gu, "heads", swap)
     stat, own_h1 = call(
         side_kernel,
         (jax.ShapeDtypeStruct((2, LANES), F32), jax.ShapeDtypeStruct((1, half), F32)),
         [SMEM] + [VMEM] * 3,
         "side",
-        scratch=(pltpu.VMEM((rows, 2 * half), F32), pltpu.VMEM(router.shape[::-1], F32)),
+        scratch=(pltpu.VMEM(router.shape[::-1], F32),),
     )(routes_t, h1, norm_gain, router.T)
     full = call(
         down_kernel,
         jax.ShapeDtypeStruct((rows, chunks, LANES), BF16),
-        [SMEM] + [VMEM] * 4,
+        [VMEM] * 5,
         "down",
-        scratch=(pltpu.VMEM((rows, chunks, LANES), F32),),
-    )(routes_t, gu, gu_other, stat, in_vmem(w_down))
+        scratch=(pltpu.VMEM((2, chunks, LANES), F32),),
+    )(gu, gu_other, stat, slots, in_vmem(w_down))
     parts = exchange(full)
     return call(sum_kernel, jax.ShapeDtypeStruct((1, half), BF16), [VMEM] * 2, "total")(
         parts, own_h1

time: 46.4 us -> 43.8 us (0.944)
  Pallas kernels: 10.8 us -> 8.05 us
    pallas_call x7 -> x8, Pallas kernels: 10.8 us -> 8.05 us  [call(): return lambda *ops: f(*ops, *more)]
where the time goes in v4:
time: 43.8 us; the launch traced here: 43.6 us
  blocking collectives  32.5 us (74%)
  Pallas kernels  8.05 us (18%)
  waiting for transfers between devices  1.57 us (4%)
  between operations  0.98 us (2%)
  local copies, waits for them, and re-layouts  0.53 us (1%)
    all_to_all x3, blocking collectives, exchange(): return lax.all_to_all(x, 'units', split_axis=0, concat_axis=0, tiled=True)  32.5 us
    pallas_call x8, Pallas kernels, call(): return lambda *ops: f(*ops, *more)  8.05 us
    ppermute x1, waiting for transfers between devices, small_body(): proj_other = lax.ppermute(proj, 'heads', swap)  1.2 us
  transfers between devices with their start and end apart: 2, of which 2 were waited for; matrix products, arithmetic and copies ran while one was open for 0% of the time, Pallas kernels for 2%

profile of v4, /device:TPU:0, one launch (start us, length us, event | category | flops | bytes accessed | tf_op | source)
XLA Modules:
  0.0 43.6 jit_solution(9135144976623012395)
XLA Ops:
  0.0 0.0 copy-start.4
  0.8 0.0 slice-start.9
  0.8 0.0 slice-start
  0.8 0.0 slice-start.6
  0.8 0.0 copy-done.9
  0.8 0.3 copy-done.1
  1.1 0.2 copy-done
  1.2 0.0 copy-done.8
  1.2 0.0 copy-done.7
  1.2 0.0 copy-done.4
  1.2 0.0 copy-start.6
  1.3 0.0 copy-start.5
  1.3 0.0 slice-start.1
  1.3 0.0 slice-start.2
  1.3 0.0 slice-start.7
  1.3 0.0 slice-start.8
  1.3 0.0 copy-start.3
  1.3 0.5 %attend.1 = bf16[8,24,128]{2,1,0:T(8,128)(2,1)S(1)} custom-call(f32[8,128]{1,0:T(8,128)S(1)} %begin.1.refs_0_, s32[1]{0:T(128)S(6)} %copy.16.refs_1_, s32[1,4]{1,0:T(1,128)S(1)} %copy-done.9, bf16[1,3072]{1,0:T(2,128)(2,1)S(1)} %copy-done.4, bf16[1,512]{1,0:T(2,128)(2,1)S(1)} %copy-done.7, bf16[1,512]{1,0:T(2,128)(2,1)S(1)} %copy-done.8, ...), custom_call_target="tpu_custom_call" | custom-call | tf_op jit(solution)/shard_map/attend/pallas_call | solution.py:354
  1.9 14.1 %all_to_all.15.refs_0_ = bf16[8,24,128]{2,1,0:T(8,128)(2,1)S(1)} all-to-all(bf16[8,24,128]{2,1,0:T(8,128)(2,1)S(1)} %attend.1), channel_id=1, replica_groups=mesh['groups'=2,'units'=8,'heads'=2] {'units'}, dimensions={0} | all-to-all | bytes 98304 | tf_op jit(solution)/shard_map/all_to_all | solution.py:336
  16.0 0.0 slice-done.9
  16.0 0.0 slice-done.10
  16.0 0.0 copy-done.6
  16.0 0.0 slice-start.3
  16.0 0.7 %proj.1 = (f32[8,768]{1,0:T(8,128)S(1)}, f32[8,128]{1,0:T(8,128)S(1)}) custom-call(bf16[8,24,128]{2,1,0:T(8,128)(2,1)S(1)} %all_to_all.15.refs_0_, bf16[3072,768]{1,0:T(8,128)(2,1)S(1)} %bitcast.9, s32[2,8]{1,0:T(2,128)S(1)} %bitcast.11), custom_call_target="tpu_custom_call" | custom-call | tf_op jit(solution)/shard_map/proj/pallas_call | solution.py:354
  16.7 0.0 collective-permute-start
  16.7 1.2 %collective-permute-done.refs_2_ = f32[8,768]{1,0:T(8,128)S(1)} collective-permute-done((f32[8,768]{1,0:T(8,128)S(1)}, f32[8,768]{1,0:T(8,128)S(1)}, u32[]{:S(2)}, u32[]{:S(2)}) %collective-permute-start) | collective-permute-done | bytes 24608 | tf_op jit(solution)/shard_map/ppermute | solution.py:375
  17.9 0.0 copy-done.5
  17.9 0.1 resid.1
  18.1 9.2 %all_to_all.16.refs_0_.refs_1_ = bf16[8,4,768]{2,1,0:T(4,128)(2,1)S(1)} all-to-all(bf16[8,4,768]{2,1,0:T(4,128)(2,1)S(1)} %resid.1), channel_id=1, replica_groups=mesh['groups'=2,'units'=8,'heads'=2] {'units'}, dimensions={0} | all-to-all | bytes 98304 | tf_op jit(solution)/shard_map/all_to_all | solution.py:336
  27.2 0.0 slice-done
  27.2 0.0 slice-done.6
  27.2 0.0 slice-done.1
  27.2 0.0 slice-done.2
  27.3 0.0 slice-done.7
  27.3 0.0 slice-done.8
  27.3 0.0 copy-done.3
  27.3 0.0 copy-start.2
  27.3 0.0 slice-start.4
  27.3 0.0 slice-start.5
  27.3 3.4 %expert.1.refs_0_ = f32[2,4096]{1,0:T(2,128)S(1)} custom-call(bf16[8,4,768]{2,1,0:T(4,128)(2,1)S(1)} %all_to_all.16.refs_0_.refs_1_, bf16[6144]{0:T(1024)(128)(2,1)S(1)} %copy-done.3, bf16[3072,2048]{1,0:T(8,128)(2,1)S(1)} %bitcast.3, bf16[3072,2048]{1,0:T(8,128)(2,1)S(1)} %bitcast.7), custom_call_target="tpu_custom_call" | custom-call | tf_op jit(solution)/shard_map/expert/pallas_call | solution.py:354
  30.7 0.0 collective-permute-start.1
  30.7 0.0 copy-done.2
  30.7 0.8 %side.1 = (f32[2,128]{1,0:T(2,128)S(1)}, f32[1,3072]{1,0:T(1,128)S(1)}) custom-call(s32[2,8]{1,0:T(2,128)S(1)} %bitcast.12, bf16[8,4,768]{2,1,0:T(4,128)(2,1)S(1)} %all_to_all.16.refs_0_.refs_1_, bf16[6144]{0:T(1024)(128)(2,1)S(1)} %copy-done.3, bf16[8,6144]{1,0:T(8,128)(2,1)S(1)} %bitcast.10), custom_call_target="tpu_custom_call" | custom-call | tf_op jit(solution)/shard_map/side/pallas_call | solution.py:354
  31.5 0.4 collective-permute-done.1.refs_1_
  31.9 0.0 slice-done.3
  31.9 1.9 %down.1 = bf16[8,24,128]{2,1,0:T(8,128)(2,1)S(1)} custom-call(f32[2,4096]{1,0:T(2,128)S(1)} %expert.1.refs_0_, f32[2,4096]{1,0:T(2,128)S(1)} %collective-permute-done.1.refs_1_, f32[2,128]{1,0:T(2,128)S(1)} %get-tuple-element.11.refs_2_, f32[8,128]{1,0:T(8,128)S(1)} %get-tuple-element.10.refs_3_, bf16[2048,3072]{1,0:T(8,128)(2,1)S(1)} %bitcast.5), custom_call_target="tpu_custom_call" | custom-call | tf_op jit(solution)/shard_map/down/pallas_call | solution.py:354
  33.8 9.2 %all_to_all.17.refs_0_ = bf16[8,24,128]{2,1,0:T(8,128)(2,1)S(1)} all-to-all(bf16[8,24,128]{2,1,0:T(8,128)(2,1)S(1)} %down.1), channel_id=1, replica_groups=mesh['groups'=2,'units'=8,'heads'=2] {'units'}, dimensions={0} | all-to-all | bytes 98304 | tf_op jit(solution)/shard_map/all_to_all | solution.py:336
  43.0 0.6 %total.1 = bf16[1,3072]{1,0:T(2,128)(2,1)} custom-call(bf16[8,24,128]{2,1,0:T(8,128)(2,1)S(1)} %all_to_all.17.refs_0_, f32[1,3072]{1,0:T(1,128)S(1)} %get-tuple-element.12.refs_1_), custom_call_target="tpu_custom_call" | custom-call | tf_op jit(solution)/shard_map/total/pallas_call | solution.py:354
  (13 shorter events, 0.0 us)
Async XLA Ops:
  0.0 0.8 %copy-start.9 = (s32[1,4]{1,0:T(1,128)S(1)}, s32[1,4]{1,0:T(1,128)}, u32[]{:S(2)}) copy-start(s32[1,4]{1,0:T(1,128)} %refs_2_.3) | copy-start | bytes 52
  0.0 1.1 %copy-start.1 = (bf16[4,128,512]{2,1,0:T(8,128)(2,1)S(1)}, bf16[4,128,512]{2,1,0:T(8,128)(2,1)}, u32[]{:S(2)}) copy-start(bf16[4,128,512]{2,1,0:T(8,128)(2,1)} %refs_7_.1) | copy-start | bytes 1572868
  0.0 1.2 %copy-start = (bf16[4,128,512]{2,1,0:T(8,128)(2,1)S(1)}, bf16[4,128,512]{2,1,0:T(8,128)(2,1)}, u32[]{:S(2)}) copy-start(bf16[4,128,512]{2,1,0:T(8,128)(2,1)} %refs_6_.1) | copy-start | bytes 1572868
  0.0 1.2 %copy-start.8 = (bf16[1,512]{1,0:T(2,128)(2,1)S(1)}, bf16[1,512]{1,0:T(2,128)(2,1)}, u32[]{:S(2)}) copy-start(bf16[1,512]{1,0:T(2,128)(2,1)} %refs_5_.1) | copy-start | bytes 3076
  0.0 1.2 %copy-start.7 = (bf16[1,512]{1,0:T(2,128)(2,1)S(1)}, bf16[1,512]{1,0:T(2,128)(2,1)}, u32[]{:S(2)}) copy-start(bf16[1,512]{1,0:T(2,128)(2,1)} %refs_4_.2) | copy-start | bytes 3076
  0.0 1.2 %copy-start.4 = (bf16[1,3072]{1,0:T(2,128)(2,1)S(1)}, bf16[1,3072]{1,0:T(2,128)(2,1)}, u32[]{:S(2)}) copy-start(bf16[1,3072]{1,0:T(2,128)(2,1)} %refs_3_.2) | copy-start | bytes 18436
  0.8 15.2 %slice-start.9 = ((s8[4718592]{0:T(1024)(128)(4,1)}), s8[4194304]{0:T(1024)(128)(4,1)S(1)}, s32[]{:S(2)}) async-start(s8[4718592]{0:T(1024)(128)(4,1)} %bitcast.8), calls=%async_computation.12 | async-start | bytes 8388608
  0.8 26.5 %slice-start = ((s8[12582912]{0:T(1024)(128)(4,1)}), s8[4194304]{0:T(1024)(128)(4,1)S(1)}, s32[]{:S(2)}) async-start(s8[12582912]{0:T(1024)(128)(4,1)} %bitcast.2), calls=%async_computation.3 | async-start | bytes 8388608
  0.8 26.5 %slice-start.6 = ((s8[12582912]{0:T(1024)(128)(4,1)}), s8[4194304]{0:T(1024)(128)(4,1)S(1)}, s32[]{:S(2)}) async-start(s8[12582912]{0:T(1024)(128)(4,1)} %bitcast.6), calls=%async_computation.9 | async-start | bytes 8388608
  1.2 14.7 %slice-start.10 = ((s8[4718592]{0:T(1024)(128)(4,1)}), s8[524288]{0:T(1024)(128)(4,1)S(1)}, s32[]{:S(2)}) async-start(s8[4718592]{0:T(1024)(128)(4,1)} %bitcast.8), calls=%async_computation.13 | async-start | bytes 1048576
  1.2 14.7 %copy-start.6 = (s32[8,2]{0,1:T(2,128)S(1)}, s32[8,2]{0,1:T(2,128)}, u32[]{:S(2)}) copy-start(s32[8,2]{0,1:T(2,128)} %param.26) | copy-start | bytes 196
  1.3 16.7 %copy-start.5 = (bf16[8,768]{1,0:T(8,128)(2,1)S(1)}, bf16[8,768]{1,0:T(8,128)(2,1)}, u32[]{:S(2)}) copy-start(bf16[8,768]{1,0:T(8,128)(2,1)} %refs_0_.3) | copy-start | bytes 36868
  1.3 26.0 %slice-start.1 = ((s8[12582912]{0:T(1024)(128)(4,1)}), s8[4194304]{0:T(1024)(128)(4,1)S(1)}, s32[]{:S(2)}) async-start(s8[12582912]{0:T(1024)(128)(4,1)} %bitcast.2), calls=%async_computation.4 | async-start | bytes 8388608
  1.3 26.0 %slice-start.2 = ((s8[12582912]{0:T(1024)(128)(4,1)}), s8[4194304]{0:T(1024)(128)(4,1)S(1)}, s32[]{:S(2)}) async-start(s8[12582912]{0:T(1024)(128)(4,1)} %bitcast.2), calls=%async_computation.5 | async-start | bytes 8388608
  1.3 26.0 %slice-start.7 = ((s8[12582912]{0:T(1024)(128)(4,1)}), s8[4194304]{0:T(1024)(128)(4,1)S(1)}, s32[]{:S(2)}) async-start(s8[12582912]{0:T(1024)(128)(4,1)} %bitcast.6), calls=%async_computation.10 | async-start | bytes 8388608
  1.3 26.0 %slice-start.8 = ((s8[12582912]{0:T(1024)(128)(4,1)}), s8[4194304]{0:T(1024)(128)(4,1)S(1)}, s32[]{:S(2)}) async-start(s8[12582912]{0:T(1024)(128)(4,1)} %bitcast.6), calls=%async_computation.11 | async-start | bytes 8388608
  1.3 26.0 %copy-start.3 = (bf16[6144]{0:T(1024)(128)(2,1)S(1)}, bf16[6144]{0:T(1024)(128)(2,1)}, u32[]{:S(2)}) copy-start(bf16[6144]{0:T(1024)(128)(2,1)} %refs_2_.5) | copy-start | bytes 36868
  16.0 15.9 %slice-start.3 = ((s8[12582912]{0:T(1024)(128)(4,1)}), s8[4194304]{0:T(1024)(128)(4,1)S(1)}, s32[]{:S(2)}) async-start(s8[12582912]{0:T(1024)(128)(4,1)} %bitcast.4), calls=%async_computation.6 | async-start | bytes 8388608
  16.7 1.2 %collective-permute-start = (f32[8,768]{1,0:T(8,128)S(1)}, f32[8,768]{1,0:T(8,128)S(1)}, u32[]{:S(2)}, u32[]{:S(2)}) collective-permute-start(f32[8,768]{1,0:T(8,128)S(1)} %get-tuple-element.9.refs_1_), channel_id=1, source_target_pairs={{0,1},{1,0},{2,3},{3,2},{4,5},{5,4},{6,7},{7,6},{8,9},{9,8},{10,11... | collective-permute-start | bytes 73736 | tf_op jit(solution)/shard_map/ppermute | solution.py:375
  27.3 3.4 %copy-start.2 = (bf16[6144,8]{0,1:T(8,128)(2,1)S(1)}, bf16[6144,8]{0,1:T(8,128)(2,1)}, u32[]{:S(2)}) copy-start(bf16[6144,8]{0,1:T(8,128)(2,1)} %param.25) | copy-start | bytes 294916
  27.3 4.6 %slice-start.4 = ((s8[12582912]{0:T(1024)(128)(4,1)}), s8[4194304]{0:T(1024)(128)(4,1)S(1)}, s32[]{:S(2)}) async-start(s8[12582912]{0:T(1024)(128)(4,1)} %bitcast.4), calls=%async_computation.7 | async-start | bytes 8388608
  27.3 4.6 %slice-start.5 = ((s8[12582912]{0:T(1024)(128)(4,1)}), s8[4194304]{0:T(1024)(128)(4,1)S(1)}, s32[]{:S(2)}) async-start(s8[12582912]{0:T(1024)(128)(4,1)} %bitcast.4), calls=%async_computation.8 | async-start | bytes 8388608
  30.7 1.2 %collective-permute-start.1 = (f32[2,4096]{1,0:T(2,128)S(1)}, f32[2,4096]{1,0:T(2,128)S(1)}, u32[]{:S(2)}, u32[]{:S(2)}) collective-permute-start(f32[2,4096]{1,0:T(2,128)S(1)} %expert.1.refs_0_), channel_id=1, source_target_pairs={{0,1},{1,0},{2,3},{3,2},{4,5},{5,4},{6,7},{7,6},{8,9},{9,8},{10,11... | collective-permute-start | bytes 98312 | tf_op jit(solution)/shard_map/ppermute | solution.py:383

commit v5 on v4

--- a/solution.py
+++ b/solution.py
@@ -207,34 +207,26 @@
     last = jnp.max(jnp.where(hit, ids, -1), axis=1, keepdims=True)
     request = lax.broadcasted_iota(jnp.int32, slot_ref.shape, 0)
     lane = lax.broadcasted_iota(jnp.int32, slot_ref.shape, 1)
-    chosen = jnp.where(lane == 0, first, jnp.where(lane == 1, last, -1))
-    slot_ref[...] = jnp.where(request == chosen, 1.0, 0.0)
+    marks = jnp.where(request == jnp.where(lane == 0, first, last), 1, 0)
+    named = jnp.where(routes_ref[0:1, :] == 0, routes_ref[1:2, :], routes_ref[0:1, :])
+    other = [jnp.sum(jnp.where(ids == r, named, 0), axis=1, keepdims=True) for r in (first, last)]
+    marks = jnp.where(lane == 2, other[0], jnp.where(lane == 3, other[1], marks))
+    slot_ref[...] = marks
 
 
 def resid_kernel(resid_ref, mine_ref, other_ref, slot_ref, o_ref):
     h1 = (resid_ref[...].astype(F32) + (mine_ref[...] + other_ref[...])).astype(BF16).astype(F32)
     routed = [
-        jnp.sum(jnp.where(slot_ref[:, s : s + 1] > 0.0, h1, 0.0), axis=0, keepdims=True) for s in range(2)
+        jnp.sum(jnp.where(slot_ref[:, s : s + 1] > 0, h1, 0.0), axis=0, keepdims=True) for s in range(2)
     ]
     for r in range(o_ref.shape[0]):
         own = h1[r : r + 1]
         o_ref[r] = jnp.concatenate(routed + [own, own], axis=0).astype(BF16)
 
 
-def routed_rows(routes_ref):
-    count = routes_ref.shape[1]
-    first = jnp.int32(count - 1)
-    last = jnp.int32(0)
-    for r in range(count):
-        hit = jnp.logical_or(routes_ref[0, r] == 0, routes_ref[1, r] == 0)
-        first = jnp.where(hit, jnp.minimum(first, r), first)
-        last = jnp.where(hit, r, last)
-    return first, last
-
-
-def expert_kernel(h1_ref, gain_ref, wg_ref, wu_ref, gu_ref):
+def first_kernel(h1_ref, gain_ref, wg_ref, wu_ref, _, gu_ref, x_ref):
     units, _, cols = h1_ref.shape
-    hidden = wg_ref.shape[1]
+    part = wg_ref.shape[1] // 2
     per_half = units // 2
     head = lax.axis_index("heads")
     half = per_half * cols
@@ -242,47 +234,65 @@
     gain = jnp.where(head == 0, gain[:, :half], gain[:, half:])
     h1 = jnp.concatenate([h1_ref[head * per_half + i].astype(F32)[:2] for i in range(per_half)], axis=1)
     x = (h1 * gain).astype(BF16)
-    gu_ref[:, :hidden] = jnp.dot(x, wg_ref[...], preferred_element_type=F32)
-    gu_ref[:, hidden:] = jnp.dot(x, wu_ref[...], preferred_element_type=F32)
-
-
-def side_kernel(routes_ref, h1_ref, gain_ref, router_ref, stat_ref, own_ref, router_all):
+    x_ref[...] = x
+    gu_ref[:, :part] = jnp.dot(x, wg_ref[:, :part], preferred_element_type=F32)
+    gu_ref[:, part:] = jnp.dot(x, wu_ref[:, :part], preferred_element_type=F32)
+
+
+def second_kernel(
+    x_ref, wg_ref, wu_ref, h1_ref, gain_ref, router_ref, slot_ref, _, gu_ref, stat_ref, own_ref
+):
+    part = wg_ref.shape[1] // 2
+    x = x_ref[...]
+    gu_ref[:, :part] = jnp.dot(x, wg_ref[:, part:], preferred_element_type=F32)
+    gu_ref[:, part:] = jnp.dot(x, wu_ref[:, part:], preferred_element_type=F32)
     units, _, cols = h1_ref.shape
     per_half = units // 2
     head = lax.axis_index("heads")
     for i in range(per_half):
         own_ref[:, i * cols : (i + 1) * cols] = h1_ref[head * per_half + i].astype(F32)[2:3]
-    router_all[...] = router_ref[...].astype(F32)
     gain = gain_ref[...].astype(F32).reshape(1, -1)
+    router = router_ref[...].astype(F32)
+    expert = lax.broadcasted_iota(jnp.int32, (router.shape[0], 1), 0)
     h = jnp.concatenate([h1_ref[u].astype(F32)[:2] for u in range(units)], axis=1)
     rstd = lax.rsqrt(jnp.mean(h * h, axis=1, keepdims=True) + 1e-05)
     xn = (h * rstd * gain).astype(BF16).astype(F32)
-    other = []
-    for r in routed_rows(routes_ref):
-        other.append(jnp.where(routes_ref[0, r] == 0, routes_ref[1, r], routes_ref[0, r]))
-    first = jnp.sum(xn * router_all[0:1, :], axis=1, keepdims=True)
-    second = jnp.sum(
-        xn * jnp.concatenate([router_all[pl.ds(e, 1), :] for e in other], axis=0), axis=1, keepdims=True
-    )
-    route = 1.0 / (1.0 + jnp.exp(second - first))
-    lane_ids = lax.broadcasted_iota(jnp.int32, stat_ref.shape, 1)
-    stat_ref[...] = jnp.where(lane_ids == 0, rstd, route)
-
-
-def down_kernel(mine_ref, other_ref, stat_ref, slot_ref, wd_ref, o_ref, full_ref):
-    hidden = wd_ref.shape[0]
+    lane_ids = lax.broadcasted_iota(jnp.int32, (1, LANES), 1)
+    for s in range(2):
+        logits = jnp.sum(router * xn[s : s + 1], axis=1, keepdims=True)
+        other = slot_ref[0:1, 2 + s : 3 + s]
+        diff = jnp.sum(
+            jnp.where(expert == other, logits, 0.0) - jnp.where(expert == 0, logits, 0.0),
+            axis=0,
+            keepdims=True,
+        )
+        route = 1.0 / (1.0 + jnp.exp(diff))
+        stat_ref[s : s + 1, :] = jnp.where(lane_ids == 0, rstd[s : s + 1], route)
+
+
+def activate(mine_ref, other_ref, stat_ref):
+    part = mine_ref.shape[1] // 2
     rstd = stat_ref[:, 0:1]
     route = stat_ref[:, 1:2]
-    gate = (mine_ref[:, :hidden] + other_ref[:, :hidden]) * rstd
-    up = (mine_ref[:, hidden:] + other_ref[:, hidden:]) * (rstd * route)
-    act = (gate / (1.0 + jnp.exp(-gate)) * up).astype(BF16)
-    full = jnp.dot(act, wd_ref[...], preferred_element_type=F32)
+    gate = (mine_ref[:, :part] + other_ref[:, :part]) * rstd
+    up = (mine_ref[:, part:] + other_ref[:, part:]) * (rstd * route)
+    return (gate / (1.0 + jnp.exp(-gate)) * up).astype(BF16)
+
+
+def down_first_kernel(mine_ref, other_ref, stat_ref, wd_ref, o_ref):
+    act = activate(mine_ref, other_ref, stat_ref)
+    o_ref[...] = jnp.dot(act, wd_ref[: act.shape[1], :], preferred_element_type=F32)
+
+
+def down_second_kernel(mine_ref, other_ref, stat_ref, wd_ref, before_ref, slot_ref, o_ref, full_ref):
+    act = activate(mine_ref, other_ref, stat_ref)
+    full = before_ref[...] + jnp.dot(act, wd_ref[act.shape[1] :, :], preferred_element_type=F32)
     for j in range(o_ref.shape[1]):
         for s in range(2):
             full_ref[s, j : j + 1, :] = full[s : s + 1, j * LANES : (j + 1) * LANES]
     for r in range(o_ref.shape[0]):
-        block = jnp.where(slot_ref[r : r + 1, 1:2] > 0.0, full_ref[1], 0.0)
-        o_ref[r] = jnp.where(slot_ref[r : r + 1, 0:1] > 0.0, full_ref[0], block).astype(BF16)
+        block = jnp.where(slot_ref[r : r + 1, 1:2] > 0, full_ref[1], 0.0)
+        o_ref[r] = jnp.where(slot_ref[r : r + 1, 0:1] > 0, full_ref[0], block).astype(BF16)
 
 
 def sum_kernel(parts_ref, own_ref, o_ref):
@@ -368,7 +378,7 @@
     attn_all = exchange(attn)
     proj, slots = call(
         proj_kernel,
-        (jax.ShapeDtypeStruct((rows, cols), F32), jax.ShapeDtypeStruct((rows, LANES), F32)),
+        (jax.ShapeDtypeStruct((rows, cols), F32), jax.ShapeDtypeStruct((rows, LANES), jnp.int32)),
         [VMEM] * 3,
         "proj",
     )(attn_all, in_vmem(w_out), routes_t)
@@ -377,24 +387,36 @@
         resid, proj, proj_other, slots
     )
     h1 = exchange(h1_cols)
-    gu = call(expert_kernel, jax.ShapeDtypeStruct((2, 2 * hidden), F32), [VMEM] * 4, "expert")(
-        h1, norm_gain, in_vmem(w_gate), in_vmem(w_up)
-    )
+    weights = (in_vmem(w_gate), in_vmem(w_up))
+    w_down_near = in_vmem(w_down)
+    gu, x = call(
+        first_kernel,
+        (jax.ShapeDtypeStruct((2, hidden), F32), jax.ShapeDtypeStruct((2, half), BF16)),
+        [VMEM] * 5,
+        "first",
+    )(h1, norm_gain, *weights, w_down_near)
     gu_other = lax.ppermute(gu, "heads", swap)
-    stat, own_h1 = call(
-        side_kernel,
-        (jax.ShapeDtypeStruct((2, LANES), F32), jax.ShapeDtypeStruct((1, half), F32)),
-        [SMEM] + [VMEM] * 3,
-        "side",
-        scratch=(pltpu.VMEM(router.shape[::-1], F32),),
-    )(routes_t, h1, norm_gain, router.T)
+    gu_late, stat, own_h1 = call(
+        second_kernel,
+        (
+            jax.ShapeDtypeStruct((2, hidden), F32),
+            jax.ShapeDtypeStruct((2, LANES), F32),
+            jax.ShapeDtypeStruct((1, half), F32),
+        ),
+        [VMEM] * 8,
+        "second",
+    )(x, *weights, h1, norm_gain, router.T, slots, w_down_near)
+    gu_late_other = lax.ppermute(gu_late, "heads", swap)
+    before = call(down_first_kernel, jax.ShapeDtypeStruct((2, half), F32), [VMEM] * 4, "down_first")(
+        gu, gu_other, stat, w_down_near
+    )
     full = call(
-        down_kernel,
+        down_second_kernel,
         jax.ShapeDtypeStruct((rows, chunks, LANES), BF16),
-        [VMEM] * 5,
-        "down",
+        [VMEM] * 6,
+        "down_second",
         scratch=(pltpu.VMEM((2, chunks, LANES), F32),),
-    )(gu, gu_other, stat, slots, in_vmem(w_down))
+    )(gu_late, gu_late_other, stat, w_down_near, before, slots)
     parts = exchange(full)
     return call(sum_kernel, jax.ShapeDtypeStruct((1, half), BF16), [VMEM] * 2, "total")(
         parts, own_h1

time: 43.8 us -> 43.5 us (level)
  starting transfers between devices: 0.01 us -> 0.52 us
  Pallas kernels: 8.05 us -> 7.6 us
    ppermute x0 -> x1, starting transfers between devices: none -> 0.51 us  [small_body(): gu_late_other = lax.ppermute(gu_late, 'heads', swap)]
    pallas_call x8 -> x9, Pallas kernels: 8.05 us -> 7.6 us  [call(): return lambda *ops: f(*ops, *more)]
  transfers between devices with their start and end apart: 2 -> 3, of which waited for: 2 -> 1; matrix products, arithmetic and copies ran while one was open for 0% -> 0% of each run, Pallas kernels for 2% -> 6%
where the time goes in v5:
time: 43.5 us; the launch traced here: 43.3 us
  blocking collectives  32.5 us (75%)
  Pallas kernels  7.6 us (17%)
  waiting for transfers between devices  1.2 us (3%)
  between operations  1.01 us (2%)
  starting transfers between devices  0.52 us (1%)
  local copies, waits for them, and re-layouts  0.51 us (1%)
    all_to_all x3, blocking collectives, exchange(): return lax.all_to_all(x, 'units', split_axis=0, concat_axis=0, tiled=True)  32.5 us
    pallas_call x9, Pallas kernels, call(): return lambda *ops: f(*ops, *more)  7.6 us
    ppermute x1, waiting for transfers between devices, small_body(): proj_other = lax.ppermute(proj, 'heads', swap)  1.2 us
  transfers between devices with their start and end apart: 3, of which 1 were waited for; matrix products, arithmetic and copies ran while one was open for 0% of the time, Pallas kernels for 6%

profile of v5, /device:TPU:0, one launch (start us, length us, event | category | flops | bytes accessed | tf_op | source)
XLA Modules:
  0.0 43.3 jit_solution(16957231512866679621)
XLA Ops:
  0.0 0.0 copy-start.4
  0.8 0.0 slice-start.9
  0.8 0.0 slice-start
  0.8 0.0 slice-start.3
  0.8 0.0 slice-start.6
  0.8 0.0 copy-done.9
  0.8 0.2 copy-done.1
  1.1 0.2 copy-done
  1.2 0.0 copy-done.7
  1.2 0.0 copy-done.6
  1.2 0.0 copy-done.4
  1.2 0.0 copy-start.8
  1.3 0.0 copy-start.5
  1.3 0.0 slice-start.1
  1.3 0.0 slice-start.2
  1.3 0.0 slice-start.4
  1.3 0.0 slice-start.5
  1.3 0.0 slice-start.7
  1.3 0.0 slice-start.8
  1.3 0.0 copy-start.3
  1.4 0.5 %attend.1 = bf16[8,24,128]{2,1,0:T(8,128)(2,1)S(1)} custom-call(f32[8,128]{1,0:T(8,128)S(1)} %begin.1.refs_0_, s32[1]{0:T(128)S(6)} %copy.16.refs_1_, s32[1,4]{1,0:T(1,128)S(1)} %copy-done.9, bf16[1,3072]{1,0:T(2,128)(2,1)S(1)} %copy-done.4, bf16[1,512]{1,0:T(2,128)(2,1)S(1)} %copy-done.6, bf16[1,512]{1,0:T(2,128)(2,1)S(1)} %copy-done.7, ...), custom_call_target="tpu_custom_call" | custom-call | tf_op jit(solution)/shard_map/attend/pallas_call | solution.py:364
  1.9 14.1 %all_to_all.15.refs_0_ = bf16[8,24,128]{2,1,0:T(8,128)(2,1)S(1)} all-to-all(bf16[8,24,128]{2,1,0:T(8,128)(2,1)S(1)} %attend.1), channel_id=1, replica_groups=mesh['groups'=2,'units'=8,'heads'=2] {'units'}, dimensions={0} | all-to-all | bytes 98304 | tf_op jit(solution)/shard_map/all_to_all | solution.py:346
  16.0 0.0 slice-done.9
  16.0 0.0 slice-done.10
  16.0 0.0 copy-done.8
  16.0 0.7 %proj.1 = (f32[8,768]{1,0:T(8,128)S(1)}, s32[8,128]{1,0:T(8,128)S(1)}) custom-call(bf16[8,24,128]{2,1,0:T(8,128)(2,1)S(1)} %all_to_all.15.refs_0_, bf16[3072,768]{1,0:T(8,128)(2,1)S(1)} %bitcast.9, s32[2,8]{1,0:T(2,128)S(1)} %bitcast.11), custom_call_target="tpu_custom_call" | custom-call | tf_op jit(solution)/shard_map/proj/pallas_call | solution.py:364
  16.7 0.0 collective-permute-start
  16.8 1.2 %collective-permute-done.refs_2_ = f32[8,768]{1,0:T(8,128)S(1)} collective-permute-done((f32[8,768]{1,0:T(8,128)S(1)}, f32[8,768]{1,0:T(8,128)S(1)}, u32[]{:S(2)}, u32[]{:S(2)}) %collective-permute-start) | collective-permute-done | bytes 24608 | tf_op jit(solution)/shard_map/ppermute | solution.py:385
  17.9 0.0 copy-done.5
  18.0 0.1 resid.1
  18.1 9.2 %all_to_all.16.refs_0_.refs_3_ = bf16[8,4,768]{2,1,0:T(4,128)(2,1)S(1)} all-to-all(bf16[8,4,768]{2,1,0:T(4,128)(2,1)S(1)} %resid.1), channel_id=1, replica_groups=mesh['groups'=2,'units'=8,'heads'=2] {'units'}, dimensions={0} | all-to-all | bytes 98304 | tf_op jit(solution)/shard_map/all_to_all | solution.py:346
  27.2 0.0 slice-done
  27.2 0.0 slice-done.3
  27.2 0.0 slice-done.6
  27.3 0.0 slice-done.1
  27.3 0.0 slice-done.2
  27.3 0.0 slice-done.4
  27.3 0.0 copy-start.2
  27.4 1.7 %first.1 = (f32[2,2048]{1,0:T(2,128)S(1)}, bf16[2,3072]{1,0:T(2,128)(2,1)S(1)}) custom-call(bf16[8,4,768]{2,1,0:T(4,128)(2,1)S(1)} %all_to_all.16.refs_0_.refs_3_, bf16[6144]{0:T(1024)(128)(2,1)S(1)} %copy-done.3, bf16[3072,2048]{1,0:T(8,128)(2,1)S(1)} %bitcast.5, bf16[3072,2048]{1,0:T(8,128)(2,1)S(1)} %bitcast.7, bf16[2048,3072]{1,0:T(8,128)(2,1)S(1)} %bitcast.3), custom_call_target="tpu_custom_call" | custom-call | tf_op jit(solution)/shard_map/first/pallas_call | solution.py:364
  29.1 0.0 collective-permute-start.2
  29.1 1.8 %second.1 = (f32[2,2048]{1,0:T(2,128)S(1)}, f32[2,128]{1,0:T(2,128)S(1)}, f32[1,3072]{1,0:T(1,128)S(1)}) custom-call(bf16[2,3072]{1,0:T(2,128)(2,1)S(1)} %get-tuple-element.14.refs_0_, bf16[3072,2048]{1,0:T(8,128)(2,1)S(1)} %bitcast.5, bf16[3072,2048]{1,0:T(8,128)(2,1)S(1)} %bitcast.7, bf16[8,4,768]{2,1,0:T(4,128)(2,1)S(1)} %all_to_all.16.refs_0_.refs_3_, ...), custom_call_target="tpu_custom_call" | custom-call | tf_op jit(solution)/shard_map/second/pallas_call | solution.py:364
  30.9 0.5 %collective-permute-start.1 = (f32[2,2048]{1,0:T(2,128)S(1)}, f32[2,2048]{1,0:T(2,128)S(1)}, u32[]{:S(2)}, u32[]{:S(2)}) collective-permute-start(f32[2,2048]{1,0:T(2,128)S(1)} %get-tuple-element.15.refs_0_), channel_id=1, source_target_pairs={{0,1},{1,0},{2,3},{3,2},{4,5},{5,4},{6,7},{7,6},{8,9},{9,8},{10,11... | collective-permute-start | bytes 49160 | tf_op jit(solution)/shard_map/ppermute | solution.py:409
  31.4 0.0 collective-permute-done.2.refs_1_
  31.4 1.0 %down_first.1.refs_4_ = f32[2,3072]{1,0:T(2,128)S(1)} custom-call(f32[2,2048]{1,0:T(2,128)S(1)} %get-tuple-element.17.refs_0_, f32[2,2048]{1,0:T(2,128)S(1)} %collective-permute-done.2.refs_1_, f32[2,128]{1,0:T(2,128)S(1)} %get-tuple-element.16.refs_2_, bf16[2048,3072]{1,0:T(8,128)(2,1)S(1)} %bitcast.3), custom_call_target="tpu_custom_call" | custom-call | tf_op jit(solution)/shard_map/down_first/pallas_call | solution.py:364
  32.4 0.0 collective-permute-done.1.refs_1_
  32.4 1.1 %down_second.1 = bf16[8,24,128]{2,1,0:T(8,128)(2,1)S(1)} custom-call(f32[2,2048]{1,0:T(2,128)S(1)} %get-tuple-element.15.refs_0_, f32[2,2048]{1,0:T(2,128)S(1)} %collective-permute-done.1.refs_1_, f32[2,128]{1,0:T(2,128)S(1)} %get-tuple-element.16.refs_2_, bf16[2048,3072]{1,0:T(8,128)(2,1)S(1)} %bitcast.3, f32[2,3072]{1,0:T(2,128)S(1)} %down_first.1.refs_4_, ...), custom_call_target="tpu_custom_call" | custom-call | tf_op jit(solution)/shard_map/down_second/pallas_call | solution.py:364
  33.5 9.2 %all_to_all.17.refs_0_ = bf16[8,24,128]{2,1,0:T(8,128)(2,1)S(1)} all-to-all(bf16[8,24,128]{2,1,0:T(8,128)(2,1)S(1)} %down_second.1), channel_id=1, replica_groups=mesh['groups'=2,'units'=8,'heads'=2] {'units'}, dimensions={0} | all-to-all | bytes 98304 | tf_op jit(solution)/shard_map/all_to_all | solution.py:346
  42.7 0.6 %total.1 = bf16[1,3072]{1,0:T(2,128)(2,1)} custom-call(bf16[8,24,128]{2,1,0:T(8,128)(2,1)S(1)} %all_to_all.17.refs_0_, f32[1,3072]{1,0:T(1,128)S(1)} %get-tuple-element.18.refs_1_), custom_call_target="tpu_custom_call" | custom-call | tf_op jit(solution)/shard_map/total/pallas_call | solution.py:364
  (16 shorter events, 0.0 us)
Async XLA Ops:
  0.0 0.8 %copy-start.9 = (s32[1,4]{1,0:T(1,128)S(1)}, s32[1,4]{1,0:T(1,128)}, u32[]{:S(2)}) copy-start(s32[1,4]{1,0:T(1,128)} %refs_2_.3) | copy-start | bytes 52
  0.0 1.1 %copy-start.1 = (bf16[4,128,512]{2,1,0:T(8,128)(2,1)S(1)}, bf16[4,128,512]{2,1,0:T(8,128)(2,1)}, u32[]{:S(2)}) copy-start(bf16[4,128,512]{2,1,0:T(8,128)(2,1)} %refs_7_.2) | copy-start | bytes 1572868
  0.0 1.2 %copy-start = (bf16[4,128,512]{2,1,0:T(8,128)(2,1)S(1)}, bf16[4,128,512]{2,1,0:T(8,128)(2,1)}, u32[]{:S(2)}) copy-start(bf16[4,128,512]{2,1,0:T(8,128)(2,1)} %refs_6_.1) | copy-start | bytes 1572868
  0.0 1.2 %copy-start.7 = (bf16[1,512]{1,0:T(2,128)(2,1)S(1)}, bf16[1,512]{1,0:T(2,128)(2,1)}, u32[]{:S(2)}) copy-start(bf16[1,512]{1,0:T(2,128)(2,1)} %refs_5_.1) | copy-start | bytes 3076
  0.0 1.2 %copy-start.6 = (bf16[1,512]{1,0:T(2,128)(2,1)S(1)}, bf16[1,512]{1,0:T(2,128)(2,1)}, u32[]{:S(2)}) copy-start(bf16[1,512]{1,0:T(2,128)(2,1)} %refs_4_.3) | copy-start | bytes 3076
  0.0 1.2 %copy-start.4 = (bf16[1,3072]{1,0:T(2,128)(2,1)S(1)}, bf16[1,3072]{1,0:T(2,128)(2,1)}, u32[]{:S(2)}) copy-start(bf16[1,3072]{1,0:T(2,128)(2,1)} %refs_3_.4) | copy-start | bytes 18436
  0.8 15.2 %slice-start.9 = ((s8[4718592]{0:T(1024)(128)(4,1)}), s8[4194304]{0:T(1024)(128)(4,1)S(1)}, s32[]{:S(2)}) async-start(s8[4718592]{0:T(1024)(128)(4,1)} %bitcast.8), calls=%async_computation.12 | async-start | bytes 8388608
  0.8 26.5 %slice-start = ((s8[12582912]{0:T(1024)(128)(4,1)}), s8[4194304]{0:T(1024)(128)(4,1)S(1)}, s32[]{:S(2)}) async-start(s8[12582912]{0:T(1024)(128)(4,1)} %bitcast.2), calls=%async_computation.3 | async-start | bytes 8388608
  0.8 26.5 %slice-start.3 = ((s8[12582912]{0:T(1024)(128)(4,1)}), s8[4194304]{0:T(1024)(128)(4,1)S(1)}, s32[]{:S(2)}) async-start(s8[12582912]{0:T(1024)(128)(4,1)} %bitcast.4), calls=%async_computation.6 | async-start | bytes 8388608
  0.8 26.5 %slice-start.6 = ((s8[12582912]{0:T(1024)(128)(4,1)}), s8[4194304]{0:T(1024)(128)(4,1)S(1)}, s32[]{:S(2)}) async-start(s8[12582912]{0:T(1024)(128)(4,1)} %bitcast.6), calls=%async_computation.9 | async-start | bytes 8388608
  1.2 14.8 %slice-start.10 = ((s8[4718592]{0:T(1024)(128)(4,1)}), s8[524288]{0:T(1024)(128)(4,1)S(1)}, s32[]{:S(2)}) async-start(s8[4718592]{0:T(1024)(128)(4,1)} %bitcast.8), calls=%async_computation.13 | async-start | bytes 1048576
  1.2 14.8 %copy-start.8 = (s32[8,2]{0,1:T(2,128)S(1)}, s32[8,2]{0,1:T(2,128)}, u32[]{:S(2)}) copy-start(s32[8,2]{0,1:T(2,128)} %param.26) | copy-start | bytes 196
  1.3 16.7 %copy-start.5 = (bf16[8,768]{1,0:T(8,128)(2,1)S(1)}, bf16[8,768]{1,0:T(8,128)(2,1)}, u32[]{:S(2)}) copy-start(bf16[8,768]{1,0:T(8,128)(2,1)} %refs_0_.3) | copy-start | bytes 36868
  1.3 26.0 %slice-start.1 = ((s8[12582912]{0:T(1024)(128)(4,1)}), s8[4194304]{0:T(1024)(128)(4,1)S(1)}, s32[]{:S(2)}) async-start(s8[12582912]{0:T(1024)(128)(4,1)} %bitcast.2), calls=%async_computation.4 | async-start | bytes 8388608
  1.3 26.0 %slice-start.2 = ((s8[12582912]{0:T(1024)(128)(4,1)}), s8[4194304]{0:T(1024)(128)(4,1)S(1)}, s32[]{:S(2)}) async-start(s8[12582912]{0:T(1024)(128)(4,1)} %bitcast.2), calls=%async_computation.5 | async-start | bytes 8388608
  1.3 26.0 %slice-start.4 = ((s8[12582912]{0:T(1024)(128)(4,1)}), s8[4194304]{0:T(1024)(128)(4,1)S(1)}, s32[]{:S(2)}) async-start(s8[12582912]{0:T(1024)(128)(4,1)} %bitcast.4), calls=%async_computation.7 | async-start | bytes 8388608
  1.3 26.0 %slice-start.5 = ((s8[12582912]{0:T(1024)(128)(4,1)}), s8[4194304]{0:T(1024)(128)(4,1)S(1)}, s32[]{:S(2)}) async-start(s8[12582912]{0:T(1024)(128)(4,1)} %bitcast.4), calls=%async_computation.8 | async-start | bytes 8388608
  1.3 26.0 %slice-start.7 = ((s8[12582912]{0:T(1024)(128)(4,1)}), s8[4194304]{0:T(1024)(128)(4,1)S(1)}, s32[]{:S(2)}) async-start(s8[12582912]{0:T(1024)(128)(4,1)} %bitcast.6), calls=%async_computation.10 | async-start | bytes 8388608
  1.3 26.0 %slice-start.8 = ((s8[12582912]{0:T(1024)(128)(4,1)}), s8[4194304]{0:T(1024)(128)(4,1)S(1)}, s32[]{:S(2)}) async-start(s8[12582912]{0:T(1024)(128)(4,1)} %bitcast.6), calls=%async_computation.11 | async-start | bytes 8388608
  1.3 26.0 %copy-start.3 = (bf16[6144]{0:T(1024)(128)(2,1)S(1)}, bf16[6144]{0:T(1024)(128)(2,1)}, u32[]{:S(2)}) copy-start(bf16[6144]{0:T(1024)(128)(2,1)} %refs_4_.5) | copy-start | bytes 36868
  16.7 1.2 %collective-permute-start = (f32[8,768]{1,0:T(8,128)S(1)}, f32[8,768]{1,0:T(8,128)S(1)}, u32[]{:S(2)}, u32[]{:S(2)}) collective-permute-start(f32[8,768]{1,0:T(8,128)S(1)} %get-tuple-element.12.refs_1_), channel_id=1, source_target_pairs={{0,1},{1,0},{2,3},{3,2},{4,5},{5,4},{6,7},{7,6},{8,9},{9,8},{10,11... | collective-permute-start | bytes 73736 | tf_op jit(solution)/shard_map/ppermute | solution.py:385
  27.3 1.7 %copy-start.2 = (bf16[6144,8]{0,1:T(8,128)(2,1)S(1)}, bf16[6144,8]{0,1:T(8,128)(2,1)}, u32[]{:S(2)}) copy-start(bf16[6144,8]{0,1:T(8,128)(2,1)} %param.25) | copy-start | bytes 294916
  29.1 2.3 %collective-permute-start.2 = (f32[2,2048]{1,0:T(2,128)S(1)}, f32[2,2048]{1,0:T(2,128)S(1)}, u32[]{:S(2)}, u32[]{:S(2)}) collective-permute-start(f32[2,2048]{1,0:T(2,128)S(1)} %get-tuple-element.17.refs_0_), channel_id=1, source_target_pairs={{0,1},{1,0},{2,3},{3,2},{4,5},{5,4},{6,7},{7,6},{8,9},{9,8},{10,11... | collective-permute-start | bytes 49160 | tf_op jit(solution)/shard_map/ppermute | solution.py:398
  30.9 1.6 %collective-permute-start.1 = (f32[2,2048]{1,0:T(2,128)S(1)}, f32[2,2048]{1,0:T(2,128)S(1)}, u32[]{:S(2)}, u32[]{:S(2)}) collective-permute-start(f32[2,2048]{1,0:T(2,128)S(1)} %get-tuple-element.15.refs_0_), channel_id=1, source_target_pairs={{0,1},{1,0},{2,3},{3,2},{4,5},{5,4},{6,7},{7,6},{8,9},{9,8},{10,11... | collective-permute-start | bytes 49160 | tf_op jit(solution)/shard_map/ppermute | solution.py:409

commit v6 on v5

--- a/solution.py
+++ b/solution.py
@@ -12,6 +12,7 @@
 F32 = jnp.float32
 BF16 = jnp.bfloat16
 MIB = 2**20
+AHEAD_PARTS = 4
 
 
 def attend(
@@ -224,40 +225,21 @@
         o_ref[r] = jnp.concatenate(routed + [own, own], axis=0).astype(BF16)
 
 
-def first_kernel(h1_ref, gain_ref, wg_ref, wu_ref, _, gu_ref, x_ref):
-    units, _, cols = h1_ref.shape
-    part = wg_ref.shape[1] // 2
-    per_half = units // 2
-    head = lax.axis_index("heads")
-    half = per_half * cols
-    gain = gain_ref[...].astype(F32).reshape(1, -1)
-    gain = jnp.where(head == 0, gain[:, :half], gain[:, half:])
-    h1 = jnp.concatenate([h1_ref[head * per_half + i].astype(F32)[:2] for i in range(per_half)], axis=1)
-    x = (h1 * gain).astype(BF16)
-    x_ref[...] = x
-    gu_ref[:, :part] = jnp.dot(x, wg_ref[:, :part], preferred_element_type=F32)
-    gu_ref[:, part:] = jnp.dot(x, wu_ref[:, :part], preferred_element_type=F32)
-
-
-def second_kernel(
-    x_ref, wg_ref, wu_ref, h1_ref, gain_ref, router_ref, slot_ref, _, gu_ref, stat_ref, own_ref
-):
-    part = wg_ref.shape[1] // 2
-    x = x_ref[...]
-    gu_ref[:, :part] = jnp.dot(x, wg_ref[:, part:], preferred_element_type=F32)
-    gu_ref[:, part:] = jnp.dot(x, wu_ref[:, part:], preferred_element_type=F32)
-    units, _, cols = h1_ref.shape
-    per_half = units // 2
-    head = lax.axis_index("heads")
-    for i in range(per_half):
-        own_ref[:, i * cols : (i + 1) * cols] = h1_ref[head * per_half + i].astype(F32)[2:3]
+def gate_up(x, w_refs, o_ref, start, stop, at, width):
+    for i, w_ref in enumerate(w_refs):
+        lanes = slice(i * width + at, i * width + at + stop - start)
+        o_ref[:, lanes] = jnp.dot(x, w_ref[:, start:stop], preferred_element_type=F32)
+
+
+def scales(h1_ref, gain_ref, router_ref, slot_ref):
     gain = gain_ref[...].astype(F32).reshape(1, -1)
     router = router_ref[...].astype(F32)
     expert = lax.broadcasted_iota(jnp.int32, (router.shape[0], 1), 0)
-    h = jnp.concatenate([h1_ref[u].astype(F32)[:2] for u in range(units)], axis=1)
+    h = jnp.concatenate([h1_ref[u].astype(F32)[:2] for u in range(h1_ref.shape[0])], axis=1)
     rstd = lax.rsqrt(jnp.mean(h * h, axis=1, keepdims=True) + 1e-05)
     xn = (h * rstd * gain).astype(BF16).astype(F32)
     lane_ids = lax.broadcasted_iota(jnp.int32, (1, LANES), 1)
+    rows = []
     for s in range(2):
         logits = jnp.sum(router * xn[s : s + 1], axis=1, keepdims=True)
         other = slot_ref[0:1, 2 + s : 3 + s]
@@ -267,26 +249,81 @@
             keepdims=True,
         )
         route = 1.0 / (1.0 + jnp.exp(diff))
-        stat_ref[s : s + 1, :] = jnp.where(lane_ids == 0, rstd[s : s + 1], route)
-
-
-def activate(mine_ref, other_ref, stat_ref):
-    part = mine_ref.shape[1] // 2
-    rstd = stat_ref[:, 0:1]
-    route = stat_ref[:, 1:2]
+        rows.append(jnp.where(lane_ids == 0, rstd[s : s + 1], route))
+    return jnp.concatenate(rows, axis=0)
+
+
+def first_kernel(
+    h1_ref, gain_ref, wg_ref, wu_ref, router_ref, slot_ref, _, gu_ref, x_ref, ahead_ref
+):
+    units, _, cols = h1_ref.shape
+    part = wg_ref.shape[1] // 2
+    ahead = ahead_ref.shape[1] // 2
+    per_half = units // 2
+    head = lax.axis_index("heads")
+    half = per_half * cols
+    gain = gain_ref[...].astype(F32).reshape(1, -1)
+    gain = jnp.where(head == 0, gain[:, :half], gain[:, half:])
+    h1 = jnp.concatenate([h1_ref[head * per_half + i].astype(F32)[:2] for i in range(per_half)], axis=1)
+    x = (h1 * gain).astype(BF16)
+    x_ref[...] = x
+    gate_up(x, (wg_ref, wu_ref), gu_ref, 0, part, 0, part)
+
+    @pl.when(head == 1)
+    def _():
+        gate_up(x_ref[...], (wg_ref, wu_ref), ahead_ref, part, part + ahead, 0, ahead)
+        gu_ref[:, 2 * part :] = scales(h1_ref, gain_ref, router_ref, slot_ref)
+
+    @pl.when(head == 0)
+    def _():
+        ahead_ref[...] = jnp.zeros(ahead_ref.shape, F32)
+        gu_ref[:, 2 * part :] = jnp.zeros((gu_ref.shape[0], LANES), F32)
+
+
+def second_kernel(
+    x_ref, wg_ref, wu_ref, h1_ref, ahead_ref, _, gu_ref, own_ref
+):
+    part = wg_ref.shape[1] // 2
+    ahead = ahead_ref.shape[1] // 2
+    first_core = lax.axis_index("heads") == 0
+
+    @pl.when(first_core)
+    def _():
+        gate_up(x_ref[...], (wg_ref, wu_ref), gu_ref, part, part + ahead, 0, part)
+
+    @pl.when(jnp.logical_not(first_core))
+    def _():
+        gu_ref[:, :ahead] = ahead_ref[:, :ahead]
+        gu_ref[:, part : part + ahead] = ahead_ref[:, ahead:]
+
+    gate_up(x_ref[...], (wg_ref, wu_ref), gu_ref, part + ahead, 2 * part, ahead, part)
+    units, _, cols = h1_ref.shape
+    per_half = units // 2
+    head = lax.axis_index("heads")
+    for i in range(per_half):
+        own_ref[:, i * cols : (i + 1) * cols] = h1_ref[head * per_half + i].astype(F32)[2:3]
+
+
+def activate(mine_ref, other_ref, stat, part):
+    rstd = stat[:, 0:1]
+    route = stat[:, 1:2]
     gate = (mine_ref[:, :part] + other_ref[:, :part]) * rstd
-    up = (mine_ref[:, part:] + other_ref[:, part:]) * (rstd * route)
+    up = (mine_ref[:, part : 2 * part] + other_ref[:, part : 2 * part]) * (rstd * route)
     return (gate / (1.0 + jnp.exp(-gate)) * up).astype(BF16)
 
 
-def down_first_kernel(mine_ref, other_ref, stat_ref, wd_ref, o_ref):
-    act = activate(mine_ref, other_ref, stat_ref)
-    o_ref[...] = jnp.dot(act, wd_ref[: act.shape[1], :], preferred_element_type=F32)
+def down_first_kernel(mine_ref, other_ref, wd_ref, o_ref, stat_ref):
+    part = wd_ref.shape[0] // 2
+    stat = mine_ref[:, 2 * part :] + other_ref[:, 2 * part :]
+    stat_ref[...] = stat
+    act = activate(mine_ref, other_ref, stat, part)
+    o_ref[...] = jnp.dot(act, wd_ref[:part, :], preferred_element_type=F32)
 
 
 def down_second_kernel(mine_ref, other_ref, stat_ref, wd_ref, before_ref, slot_ref, o_ref, full_ref):
-    act = activate(mine_ref, other_ref, stat_ref)
-    full = before_ref[...] + jnp.dot(act, wd_ref[act.shape[1] :, :], preferred_element_type=F32)
+    part = wd_ref.shape[0] // 2
+    act = activate(mine_ref, other_ref, stat_ref[...], part)
+    full = before_ref[...] + jnp.dot(act, wd_ref[part:, :], preferred_element_type=F32)
     for j in range(o_ref.shape[1]):
         for s in range(2):
             full_ref[s, j : j + 1, :] = full[s : s + 1, j * LANES : (j + 1) * LANES]
@@ -389,27 +426,30 @@
     h1 = exchange(h1_cols)
     weights = (in_vmem(w_gate), in_vmem(w_up))
     w_down_near = in_vmem(w_down)
-    gu, x = call(
+    gu, x, ahead = call(
         first_kernel,
-        (jax.ShapeDtypeStruct((2, hidden), F32), jax.ShapeDtypeStruct((2, half), BF16)),
-        [VMEM] * 5,
+        (
+            jax.ShapeDtypeStruct((2, hidden + LANES), F32),
+            jax.ShapeDtypeStruct((2, half), BF16),
+            jax.ShapeDtypeStruct((2, 2 * AHEAD_PARTS * (hidden // 16)), F32),
+        ),
+        [VMEM] * 7,
         "first",
-    )(h1, norm_gain, *weights, w_down_near)
+    )(h1, norm_gain, *weights, router.T, slots, w_down_near)
     gu_other = lax.ppermute(gu, "heads", swap)
-    gu_late, stat, own_h1 = call(
+    gu_late, own_h1 = call(
         second_kernel,
-        (
-            jax.ShapeDtypeStruct((2, hidden), F32),
-            jax.ShapeDtypeStruct((2, LANES), F32),
-            jax.ShapeDtypeStruct((1, half), F32),
-        ),
-        [VMEM] * 8,
+        (jax.ShapeDtypeStruct((2, hidden), F32), jax.ShapeDtypeStruct((1, half), F32)),
+        [VMEM] * 6,
         "second",
-    )(x, *weights, h1, norm_gain, router.T, slots, w_down_near)
+    )(x, *weights, h1, ahead, w_down_near)
     gu_late_other = lax.ppermute(gu_late, "heads", swap)
-    before = call(down_first_kernel, jax.ShapeDtypeStruct((2, half), F32), [VMEM] * 4, "down_first")(
-        gu, gu_other, stat, w_down_near
-    )
+    before, stat = call(
+        down_first_kernel,
+        (jax.ShapeDtypeStruct((2, half), F32), jax.ShapeDtypeStruct((2, LANES), F32)),
+        [VMEM] * 3,
+        "down_first",
+    )(gu, gu_other, w_down_near)
     full = call(
         down_second_kernel,
         jax.ShapeDtypeStruct((rows, chunks, LANES), BF16),

time: 43.5 us -> 43.3 us (level)
  starting transfers between devices: 0.52 us -> 0.01 us
    ppermute x1, starting transfers between devices: 0.51 us -> 0.01 us  [small_body(): gu_late_other = lax.ppermute(gu_late, 'heads', swap)]
  transfers between devices with their start and end apart: 3 -> 3, of which waited for: 1 -> 2; matrix products, arithmetic and copies ran while one was open for 0% -> 0% of each run, Pallas kernels for 6% -> 7%
where the time goes in v6:
time: 43.3 us; the launch traced here: 43.1 us
  blocking collectives  32.5 us (75%)
  Pallas kernels  7.69 us (18%)
  waiting for transfers between devices  1.35 us (3%)
  between operations  1.01 us (2%)
  local copies, waits for them, and re-layouts  0.51 us (1%)
    all_to_all x3, blocking collectives, exchange(): return lax.all_to_all(x, 'units', split_axis=0, concat_axis=0, tiled=True)  32.5 us
    pallas_call x9, Pallas kernels, call(): return lambda *ops: f(*ops, *more)  7.69 us
    ppermute x1, waiting for transfers between devices, small_body(): proj_other = lax.ppermute(proj, 'heads', swap)  1.2 us
  transfers between devices with their start and end apart: 3, of which 2 were waited for; matrix products, arithmetic and copies ran while one was open for 0% of the time, Pallas kernels for 7%

profile of v6, /device:TPU:0, one launch (start us, length us, event | category | flops | bytes accessed | tf_op | source)
XLA Modules:
  0.0 43.1 jit_solution(15444153010257594969)
XLA Ops:
  0.0 0.0 copy-start.3
  0.8 0.0 slice-start.9
  0.8 0.0 slice-start
  0.8 0.0 slice-start.3
  0.8 0.0 slice-start.6
  0.8 0.0 copy-done.9
  0.8 0.2 copy-done.1
  1.1 0.2 copy-done
  1.2 0.0 copy-done.7
  1.2 0.0 copy-done.6
  1.2 0.0 copy-done.3
  1.2 0.0 copy-start.8
  1.3 0.0 copy-start.5
  1.3 0.0 slice-start.1
  1.3 0.0 slice-start.2
  1.3 0.0 slice-start.4
  1.3 0.0 slice-start.5
  1.3 0.0 slice-start.7
  1.3 0.0 slice-start.8
  1.3 0.0 copy-start.2
  1.4 0.0 copy-start.4
  1.4 0.5 %attend.1 = bf16[8,24,128]{2,1,0:T(8,128)(2,1)S(1)} custom-call(f32[8,128]{1,0:T(8,128)S(1)} %begin.1.refs_0_, s32[1]{0:T(128)S(6)} %copy.16.refs_1_, s32[1,4]{1,0:T(1,128)S(1)} %copy-done.9, bf16[1,3072]{1,0:T(2,128)(2,1)S(1)} %copy-done.3, bf16[1,512]{1,0:T(2,128)(2,1)S(1)} %copy-done.6, bf16[1,512]{1,0:T(2,128)(2,1)S(1)} %copy-done.7, ...), custom_call_target="tpu_custom_call" | custom-call | tf_op jit(solution)/shard_map/attend/pallas_call | solution.py:401
  1.9 14.1 %all_to_all.15.refs_0_ = bf16[8,24,128]{2,1,0:T(8,128)(2,1)S(1)} all-to-all(bf16[8,24,128]{2,1,0:T(8,128)(2,1)S(1)} %attend.1), channel_id=1, replica_groups=mesh['groups'=2,'units'=8,'heads'=2] {'units'}, dimensions={0} | all-to-all | bytes 98304 | tf_op jit(solution)/shard_map/all_to_all | solution.py:383
  16.0 0.0 slice-done.9
  16.0 0.0 slice-done.10
  16.0 0.0 copy-done.8
  16.0 0.7 %proj.1 = (f32[8,768]{1,0:T(8,128)S(1)}, s32[8,128]{1,0:T(8,128)S(1)}) custom-call(bf16[8,24,128]{2,1,0:T(8,128)(2,1)S(1)} %all_to_all.15.refs_0_, bf16[3072,768]{1,0:T(8,128)(2,1)S(1)} %bitcast.9, s32[2,8]{1,0:T(2,128)S(1)} %bitcast.11), custom_call_target="tpu_custom_call" | custom-call | tf_op jit(solution)/shard_map/proj/pallas_call | solution.py:401
  16.8 0.0 collective-permute-start
  16.8 1.2 %collective-permute-done.refs_2_ = f32[8,768]{1,0:T(8,128)S(1)} collective-permute-done((f32[8,768]{1,0:T(8,128)S(1)}, f32[8,768]{1,0:T(8,128)S(1)}, u32[]{:S(2)}, u32[]{:S(2)}) %collective-permute-start) | collective-permute-done | bytes 24608 | tf_op jit(solution)/shard_map/ppermute | solution.py:422
  18.0 0.0 copy-done.5
  18.0 0.1 resid.1
  18.1 9.2 %all_to_all.16.refs_0_.refs_3_ = bf16[8,4,768]{2,1,0:T(4,128)(2,1)S(1)} all-to-all(bf16[8,4,768]{2,1,0:T(4,128)(2,1)S(1)} %resid.1), channel_id=1, replica_groups=mesh['groups'=2,'units'=8,'heads'=2] {'units'}, dimensions={0} | all-to-all | bytes 98304 | tf_op jit(solution)/shard_map/all_to_all | solution.py:383
  27.3 0.0 slice-done
  27.3 0.0 slice-done.3
  27.3 0.0 slice-done.6
  27.3 0.0 slice-done.1
  27.3 0.0 slice-done.2
  27.3 0.0 slice-done.4
  27.4 1.7 %first.1 = (f32[2,2176]{1,0:T(2,128)S(1)}, bf16[2,3072]{1,0:T(2,128)(2,1)S(1)}, f32[2,1024]{1,0:T(2,128)S(1)}) custom-call(bf16[8,4,768]{2,1,0:T(4,128)(2,1)S(1)} %all_to_all.16.refs_0_.refs_3_, bf16[6144]{0:T(1024)(128)(2,1)S(1)} %copy-done.4, bf16[3072,2048]{1,0:T(8,128)(2,1)S(1)} %bitcast.5, bf16[3072,2048]{1,0:T(8,128)(2,1)S(1)} %bitcast.7, ...), custom_call_target="tpu_custom_call" | custom-call | tf_op jit(solution)/shard_map/first/pallas_call | solution.py:401
  29.1 0.0 collective-permute-start.2
  29.1 1.9 %second.1 = (f32[2,2048]{1,0:T(2,128)S(1)}, f32[1,3072]{1,0:T(1,128)S(1)}) custom-call(bf16[2,3072]{1,0:T(2,128)(2,1)S(1)} %get-tuple-element.16.refs_0_, bf16[3072,2048]{1,0:T(8,128)(2,1)S(1)} %bitcast.5, bf16[3072,2048]{1,0:T(8,128)(2,1)S(1)} %bitcast.7, bf16[8,4,768]{2,1,0:T(4,128)(2,1)S(1)} %all_to_all.16.refs_0_.refs_3_, ...), custom_call_target="tpu_custom_call" | custom-call | tf_op jit(solution)/shard_map/second/pallas_call | solution.py:401
  31.0 0.0 collective-permute-start.1
  31.0 0.0 collective-permute-done.2.refs_1_
  31.0 1.0 %down_first.1 = (f32[2,3072]{1,0:T(2,128)S(1)}, f32[2,128]{1,0:T(2,128)S(1)}) custom-call(f32[2,2176]{1,0:T(2,128)S(1)} %get-tuple-element.19.refs_0_, f32[2,2176]{1,0:T(2,128)S(1)} %collective-permute-done.2.refs_1_, bf16[2048,3072]{1,0:T(8,128)(2,1)S(1)} %bitcast.3), custom_call_target="tpu_custom_call" | custom-call | tf_op jit(solution)/shard_map/down_first/pallas_call | solution.py:401
  32.0 0.1 collective-permute-done.1.refs_1_
  32.2 1.1 %down_second.1 = bf16[8,24,128]{2,1,0:T(8,128)(2,1)S(1)} custom-call(f32[2,2048]{1,0:T(2,128)S(1)} %get-tuple-element.18.refs_0_, f32[2,2048]{1,0:T(2,128)S(1)} %collective-permute-done.1.refs_1_, f32[2,128]{1,0:T(2,128)S(1)} %get-tuple-element.20.refs_2_, bf16[2048,3072]{1,0:T(8,128)(2,1)S(1)} %bitcast.3, f32[2,3072]{1,0:T(2,128)S(1)} %get-tuple-element.21.refs_4_, ...), custom_call_target="tpu_custom_call" | custom-call | tf_op jit(solution)/shard_map/down_second/pallas_call | solution.py:401
  33.2 9.2 %all_to_all.17.refs_0_ = bf16[8,24,128]{2,1,0:T(8,128)(2,1)S(1)} all-to-all(bf16[8,24,128]{2,1,0:T(8,128)(2,1)S(1)} %down_second.1), channel_id=1, replica_groups=mesh['groups'=2,'units'=8,'heads'=2] {'units'}, dimensions={0} | all-to-all | bytes 98304 | tf_op jit(solution)/shard_map/all_to_all | solution.py:383
  42.4 0.6 %total.1 = bf16[1,3072]{1,0:T(2,128)(2,1)} custom-call(bf16[8,24,128]{2,1,0:T(8,128)(2,1)S(1)} %all_to_all.17.refs_0_, f32[1,3072]{1,0:T(1,128)S(1)} %get-tuple-element.22.refs_1_), custom_call_target="tpu_custom_call" | custom-call | tf_op jit(solution)/shard_map/total/pallas_call | solution.py:401
  (16 shorter events, 0.0 us)
Async XLA Ops:
  0.0 0.8 %copy-start.9 = (s32[1,4]{1,0:T(1,128)S(1)}, s32[1,4]{1,0:T(1,128)}, u32[]{:S(2)}) copy-start(s32[1,4]{1,0:T(1,128)} %refs_2_.4) | copy-start | bytes 52
  0.0 1.1 %copy-start.1 = (bf16[4,128,512]{2,1,0:T(8,128)(2,1)S(1)}, bf16[4,128,512]{2,1,0:T(8,128)(2,1)}, u32[]{:S(2)}) copy-start(bf16[4,128,512]{2,1,0:T(8,128)(2,1)} %refs_7_.1) | copy-start | bytes 1572868
  0.0 1.2 %copy-start = (bf16[4,128,512]{2,1,0:T(8,128)(2,1)S(1)}, bf16[4,128,512]{2,1,0:T(8,128)(2,1)}, u32[]{:S(2)}) copy-start(bf16[4,128,512]{2,1,0:T(8,128)(2,1)} %refs_6_.2) | copy-start | bytes 1572868
  0.0 1.2 %copy-start.7 = (bf16[1,512]{1,0:T(2,128)(2,1)S(1)}, bf16[1,512]{1,0:T(2,128)(2,1)}, u32[]{:S(2)}) copy-start(bf16[1,512]{1,0:T(2,128)(2,1)} %refs_5_.2) | copy-start | bytes 3076
  0.0 1.2 %copy-start.6 = (bf16[1,512]{1,0:T(2,128)(2,1)S(1)}, bf16[1,512]{1,0:T(2,128)(2,1)}, u32[]{:S(2)}) copy-start(bf16[1,512]{1,0:T(2,128)(2,1)} %refs_4_.1) | copy-start | bytes 3076
  0.0 1.2 %copy-start.3 = (bf16[1,3072]{1,0:T(2,128)(2,1)S(1)}, bf16[1,3072]{1,0:T(2,128)(2,1)}, u32[]{:S(2)}) copy-start(bf16[1,3072]{1,0:T(2,128)(2,1)} %refs_3_.3) | copy-start | bytes 18436
  0.8 15.3 %slice-start.9 = ((s8[4718592]{0:T(1024)(128)(4,1)}), s8[4194304]{0:T(1024)(128)(4,1)S(1)}, s32[]{:S(2)}) async-start(s8[4718592]{0:T(1024)(128)(4,1)} %bitcast.8), calls=%async_computation.12 | async-start | bytes 8388608
  0.8 26.5 %slice-start = ((s8[12582912]{0:T(1024)(128)(4,1)}), s8[4194304]{0:T(1024)(128)(4,1)S(1)}, s32[]{:S(2)}) async-start(s8[12582912]{0:T(1024)(128)(4,1)} %bitcast.2), calls=%async_computation.3 | async-start | bytes 8388608
  0.8 26.5 %slice-start.3 = ((s8[12582912]{0:T(1024)(128)(4,1)}), s8[4194304]{0:T(1024)(128)(4,1)S(1)}, s32[]{:S(2)}) async-start(s8[12582912]{0:T(1024)(128)(4,1)} %bitcast.4), calls=%async_computation.6 | async-start | bytes 8388608
  0.8 26.5 %slice-start.6 = ((s8[12582912]{0:T(1024)(128)(4,1)}), s8[4194304]{0:T(1024)(128)(4,1)S(1)}, s32[]{:S(2)}) async-start(s8[12582912]{0:T(1024)(128)(4,1)} %bitcast.6), calls=%async_computation.9 | async-start | bytes 8388608
  1.2 14.8 %slice-start.10 = ((s8[4718592]{0:T(1024)(128)(4,1)}), s8[524288]{0:T(1024)(128)(4,1)S(1)}, s32[]{:S(2)}) async-start(s8[4718592]{0:T(1024)(128)(4,1)} %bitcast.8), calls=%async_computation.13 | async-start | bytes 1048576
  1.2 14.8 %copy-start.8 = (s32[8,2]{0,1:T(2,128)S(1)}, s32[8,2]{0,1:T(2,128)}, u32[]{:S(2)}) copy-start(s32[8,2]{0,1:T(2,128)} %param.26) | copy-start | bytes 196
  1.3 16.7 %copy-start.5 = (bf16[8,768]{1,0:T(8,128)(2,1)S(1)}, bf16[8,768]{1,0:T(8,128)(2,1)}, u32[]{:S(2)}) copy-start(bf16[8,768]{1,0:T(8,128)(2,1)} %refs_0_.3) | copy-start | bytes 36868
  1.3 26.0 %slice-start.1 = ((s8[12582912]{0:T(1024)(128)(4,1)}), s8[4194304]{0:T(1024)(128)(4,1)S(1)}, s32[]{:S(2)}) async-start(s8[12582912]{0:T(1024)(128)(4,1)} %bitcast.2), calls=%async_computation.4 | async-start | bytes 8388608
  1.3 26.0 %slice-start.2 = ((s8[12582912]{0:T(1024)(128)(4,1)}), s8[4194304]{0:T(1024)(128)(4,1)S(1)}, s32[]{:S(2)}) async-start(s8[12582912]{0:T(1024)(128)(4,1)} %bitcast.2), calls=%async_computation.5 | async-start | bytes 8388608
  1.3 26.0 %slice-start.4 = ((s8[12582912]{0:T(1024)(128)(4,1)}), s8[4194304]{0:T(1024)(128)(4,1)S(1)}, s32[]{:S(2)}) async-start(s8[12582912]{0:T(1024)(128)(4,1)} %bitcast.4), calls=%async_computation.7 | async-start | bytes 8388608
  1.3 26.0 %slice-start.5 = ((s8[12582912]{0:T(1024)(128)(4,1)}), s8[4194304]{0:T(1024)(128)(4,1)S(1)}, s32[]{:S(2)}) async-start(s8[12582912]{0:T(1024)(128)(4,1)} %bitcast.4), calls=%async_computation.8 | async-start | bytes 8388608
  1.3 26.0 %slice-start.7 = ((s8[12582912]{0:T(1024)(128)(4,1)}), s8[4194304]{0:T(1024)(128)(4,1)S(1)}, s32[]{:S(2)}) async-start(s8[12582912]{0:T(1024)(128)(4,1)} %bitcast.6), calls=%async_computation.10 | async-start | bytes 8388608
  1.3 26.0 %slice-start.8 = ((s8[12582912]{0:T(1024)(128)(4,1)}), s8[4194304]{0:T(1024)(128)(4,1)S(1)}, s32[]{:S(2)}) async-start(s8[12582912]{0:T(1024)(128)(4,1)} %bitcast.6), calls=%async_computation.11 | async-start | bytes 8388608
  1.3 26.0 %copy-start.2 = (bf16[6144,8]{0,1:T(8,128)(2,1)S(1)}, bf16[6144,8]{0,1:T(8,128)(2,1)}, u32[]{:S(2)}) copy-start(bf16[6144,8]{0,1:T(8,128)(2,1)} %param.25) | copy-start | bytes 294916
  1.4 26.0 %copy-start.4 = (bf16[6144]{0:T(1024)(128)(2,1)S(1)}, bf16[6144]{0:T(1024)(128)(2,1)}, u32[]{:S(2)}) copy-start(bf16[6144]{0:T(1024)(128)(2,1)} %refs_1_.5) | copy-start | bytes 36868
  16.8 1.2 %collective-permute-start = (f32[8,768]{1,0:T(8,128)S(1)}, f32[8,768]{1,0:T(8,128)S(1)}, u32[]{:S(2)}, u32[]{:S(2)}) collective-permute-start(f32[8,768]{1,0:T(8,128)S(1)} %get-tuple-element.14.refs_1_), channel_id=1, source_target_pairs={{0,1},{1,0},{2,3},{3,2},{4,5},{5,4},{6,7},{7,6},{8,9},{9,8},{10,11... | collective-permute-start | bytes 73736 | tf_op jit(solution)/shard_map/ppermute | solution.py:422
  29.1 1.9 %collective-permute-start.2 = (f32[2,2176]{1,0:T(2,128)S(1)}, f32[2,2176]{1,0:T(2,128)S(1)}, u32[]{:S(2)}, u32[]{:S(2)}) collective-permute-start(f32[2,2176]{1,0:T(2,128)S(1)} %get-tuple-element.19.refs_0_), channel_id=1, source_target_pairs={{0,1},{1,0},{2,3},{3,2},{4,5},{5,4},{6,7},{7,6},{8,9},{9,8},{10,11... | collective-permute-start | bytes 52232 | tf_op jit(solution)/shard_map/ppermute | solution.py:439
  31.0 1.2 %collective-permute-start.1 = (f32[2,2048]{1,0:T(2,128)S(1)}, f32[2,2048]{1,0:T(2,128)S(1)}, u32[]{:S(2)}, u32[]{:S(2)}) collective-permute-start(f32[2,2048]{1,0:T(2,128)S(1)} %get-tuple-element.18.refs_0_), channel_id=1, source_target_pairs={{0,1},{1,0},{2,3},{3,2},{4,5},{5,4},{6,7},{7,6},{8,9},{9,8},{10,11... | collective-permute-start | bytes 49160 | tf_op jit(solution)/shard_map/ppermute | solution.py:446

commit v7 on v6

--- a/solution.py
+++ b/solution.py
@@ -12,7 +12,7 @@
 F32 = jnp.float32
 BF16 = jnp.bfloat16
 MIB = 2**20
-AHEAD_PARTS = 4
+AHEAD_PARTS = 2
 
 
 def attend(

time: 43.3 us -> 43.3 us (level)
  no operation moved by 1% of the time
where the time goes in v7:
time: 43.3 us; the launch traced here: 43.1 us
  blocking collectives  32.5 us (75%)
  Pallas kernels  7.69 us (18%)
  waiting for transfers between devices  1.35 us (3%)
  between operations  1.01 us (2%)
  local copies, waits for them, and re-layouts  0.51 us (1%)
    all_to_all x3, blocking collectives, exchange(): return lax.all_to_all(x, 'units', split_axis=0, concat_axis=0, tiled=True)  32.5 us
    pallas_call x9, Pallas kernels, call(): return lambda *ops: f(*ops, *more)  7.69 us
    ppermute x1, waiting for transfers between devices, small_body(): proj_other = lax.ppermute(proj, 'heads', swap)  1.2 us
  transfers between devices with their start and end apart: 3, of which 2 were waited for; matrix products, arithmetic and copies ran while one was open for 0% of the time, Pallas kernels for 7%

profile of v7, /device:TPU:0, one launch (start us, length us, event | category | flops | bytes accessed | tf_op | source)
XLA Modules:
  0.0 43.1 jit_solution(8714902818787792881)
XLA Ops:
  0.0 0.0 copy-start.3
  0.8 0.0 slice-start.9
  0.8 0.0 slice-start
  0.8 0.0 slice-start.3
  0.8 0.0 slice-start.6
  0.8 0.0 copy-done.9
  0.8 0.2 copy-done.1
  1.1 0.2 copy-done
  1.2 0.0 copy-done.7
  1.2 0.0 copy-done.6
  1.2 0.0 copy-done.3
  1.2 0.0 copy-start.8
  1.3 0.0 copy-start.5
  1.3 0.0 slice-start.1
  1.3 0.0 slice-start.2
  1.3 0.0 slice-start.4
  1.3 0.0 slice-start.5
  1.3 0.0 slice-start.7
  1.3 0.0 slice-start.8
  1.3 0.0 copy-start.2
  1.4 0.0 copy-start.4
  1.4 0.5 %attend.1 = bf16[8,24,128]{2,1,0:T(8,128)(2,1)S(1)} custom-call(f32[8,128]{1,0:T(8,128)S(1)} %begin.1.refs_0_, s32[1]{0:T(128)S(6)} %copy.16.refs_1_, s32[1,4]{1,0:T(1,128)S(1)} %copy-done.9, bf16[1,3072]{1,0:T(2,128)(2,1)S(1)} %copy-done.3, bf16[1,512]{1,0:T(2,128)(2,1)S(1)} %copy-done.6, bf16[1,512]{1,0:T(2,128)(2,1)S(1)} %copy-done.7, ...), custom_call_target="tpu_custom_call" | custom-call | tf_op jit(solution)/shard_map/attend/pallas_call | solution.py:401
  1.9 14.1 %all_to_all.15.refs_0_ = bf16[8,24,128]{2,1,0:T(8,128)(2,1)S(1)} all-to-all(bf16[8,24,128]{2,1,0:T(8,128)(2,1)S(1)} %attend.1), channel_id=1, replica_groups=mesh['groups'=2,'units'=8,'heads'=2] {'units'}, dimensions={0} | all-to-all | bytes 98304 | tf_op jit(solution)/shard_map/all_to_all | solution.py:383
  16.0 0.0 slice-done.9
  16.0 0.0 slice-done.10
  16.0 0.0 copy-done.8
  16.0 0.7 %proj.1 = (f32[8,768]{1,0:T(8,128)S(1)}, s32[8,128]{1,0:T(8,128)S(1)}) custom-call(bf16[8,24,128]{2,1,0:T(8,128)(2,1)S(1)} %all_to_all.15.refs_0_, bf16[3072,768]{1,0:T(8,128)(2,1)S(1)} %bitcast.9, s32[2,8]{1,0:T(2,128)S(1)} %bitcast.11), custom_call_target="tpu_custom_call" | custom-call | tf_op jit(solution)/shard_map/proj/pallas_call | solution.py:401
  16.8 0.0 collective-permute-start
  16.8 1.2 %collective-permute-done.refs_2_ = f32[8,768]{1,0:T(8,128)S(1)} collective-permute-done((f32[8,768]{1,0:T(8,128)S(1)}, f32[8,768]{1,0:T(8,128)S(1)}, u32[]{:S(2)}, u32[]{:S(2)}) %collective-permute-start) | collective-permute-done | bytes 24608 | tf_op jit(solution)/shard_map/ppermute | solution.py:422
  18.0 0.0 copy-done.5
  18.0 0.1 resid.1
  18.1 9.2 %all_to_all.16.refs_0_.refs_3_ = bf16[8,4,768]{2,1,0:T(4,128)(2,1)S(1)} all-to-all(bf16[8,4,768]{2,1,0:T(4,128)(2,1)S(1)} %resid.1), channel_id=1, replica_groups=mesh['groups'=2,'units'=8,'heads'=2] {'units'}, dimensions={0} | all-to-all | bytes 98304 | tf_op jit(solution)/shard_map/all_to_all | solution.py:383
  27.3 0.0 slice-done
  27.3 0.0 slice-done.3
  27.3 0.0 slice-done.6
  27.3 0.0 slice-done.1
  27.3 0.0 slice-done.2
  27.3 0.0 slice-done.4
  27.4 1.7 %first.1 = (f32[2,2176]{1,0:T(2,128)S(1)}, bf16[2,3072]{1,0:T(2,128)(2,1)S(1)}, f32[2,512]{1,0:T(2,128)S(1)}) custom-call(bf16[8,4,768]{2,1,0:T(4,128)(2,1)S(1)} %all_to_all.16.refs_0_.refs_3_, bf16[6144]{0:T(1024)(128)(2,1)S(1)} %copy-done.4, bf16[3072,2048]{1,0:T(8,128)(2,1)S(1)} %bitcast.5, bf16[3072,2048]{1,0:T(8,128)(2,1)S(1)} %bitcast.7, ...), custom_call_target="tpu_custom_call" | custom-call | tf_op jit(solution)/shard_map/first/pallas_call | solution.py:401
  29.1 0.0 collective-permute-start.2
  29.1 1.9 %second.1 = (f32[2,2048]{1,0:T(2,128)S(1)}, f32[1,3072]{1,0:T(1,128)S(1)}) custom-call(bf16[2,3072]{1,0:T(2,128)(2,1)S(1)} %get-tuple-element.16.refs_0_, bf16[3072,2048]{1,0:T(8,128)(2,1)S(1)} %bitcast.5, bf16[3072,2048]{1,0:T(8,128)(2,1)S(1)} %bitcast.7, bf16[8,4,768]{2,1,0:T(4,128)(2,1)S(1)} %all_to_all.16.refs_0_.refs_3_, ...), custom_call_target="tpu_custom_call" | custom-call | tf_op jit(solution)/shard_map/second/pallas_call | solution.py:401
  31.0 0.0 collective-permute-start.1
  31.0 0.0 collective-permute-done.2.refs_1_
  31.0 1.0 %down_first.1 = (f32[2,3072]{1,0:T(2,128)S(1)}, f32[2,128]{1,0:T(2,128)S(1)}) custom-call(f32[2,2176]{1,0:T(2,128)S(1)} %get-tuple-element.19.refs_0_, f32[2,2176]{1,0:T(2,128)S(1)} %collective-permute-done.2.refs_1_, bf16[2048,3072]{1,0:T(8,128)(2,1)S(1)} %bitcast.3), custom_call_target="tpu_custom_call" | custom-call | tf_op jit(solution)/shard_map/down_first/pallas_call | solution.py:401
  32.0 0.1 collective-permute-done.1.refs_1_
  32.2 1.1 %down_second.1 = bf16[8,24,128]{2,1,0:T(8,128)(2,1)S(1)} custom-call(f32[2,2048]{1,0:T(2,128)S(1)} %get-tuple-element.18.refs_0_, f32[2,2048]{1,0:T(2,128)S(1)} %collective-permute-done.1.refs_1_, f32[2,128]{1,0:T(2,128)S(1)} %get-tuple-element.20.refs_2_, bf16[2048,3072]{1,0:T(8,128)(2,1)S(1)} %bitcast.3, f32[2,3072]{1,0:T(2,128)S(1)} %get-tuple-element.21.refs_4_, ...), custom_call_target="tpu_custom_call" | custom-call | tf_op jit(solution)/shard_map/down_second/pallas_call | solution.py:401
  33.2 9.2 %all_to_all.17.refs_0_ = bf16[8,24,128]{2,1,0:T(8,128)(2,1)S(1)} all-to-all(bf16[8,24,128]{2,1,0:T(8,128)(2,1)S(1)} %down_second.1), channel_id=1, replica_groups=mesh['groups'=2,'units'=8,'heads'=2] {'units'}, dimensions={0} | all-to-all | bytes 98304 | tf_op jit(solution)/shard_map/all_to_all | solution.py:383
  42.4 0.6 %total.1 = bf16[1,3072]{1,0:T(2,128)(2,1)} custom-call(bf16[8,24,128]{2,1,0:T(8,128)(2,1)S(1)} %all_to_all.17.refs_0_, f32[1,3072]{1,0:T(1,128)S(1)} %get-tuple-element.22.refs_1_), custom_call_target="tpu_custom_call" | custom-call | tf_op jit(solution)/shard_map/total/pallas_call | solution.py:401
  (16 shorter events, 0.0 us)
Async XLA Ops:
  0.0 0.8 %copy-start.9 = (s32[1,4]{1,0:T(1,128)S(1)}, s32[1,4]{1,0:T(1,128)}, u32[]{:S(2)}) copy-start(s32[1,4]{1,0:T(1,128)} %refs_2_.4) | copy-start | bytes 52
  0.0 1.1 %copy-start.1 = (bf16[4,128,512]{2,1,0:T(8,128)(2,1)S(1)}, bf16[4,128,512]{2,1,0:T(8,128)(2,1)}, u32[]{:S(2)}) copy-start(bf16[4,128,512]{2,1,0:T(8,128)(2,1)} %refs_7_.1) | copy-start | bytes 1572868
  0.0 1.2 %copy-start = (bf16[4,128,512]{2,1,0:T(8,128)(2,1)S(1)}, bf16[4,128,512]{2,1,0:T(8,128)(2,1)}, u32[]{:S(2)}) copy-start(bf16[4,128,512]{2,1,0:T(8,128)(2,1)} %refs_6_.2) | copy-start | bytes 1572868
  0.0 1.2 %copy-start.7 = (bf16[1,512]{1,0:T(2,128)(2,1)S(1)}, bf16[1,512]{1,0:T(2,128)(2,1)}, u32[]{:S(2)}) copy-start(bf16[1,512]{1,0:T(2,128)(2,1)} %refs_5_.2) | copy-start | bytes 3076
  0.0 1.2 %copy-start.6 = (bf16[1,512]{1,0:T(2,128)(2,1)S(1)}, bf16[1,512]{1,0:T(2,128)(2,1)}, u32[]{:S(2)}) copy-start(bf16[1,512]{1,0:T(2,128)(2,1)} %refs_4_.1) | copy-start | bytes 3076
  0.0 1.2 %copy-start.3 = (bf16[1,3072]{1,0:T(2,128)(2,1)S(1)}, bf16[1,3072]{1,0:T(2,128)(2,1)}, u32[]{:S(2)}) copy-start(bf16[1,3072]{1,0:T(2,128)(2,1)} %refs_3_.3) | copy-start | bytes 18436
  0.8 15.3 %slice-start.9 = ((s8[4718592]{0:T(1024)(128)(4,1)}), s8[4194304]{0:T(1024)(128)(4,1)S(1)}, s32[]{:S(2)}) async-start(s8[4718592]{0:T(1024)(128)(4,1)} %bitcast.8), calls=%async_computation.12 | async-start | bytes 8388608
  0.8 26.5 %slice-start = ((s8[12582912]{0:T(1024)(128)(4,1)}), s8[4194304]{0:T(1024)(128)(4,1)S(1)}, s32[]{:S(2)}) async-start(s8[12582912]{0:T(1024)(128)(4,1)} %bitcast.2), calls=%async_computation.3 | async-start | bytes 8388608
  0.8 26.5 %slice-start.3 = ((s8[12582912]{0:T(1024)(128)(4,1)}), s8[4194304]{0:T(1024)(128)(4,1)S(1)}, s32[]{:S(2)}) async-start(s8[12582912]{0:T(1024)(128)(4,1)} %bitcast.4), calls=%async_computation.6 | async-start | bytes 8388608
  0.8 26.5 %slice-start.6 = ((s8[12582912]{0:T(1024)(128)(4,1)}), s8[4194304]{0:T(1024)(128)(4,1)S(1)}, s32[]{:S(2)}) async-start(s8[12582912]{0:T(1024)(128)(4,1)} %bitcast.6), calls=%async_computation.9 | async-start | bytes 8388608
  1.2 14.8 %slice-start.10 = ((s8[4718592]{0:T(1024)(128)(4,1)}), s8[524288]{0:T(1024)(128)(4,1)S(1)}, s32[]{:S(2)}) async-start(s8[4718592]{0:T(1024)(128)(4,1)} %bitcast.8), calls=%async_computation.13 | async-start | bytes 1048576
  1.2 14.8 %copy-start.8 = (s32[8,2]{0,1:T(2,128)S(1)}, s32[8,2]{0,1:T(2,128)}, u32[]{:S(2)}) copy-start(s32[8,2]{0,1:T(2,128)} %param.26) | copy-start | bytes 196
  1.3 16.7 %copy-start.5 = (bf16[8,768]{1,0:T(8,128)(2,1)S(1)}, bf16[8,768]{1,0:T(8,128)(2,1)}, u32[]{:S(2)}) copy-start(bf16[8,768]{1,0:T(8,128)(2,1)} %refs_0_.3) | copy-start | bytes 36868
  1.3 26.0 %slice-start.1 = ((s8[12582912]{0:T(1024)(128)(4,1)}), s8[4194304]{0:T(1024)(128)(4,1)S(1)}, s32[]{:S(2)}) async-start(s8[12582912]{0:T(1024)(128)(4,1)} %bitcast.2), calls=%async_computation.4 | async-start | bytes 8388608
  1.3 26.0 %slice-start.2 = ((s8[12582912]{0:T(1024)(128)(4,1)}), s8[4194304]{0:T(1024)(128)(4,1)S(1)}, s32[]{:S(2)}) async-start(s8[12582912]{0:T(1024)(128)(4,1)} %bitcast.2), calls=%async_computation.5 | async-start | bytes 8388608
  1.3 26.0 %slice-start.4 = ((s8[12582912]{0:T(1024)(128)(4,1)}), s8[4194304]{0:T(1024)(128)(4,1)S(1)}, s32[]{:S(2)}) async-start(s8[12582912]{0:T(1024)(128)(4,1)} %bitcast.4), calls=%async_computation.7 | async-start | bytes 8388608
  1.3 26.0 %slice-start.5 = ((s8[12582912]{0:T(1024)(128)(4,1)}), s8[4194304]{0:T(1024)(128)(4,1)S(1)}, s32[]{:S(2)}) async-start(s8[12582912]{0:T(1024)(128)(4,1)} %bitcast.4), calls=%async_computation.8 | async-start | bytes 8388608
  1.3 26.0 %slice-start.7 = ((s8[12582912]{0:T(1024)(128)(4,1)}), s8[4194304]{0:T(1024)(128)(4,1)S(1)}, s32[]{:S(2)}) async-start(s8[12582912]{0:T(1024)(128)(4,1)} %bitcast.6), calls=%async_computation.10 | async-start | bytes 8388608
  1.3 26.0 %slice-start.8 = ((s8[12582912]{0:T(1024)(128)(4,1)}), s8[4194304]{0:T(1024)(128)(4,1)S(1)}, s32[]{:S(2)}) async-start(s8[12582912]{0:T(1024)(128)(4,1)} %bitcast.6), calls=%async_computation.11 | async-start | bytes 8388608
  1.3 26.0 %copy-start.2 = (bf16[6144,8]{0,1:T(8,128)(2,1)S(1)}, bf16[6144,8]{0,1:T(8,128)(2,1)}, u32[]{:S(2)}) copy-start(bf16[6144,8]{0,1:T(8,128)(2,1)} %param.25) | copy-start | bytes 294916
  1.4 26.0 %copy-start.4 = (bf16[6144]{0:T(1024)(128)(2,1)S(1)}, bf16[6144]{0:T(1024)(128)(2,1)}, u32[]{:S(2)}) copy-start(bf16[6144]{0:T(1024)(128)(2,1)} %refs_1_.5) | copy-start | bytes 36868
  16.8 1.2 %collective-permute-start = (f32[8,768]{1,0:T(8,128)S(1)}, f32[8,768]{1,0:T(8,128)S(1)}, u32[]{:S(2)}, u32[]{:S(2)}) collective-permute-start(f32[8,768]{1,0:T(8,128)S(1)} %get-tuple-element.14.refs_1_), channel_id=1, source_target_pairs={{0,1},{1,0},{2,3},{3,2},{4,5},{5,4},{6,7},{7,6},{8,9},{9,8},{10,11... | collective-permute-start | bytes 73736 | tf_op jit(solution)/shard_map/ppermute | solution.py:422
  29.1 1.9 %collective-permute-start.2 = (f32[2,2176]{1,0:T(2,128)S(1)}, f32[2,2176]{1,0:T(2,128)S(1)}, u32[]{:S(2)}, u32[]{:S(2)}) collective-permute-start(f32[2,2176]{1,0:T(2,128)S(1)} %get-tuple-element.19.refs_0_), channel_id=1, source_target_pairs={{0,1},{1,0},{2,3},{3,2},{4,5},{5,4},{6,7},{7,6},{8,9},{9,8},{10,11... | collective-permute-start | bytes 52232 | tf_op jit(solution)/shard_map/ppermute | solution.py:439
  31.0 1.2 %collective-permute-start.1 = (f32[2,2048]{1,0:T(2,128)S(1)}, f32[2,2048]{1,0:T(2,128)S(1)}, u32[]{:S(2)}, u32[]{:S(2)}) collective-permute-start(f32[2,2048]{1,0:T(2,128)S(1)} %get-tuple-element.18.refs_0_), channel_id=1, source_target_pairs={{0,1},{1,0},{2,3},{3,2},{4,5},{5,4},{6,7},{7,6},{8,9},{9,8},{10,11... | collective-permute-start | bytes 49160 | tf_op jit(solution)/shard_map/ppermute | solution.py:446

commit v8 on v6

--- a/solution.py
+++ b/solution.py
@@ -336,9 +336,8 @@
     moe = parts_ref[0].astype(F32)
     for u in range(1, parts_ref.shape[0]):
         moe = moe + parts_ref[u].astype(F32)
-    for j in range(parts_ref.shape[1]):
-        lanes = slice(j * LANES, (j + 1) * LANES)
-        o_ref[:, lanes] = (own_ref[:, lanes] + moe[j : j + 1, :]).astype(o_ref.dtype)
+    flat = jnp.concatenate([moe[j : j + 1, :] for j in range(parts_ref.shape[1])], axis=1)
+    o_ref[...] = (own_ref[...] + flat).astype(o_ref.dtype)
 
 
 SMEM = pl.BlockSpec(memory_space=pltpu.SMEM)

time: 43.3 us -> 43.3 us (level)
  no operation moved by 1% of the time
where the time goes in v8:
time: 43.3 us; the launch traced here: 43.1 us
  blocking collectives  32.5 us (75%)
  Pallas kernels  7.69 us (18%)
  waiting for transfers between devices  1.35 us (3%)
  between operations  1.01 us (2%)
  local copies, waits for them, and re-layouts  0.51 us (1%)
    all_to_all x3, blocking collectives, exchange(): return lax.all_to_all(x, 'units', split_axis=0, concat_axis=0, tiled=True)  32.5 us
    pallas_call x9, Pallas kernels, call(): return lambda *ops: f(*ops, *more)  7.69 us
    ppermute x1, waiting for transfers between devices, small_body(): proj_other = lax.ppermute(proj, 'heads', swap)  1.2 us
  transfers between devices with their start and end apart: 3, of which 2 were waited for; matrix products, arithmetic and copies ran while one was open for 0% of the time, Pallas kernels for 7%

profile of v8, /device:TPU:0, one launch (start us, length us, event | category | flops | bytes accessed | tf_op | source)
XLA Modules:
  0.0 43.1 jit_solution(8236106526736420860)
XLA Ops:
  0.0 0.0 copy-start.3
  0.8 0.0 slice-start.9
  0.8 0.0 slice-start
  0.8 0.0 slice-start.3
  0.8 0.0 slice-start.6
  0.8 0.0 copy-done.9
  0.8 0.2 copy-done.1
  1.1 0.2 copy-done
  1.2 0.0 copy-done.7
  1.2 0.0 copy-done.6
  1.2 0.0 copy-done.3
  1.2 0.0 copy-start.8
  1.3 0.0 copy-start.5
  1.3 0.0 slice-start.1
  1.3 0.0 slice-start.2
  1.3 0.0 slice-start.4
  1.3 0.0 slice-start.5
  1.3 0.0 slice-start.7
  1.3 0.0 slice-start.8
  1.3 0.0 copy-start.2
  1.4 0.0 copy-start.4
  1.4 0.5 %attend.1 = bf16[8,24,128]{2,1,0:T(8,128)(2,1)S(1)} custom-call(f32[8,128]{1,0:T(8,128)S(1)} %begin.1.refs_0_, s32[1]{0:T(128)S(6)} %copy.16.refs_1_, s32[1,4]{1,0:T(1,128)S(1)} %copy-done.9, bf16[1,3072]{1,0:T(2,128)(2,1)S(1)} %copy-done.3, bf16[1,512]{1,0:T(2,128)(2,1)S(1)} %copy-done.6, bf16[1,512]{1,0:T(2,128)(2,1)S(1)} %copy-done.7, ...), custom_call_target="tpu_custom_call" | custom-call | tf_op jit(solution)/shard_map/attend/pallas_call | solution.py:400
  1.9 14.1 %all_to_all.15.refs_0_ = bf16[8,24,128]{2,1,0:T(8,128)(2,1)S(1)} all-to-all(bf16[8,24,128]{2,1,0:T(8,128)(2,1)S(1)} %attend.1), channel_id=1, replica_groups=mesh['groups'=2,'units'=8,'heads'=2] {'units'}, dimensions={0} | all-to-all | bytes 98304 | tf_op jit(solution)/shard_map/all_to_all | solution.py:382
  16.0 0.0 slice-done.9
  16.0 0.0 slice-done.10
  16.0 0.0 copy-done.8
  16.0 0.7 %proj.1 = (f32[8,768]{1,0:T(8,128)S(1)}, s32[8,128]{1,0:T(8,128)S(1)}) custom-call(bf16[8,24,128]{2,1,0:T(8,128)(2,1)S(1)} %all_to_all.15.refs_0_, bf16[3072,768]{1,0:T(8,128)(2,1)S(1)} %bitcast.9, s32[2,8]{1,0:T(2,128)S(1)} %bitcast.11), custom_call_target="tpu_custom_call" | custom-call | tf_op jit(solution)/shard_map/proj/pallas_call | solution.py:400
  16.8 0.0 collective-permute-start
  16.8 1.2 %collective-permute-done.refs_2_ = f32[8,768]{1,0:T(8,128)S(1)} collective-permute-done((f32[8,768]{1,0:T(8,128)S(1)}, f32[8,768]{1,0:T(8,128)S(1)}, u32[]{:S(2)}, u32[]{:S(2)}) %collective-permute-start) | collective-permute-done | bytes 24608 | tf_op jit(solution)/shard_map/ppermute | solution.py:421
  18.0 0.0 copy-done.5
  18.0 0.1 resid.1
  18.1 9.2 %all_to_all.16.refs_0_.refs_3_ = bf16[8,4,768]{2,1,0:T(4,128)(2,1)S(1)} all-to-all(bf16[8,4,768]{2,1,0:T(4,128)(2,1)S(1)} %resid.1), channel_id=1, replica_groups=mesh['groups'=2,'units'=8,'heads'=2] {'units'}, dimensions={0} | all-to-all | bytes 98304 | tf_op jit(solution)/shard_map/all_to_all | solution.py:382
  27.3 0.0 slice-done
  27.3 0.0 slice-done.3
  27.3 0.0 slice-done.6
  27.3 0.0 slice-done.1
  27.3 0.0 slice-done.2
  27.3 0.0 slice-done.4
  27.4 1.7 %first.1 = (f32[2,2176]{1,0:T(2,128)S(1)}, bf16[2,3072]{1,0:T(2,128)(2,1)S(1)}, f32[2,1024]{1,0:T(2,128)S(1)}) custom-call(bf16[8,4,768]{2,1,0:T(4,128)(2,1)S(1)} %all_to_all.16.refs_0_.refs_3_, bf16[6144]{0:T(1024)(128)(2,1)S(1)} %copy-done.4, bf16[3072,2048]{1,0:T(8,128)(2,1)S(1)} %bitcast.5, bf16[3072,2048]{1,0:T(8,128)(2,1)S(1)} %bitcast.7, ...), custom_call_target="tpu_custom_call" | custom-call | tf_op jit(solution)/shard_map/first/pallas_call | solution.py:400
  29.1 0.0 collective-permute-start.2
  29.1 1.9 %second.1 = (f32[2,2048]{1,0:T(2,128)S(1)}, f32[1,3072]{1,0:T(1,128)S(1)}) custom-call(bf16[2,3072]{1,0:T(2,128)(2,1)S(1)} %get-tuple-element.16.refs_0_, bf16[3072,2048]{1,0:T(8,128)(2,1)S(1)} %bitcast.5, bf16[3072,2048]{1,0:T(8,128)(2,1)S(1)} %bitcast.7, bf16[8,4,768]{2,1,0:T(4,128)(2,1)S(1)} %all_to_all.16.refs_0_.refs_3_, ...), custom_call_target="tpu_custom_call" | custom-call | tf_op jit(solution)/shard_map/second/pallas_call | solution.py:400
  31.0 0.0 collective-permute-start.1
  31.0 0.0 collective-permute-done.2.refs_1_
  31.0 1.0 %down_first.1 = (f32[2,3072]{1,0:T(2,128)S(1)}, f32[2,128]{1,0:T(2,128)S(1)}) custom-call(f32[2,2176]{1,0:T(2,128)S(1)} %get-tuple-element.19.refs_0_, f32[2,2176]{1,0:T(2,128)S(1)} %collective-permute-done.2.refs_1_, bf16[2048,3072]{1,0:T(8,128)(2,1)S(1)} %bitcast.3), custom_call_target="tpu_custom_call" | custom-call | tf_op jit(solution)/shard_map/down_first/pallas_call | solution.py:400
  32.0 0.1 collective-permute-done.1.refs_1_
  32.2 1.1 %down_second.1 = bf16[8,24,128]{2,1,0:T(8,128)(2,1)S(1)} custom-call(f32[2,2048]{1,0:T(2,128)S(1)} %get-tuple-element.18.refs_0_, f32[2,2048]{1,0:T(2,128)S(1)} %collective-permute-done.1.refs_1_, f32[2,128]{1,0:T(2,128)S(1)} %get-tuple-element.20.refs_2_, bf16[2048,3072]{1,0:T(8,128)(2,1)S(1)} %bitcast.3, f32[2,3072]{1,0:T(2,128)S(1)} %get-tuple-element.21.refs_4_, ...), custom_call_target="tpu_custom_call" | custom-call | tf_op jit(solution)/shard_map/down_second/pallas_call | solution.py:400
  33.2 9.2 %all_to_all.17.refs_0_ = bf16[8,24,128]{2,1,0:T(8,128)(2,1)S(1)} all-to-all(bf16[8,24,128]{2,1,0:T(8,128)(2,1)S(1)} %down_second.1), channel_id=1, replica_groups=mesh['groups'=2,'units'=8,'heads'=2] {'units'}, dimensions={0} | all-to-all | bytes 98304 | tf_op jit(solution)/shard_map/all_to_all | solution.py:382
  42.4 0.6 %total.1 = bf16[1,3072]{1,0:T(2,128)(2,1)} custom-call(bf16[8,24,128]{2,1,0:T(8,128)(2,1)S(1)} %all_to_all.17.refs_0_, f32[1,3072]{1,0:T(1,128)S(1)} %get-tuple-element.22.refs_1_), custom_call_target="tpu_custom_call" | custom-call | tf_op jit(solution)/shard_map/total/pallas_call | solution.py:400
  (16 shorter events, 0.0 us)
Async XLA Ops:
  0.0 0.8 %copy-start.9 = (s32[1,4]{1,0:T(1,128)S(1)}, s32[1,4]{1,0:T(1,128)}, u32[]{:S(2)}) copy-start(s32[1,4]{1,0:T(1,128)} %refs_2_.4) | copy-start | bytes 52
  0.0 1.1 %copy-start.1 = (bf16[4,128,512]{2,1,0:T(8,128)(2,1)S(1)}, bf16[4,128,512]{2,1,0:T(8,128)(2,1)}, u32[]{:S(2)}) copy-start(bf16[4,128,512]{2,1,0:T(8,128)(2,1)} %refs_7_.1) | copy-start | bytes 1572868
  0.0 1.2 %copy-start = (bf16[4,128,512]{2,1,0:T(8,128)(2,1)S(1)}, bf16[4,128,512]{2,1,0:T(8,128)(2,1)}, u32[]{:S(2)}) copy-start(bf16[4,128,512]{2,1,0:T(8,128)(2,1)} %refs_6_.2) | copy-start | bytes 1572868
  0.0 1.2 %copy-start.7 = (bf16[1,512]{1,0:T(2,128)(2,1)S(1)}, bf16[1,512]{1,0:T(2,128)(2,1)}, u32[]{:S(2)}) copy-start(bf16[1,512]{1,0:T(2,128)(2,1)} %refs_5_.2) | copy-start | bytes 3076
  0.0 1.2 %copy-start.6 = (bf16[1,512]{1,0:T(2,128)(2,1)S(1)}, bf16[1,512]{1,0:T(2,128)(2,1)}, u32[]{:S(2)}) copy-start(bf16[1,512]{1,0:T(2,128)(2,1)} %refs_4_.1) | copy-start | bytes 3076
  0.0 1.2 %copy-start.3 = (bf16[1,3072]{1,0:T(2,128)(2,1)S(1)}, bf16[1,3072]{1,0:T(2,128)(2,1)}, u32[]{:S(2)}) copy-start(bf16[1,3072]{1,0:T(2,128)(2,1)} %refs_3_.3) | copy-start | bytes 18436
  0.8 15.3 %slice-start.9 = ((s8[4718592]{0:T(1024)(128)(4,1)}), s8[4194304]{0:T(1024)(128)(4,1)S(1)}, s32[]{:S(2)}) async-start(s8[4718592]{0:T(1024)(128)(4,1)} %bitcast.8), calls=%async_computation.12 | async-start | bytes 8388608
  0.8 26.5 %slice-start = ((s8[12582912]{0:T(1024)(128)(4,1)}), s8[4194304]{0:T(1024)(128)(4,1)S(1)}, s32[]{:S(2)}) async-start(s8[12582912]{0:T(1024)(128)(4,1)} %bitcast.2), calls=%async_computation.3 | async-start | bytes 8388608
  0.8 26.5 %slice-start.3 = ((s8[12582912]{0:T(1024)(128)(4,1)}), s8[4194304]{0:T(1024)(128)(4,1)S(1)}, s32[]{:S(2)}) async-start(s8[12582912]{0:T(1024)(128)(4,1)} %bitcast.4), calls=%async_computation.6 | async-start | bytes 8388608
  0.8 26.5 %slice-start.6 = ((s8[12582912]{0:T(1024)(128)(4,1)}), s8[4194304]{0:T(1024)(128)(4,1)S(1)}, s32[]{:S(2)}) async-start(s8[12582912]{0:T(1024)(128)(4,1)} %bitcast.6), calls=%async_computation.9 | async-start | bytes 8388608
  1.2 14.8 %slice-start.10 = ((s8[4718592]{0:T(1024)(128)(4,1)}), s8[524288]{0:T(1024)(128)(4,1)S(1)}, s32[]{:S(2)}) async-start(s8[4718592]{0:T(1024)(128)(4,1)} %bitcast.8), calls=%async_computation.13 | async-start | bytes 1048576
  1.2 14.8 %copy-start.8 = (s32[8,2]{0,1:T(2,128)S(1)}, s32[8,2]{0,1:T(2,128)}, u32[]{:S(2)}) copy-start(s32[8,2]{0,1:T(2,128)} %param.26) | copy-start | bytes 196
  1.3 16.7 %copy-start.5 = (bf16[8,768]{1,0:T(8,128)(2,1)S(1)}, bf16[8,768]{1,0:T(8,128)(2,1)}, u32[]{:S(2)}) copy-start(bf16[8,768]{1,0:T(8,128)(2,1)} %refs_0_.3) | copy-start | bytes 36868
  1.3 26.0 %slice-start.1 = ((s8[12582912]{0:T(1024)(128)(4,1)}), s8[4194304]{0:T(1024)(128)(4,1)S(1)}, s32[]{:S(2)}) async-start(s8[12582912]{0:T(1024)(128)(4,1)} %bitcast.2), calls=%async_computation.4 | async-start | bytes 8388608
  1.3 26.0 %slice-start.2 = ((s8[12582912]{0:T(1024)(128)(4,1)}), s8[4194304]{0:T(1024)(128)(4,1)S(1)}, s32[]{:S(2)}) async-start(s8[12582912]{0:T(1024)(128)(4,1)} %bitcast.2), calls=%async_computation.5 | async-start | bytes 8388608
  1.3 26.0 %slice-start.4 = ((s8[12582912]{0:T(1024)(128)(4,1)}), s8[4194304]{0:T(1024)(128)(4,1)S(1)}, s32[]{:S(2)}) async-start(s8[12582912]{0:T(1024)(128)(4,1)} %bitcast.4), calls=%async_computation.7 | async-start | bytes 8388608
  1.3 26.0 %slice-start.5 = ((s8[12582912]{0:T(1024)(128)(4,1)}), s8[4194304]{0:T(1024)(128)(4,1)S(1)}, s32[]{:S(2)}) async-start(s8[12582912]{0:T(1024)(128)(4,1)} %bitcast.4), calls=%async_computation.8 | async-start | bytes 8388608
  1.3 26.0 %slice-start.7 = ((s8[12582912]{0:T(1024)(128)(4,1)}), s8[4194304]{0:T(1024)(128)(4,1)S(1)}, s32[]{:S(2)}) async-start(s8[12582912]{0:T(1024)(128)(4,1)} %bitcast.6), calls=%async_computation.10 | async-start | bytes 8388608
  1.3 26.0 %slice-start.8 = ((s8[12582912]{0:T(1024)(128)(4,1)}), s8[4194304]{0:T(1024)(128)(4,1)S(1)}, s32[]{:S(2)}) async-start(s8[12582912]{0:T(1024)(128)(4,1)} %bitcast.6), calls=%async_computation.11 | async-start | bytes 8388608
  1.3 26.0 %copy-start.2 = (bf16[6144,8]{0,1:T(8,128)(2,1)S(1)}, bf16[6144,8]{0,1:T(8,128)(2,1)}, u32[]{:S(2)}) copy-start(bf16[6144,8]{0,1:T(8,128)(2,1)} %param.25) | copy-start | bytes 294916
  1.4 26.0 %copy-start.4 = (bf16[6144]{0:T(1024)(128)(2,1)S(1)}, bf16[6144]{0:T(1024)(128)(2,1)}, u32[]{:S(2)}) copy-start(bf16[6144]{0:T(1024)(128)(2,1)} %refs_1_.5) | copy-start | bytes 36868
  16.8 1.2 %collective-permute-start = (f32[8,768]{1,0:T(8,128)S(1)}, f32[8,768]{1,0:T(8,128)S(1)}, u32[]{:S(2)}, u32[]{:S(2)}) collective-permute-start(f32[8,768]{1,0:T(8,128)S(1)} %get-tuple-element.14.refs_1_), channel_id=1, source_target_pairs={{0,1},{1,0},{2,3},{3,2},{4,5},{5,4},{6,7},{7,6},{8,9},{9,8},{10,11... | collective-permute-start | bytes 73736 | tf_op jit(solution)/shard_map/ppermute | solution.py:421
  29.1 1.9 %collective-permute-start.2 = (f32[2,2176]{1,0:T(2,128)S(1)}, f32[2,2176]{1,0:T(2,128)S(1)}, u32[]{:S(2)}, u32[]{:S(2)}) collective-permute-start(f32[2,2176]{1,0:T(2,128)S(1)} %get-tuple-element.19.refs_0_), channel_id=1, source_target_pairs={{0,1},{1,0},{2,3},{3,2},{4,5},{5,4},{6,7},{7,6},{8,9},{9,8},{10,11... | collective-permute-start | bytes 52232 | tf_op jit(solution)/shard_map/ppermute | solution.py:438
  31.0 1.2 %collective-permute-start.1 = (f32[2,2048]{1,0:T(2,128)S(1)}, f32[2,2048]{1,0:T(2,128)S(1)}, u32[]{:S(2)}, u32[]{:S(2)}) collective-permute-start(f32[2,2048]{1,0:T(2,128)S(1)} %get-tuple-element.18.refs_0_), channel_id=1, source_target_pairs={{0,1},{1,0},{2,3},{3,2},{4,5},{5,4},{6,7},{7,6},{8,9},{9,8},{10,11... | collective-permute-start | bytes 49160 | tf_op jit(solution)/shard_map/ppermute | solution.py:445
